TPU v7x, 32 devices: a whole 2x2x4 slice. The times are simulated.
32 devices in a mesh: hist: 8 (over z, y), col: 4 (over x, core).
Axes of the slice: x: 2, y: 2, z: 4, core: 2. Of those that a mesh axis runs over, the one named last changes fastest.
Arguments:
- sigma_ret: bfloat16 [4, 32, 64, 128], P(None, 'hist', 'col'), may hold values from -6 to 6
- sigma_less: bfloat16 [4, 32, 64, 128], P(None, 'hist', 'col'), may hold values from -6 to 6
- green_less: bfloat16 [32, 96, 64, 128], P('hist', 'col'), may hold values from -0.09375 to 0.09375
- green_adv: bfloat16 [32, 96, 64, 128], P('hist', 'col'), may hold values from -0.09375 to 0.09375
- time_now: int32 [4], replicated, may hold values from 16 to 31, as said below
- col_start: int32 [96], P('col'), may hold values from 0 to 15
Outputs:
- collision: bfloat16 [4, 96, 64, 128], P(None, 'col')
Inputs may be any that keep to these rules, and one draw needn't show every extreme that they name: Some time row has time_now = 31.
All inputs are finite; a program needn't handle non-finite values.
Results may differ from a plain program's by a relative error of at most 0.001.
Values may be sent and summed in bfloat16 or wider, within the bound.
No kernel may reach another device: no remote copies, remote signals or barrier semaphores. Data moves between devices by JAX's collectives and lax.ppermute only.
A program may use at most 64 MiB of HBM per device.

v0:
```python
import jax
import jax.numpy as jnp
from jax import lax
from jax.sharding import PartitionSpec as P


def widen(green, norb):
    real_part = green[..., :norb]
    imag_part = green[..., norb:]
    lower = jnp.concatenate([-imag_part, real_part], axis=-1)
    return jnp.concatenate([green, lower], axis=-2)


def on_device(sigma_ret, sigma_less, green_less, green_adv, time_now, col_start):
    norb = green_less.shape[2]
    tb_local = green_less.shape[0]
    full_ret, full_less = (
        lax.all_gather(sigma_ret, "col", axis=2, tiled=True),
        lax.all_gather(sigma_less, "col", axis=2, tiled=True),
    )
    tbar = lax.axis_index("hist") * tb_local + jnp.arange(tb_local, dtype=jnp.int32)
    zero = jnp.zeros((), green_less.dtype)
    before = (tbar[None, :] <= time_now[:, None])[:, :, None, None]
    full_ret = jnp.where(before, full_ret, zero)
    full_less = jnp.where(before, full_less, zero)
    after = (tbar[:, None] >= col_start[None, :])[:, :, None, None]
    b_less = jnp.where(after, widen(green_less, norb), zero)
    b_adv = jnp.where(after, widen(green_adv, norb), zero)
    term = jnp.einsum("tbik,bckn->tcin", full_ret, b_less, preferred_element_type=jnp.float32)
    term = term + jnp.einsum(
        "tbik,bckn->tcin", full_less, b_adv, preferred_element_type=jnp.float32
    )
    total = lax.psum(term, "hist")
    return total.astype(jnp.bfloat16)


def solution(mesh):
    return jax.shard_map(
        on_device,
        mesh=mesh,
        in_specs=(
            P(None, "hist", "col", None),
            P(None, "hist", "col", None),
            P("hist", "col", None, None),
            P("hist", "col", None, None),
            P(),
            P("col"),
        ),
        out_specs=P(None, "col", None, None),
        check_vma=False,
    )
```

profile of v0, /device:TPU:0, one launch (start us, length us, event | category | flops | bytes accessed | tf_op | source)
XLA Modules:
  0.0 158.2 jit_solution(5234731373101541399)
XLA Ops:
  0.0 0.0 copy-start.1
  0.0 0.0 copy-start
  0.0 0.0 copy-start.4
  0.0 7.0 %slice_negate_fusion = (bf16[4,24,64,64]{3,2,1,0:T(8,128)(2,1)}, bf16[4,24,64,64]{3,2,1,0:T(8,128)(2,1)}, bf16[4,24,64,64]{3,2,1,0:T(8,128)(2,1)}, bf16[4,24,64,64]{3,2,1,0:T(8,128)(2,1)}) fusion(bf16[4,24,64,128]{3,2,1,0:T(8,128)(2,1)} %param.9, bf16[4,24,64,128]{3,2,1,0:T(8,128)(2,1)} %param.8), kind=kLoop, calls=%fused_computation.10 | loop fusion | flops 786432 | bytes 6291456 | tf_op jit(solution)/shard_map/neg | solution.py:10
  7.0 0.0 copy-done.4
  7.0 0.1 broadcast_compare_fusion.1
  7.1 0.0 copy-done.1
  7.1 0.0 copy-done
  7.1 0.0 copy-start.5
  7.1 0.0 copy-start.2
  7.1 5.4 %fusion = (bf16[4,24,128,128,1]{3,2,1,0,4:T(8,128)(2,1)S(1)}, bf16[4,24,128,128,1]{3,2,1,0,4:T(8,128)(2,1)S(1)}) fusion(bf16[4,24,64,64]{3,2,1,0:T(8,128)(2,1)} %get-tuple-element.11, bf16[4,24,64,64]{3,2,1,0:T(8,128)(2,1)} %get-tuple-element.12, bf16[4,24,64,128]{3,2,1,0:T(8,128)(2,1)S(1)} %copy-done.1, pred[4,24]{1,0:T(4,128)(4,1)S(1)} %broadcast_compare_fusion.1, ...), kind=kLoop, calls=%fused_computation.1 | loop fusion | flops 22020096 | bytes 12583008 | tf_op jit(solution)/shard_map/jit(_where)/select_n | solution.py:27
  12.4 0.0 copy-done.5
  12.5 0.1 broadcast_compare_fusion
  12.5 0.0 copy-done.2
  12.5 7.2 %all_gather.7 = bf16[4,4,64,128]{3,2,1,0:T(8,128)(2,1)S(1)} all-gather(bf16[4,4,16,128]{3,2,1,0:T(8,128)(2,1)S(1)} %copy-done.2), channel_id=1, replica_groups=mesh['hist'=8,'col'=4] {'col'}, dimensions={2}, use_global_device_ids=true | all-gather | bytes 327680 | tf_op jit(solution)/shard_map/all_gather | solution.py:19
  19.7 0.0 copy-start.3
  19.7 1.0 fusion.3
  20.8 0.0 copy-done.3
  20.8 5.9 %all_gather.6 = bf16[4,4,64,128]{3,2,1,0:T(8,128)(2,1)S(1)} all-gather(bf16[4,4,16,128]{3,2,1,0:T(8,128)(2,1)S(1)} %copy-done.3), channel_id=1, replica_groups=mesh['hist'=8,'col'=4] {'col'}, dimensions={2}, use_global_device_ids=true | all-gather | bytes 327680 | tf_op jit(solution)/shard_map/all_gather | solution.py:18
  26.6 1.1 fusion.2
  27.7 127.7 %all-reduce.1 = bf16[4,24,64,128]{3,2,0,1:T(8,128)(2,1)} all-reduce(f32[4,24,64,128]{3,2,0,1:T(8,128)S(1)} %fusion.2), channel_id=1, replica_groups=mesh['hist'=8,'col'=4] {'hist'}, use_global_device_ids=true, to_apply=%region_0.1 | all-reduce | flops 786432 | bytes 4718592 | tf_op jit(solution)/shard_map/psum | solution.py:33
  155.5 2.7 %copy.9 = bf16[4,24,64,128]{3,2,1,0:T(8,128)(2,1)} copy(bf16[4,24,64,128]{3,2,0,1:T(8,128)(2,1)} %all-reduce.1) | data formatting | bytes 3145728 | tf_op jit(solution)/shard_map/convert_element_type | solution.py:34
  (1 shorter events, 0.0 us)
Async XLA Ops:
  0.0 7.1 %copy-start.1 = (bf16[4,24,64,128]{3,2,1,0:T(8,128)(2,1)S(1)}, bf16[4,24,64,128]{3,2,1,0:T(8,128)(2,1)}, u32[]{:S(2)}) copy-start(bf16[4,24,64,128]{3,2,1,0:T(8,128)(2,1)} %param.8) | copy-start | bytes 4718596
  0.0 7.1 %copy-start = (bf16[4,24,64,128]{3,2,1,0:T(8,128)(2,1)S(1)}, bf16[4,24,64,128]{3,2,1,0:T(8,128)(2,1)}, u32[]{:S(2)}) copy-start(bf16[4,24,64,128]{3,2,1,0:T(8,128)(2,1)} %param.9) | copy-start | bytes 4718596
  0.0 7.0 %copy-start.4 = (s32[24]{0:T(128)S(1)}, s32[24]{0:T(128)}, u32[]{:S(2)}) copy-start(s32[24]{0:T(128)} %param.11) | copy-start | bytes 292
  7.1 5.4 %copy-start.5 = (s32[4]{0:T(128)S(1)}, s32[4]{0:T(128)}, u32[]{:S(2)}) copy-start(s32[4]{0:T(128)} %param.10) | copy-start | bytes 52
  7.1 5.5 %copy-start.2 = (bf16[4,4,16,128]{3,2,1,0:T(8,128)(2,1)S(1)}, bf16[4,4,16,128]{3,2,1,0:T(8,128)(2,1)}, u32[]{:S(2)}) copy-start(bf16[4,4,16,128]{3,2,1,0:T(8,128)(2,1)} %param.7) | copy-start | bytes 196612
  19.7 1.0 copy-start.3
where the time goes:
time: 158 us
  blocking collectives  141 us (89%)
  other arithmetic  12.5 us (8%)
  local copies, waits for them, and re-layouts  2.73 us (2%)
  matrix products  2.13 us (1%)
    psum x1, blocking collectives, on_device(): total = lax.psum(term, 'hist')  128 us
    all_gather x1, blocking collectives, on_device(): lax.all_gather(sigma_less, 'col', axis=2, tiled=True)  7.18 us
    neg x1, other arithmetic, widen(): lower = jnp.concatenate([-imag_part, real_part], axis=-1)  6.97 us
    all_gather x1, blocking collectives, on_device(): lax.all_gather(sigma_ret, 'col', axis=2, tiled=True)  5.86 us
    select_n x1, other arithmetic, on_device(): b_less = jnp.where(after, widen(green_less, norb), zero)  5.36 us

commit v1 on v0

v1 whole, which is shorter than its diff:
```python
import functools

import jax
import jax.numpy as jnp
from jax import lax
from jax.experimental import pallas as pl
from jax.experimental.pallas import tpu as pltpu
from jax.sharding import PartitionSpec as P

BITS = {"y": 0, "z0": 1, "z1": 2}
ORDERS = ((("y", "z0", "z1", "z0", "y"), ("z0", "y", "z1", "z0", "y")), (("y", "z1", "z0", "y", "z1"), ("z1", "y", "z0", "z1", "y")), (("y", "z0", "z1", "y", "z0"), ("z0", "y", "z1", "z0", "y")), (("z1", "y", "z0", "z1", "y"), ("y", "z0", "z1", "y", "z0")))
STEPS = (0, 1, 2, 0, 3, 1, 2, 0, 3, 1, 2, 0, 3, 2, 1, 3)
PLACES = (((0, 0), (1, 0), (2, 0), (3, 0), (0, 1)), ((2, 1), (1, 1), (3, 1)))
CHAIN = (1, 1, 1, 1, 1, 1, 1, 1, 1, 1, 1, 1, 1, 1, 1, 1)
FIRST, COL, CORE, FIELDS = 4, 5, 6, 8
GROUP = 3
STEPS_PER_OCTAVE = 128.0
TOP = 32512.0
LEAST = 2.0 ** -110
MIB = 2 ** 20
PARAMS = pltpu.CompilerParams(vmem_limit_bytes=40 * MIB)


def widen(green, norb):
    real_part = green[..., :norb]
    imag_part = green[..., norb:]
    lower = jnp.concatenate([-imag_part, real_part], axis=-1)
    return jnp.concatenate([green, lower], axis=-2)


def encode(read, tiles, ni, out_ref):
    rows = []
    for first in range(0, tiles, GROUP):
        values = read(first)
        most = jnp.max(jnp.max(jnp.abs(values), axis=0), axis=0, keepdims=True)
        index = jnp.ceil(jnp.log2(jnp.maximum(most, LEAST) * (1.0 / TOP)) * STEPS_PER_OCTAVE)
        codes = jnp.round(values * jnp.exp2(index * (-1.0 / STEPS_PER_OCTAVE))[None])
        out_ref[first:first + GROUP] = codes.astype(jnp.int32).astype(jnp.int16)
        rows.append(index)
    rows = rows + [jnp.zeros_like(rows[0])] * (ni - len(rows))
    out_ref[tiles] = jnp.concatenate(rows, axis=0).astype(jnp.int32).astype(jnp.int16)


def decode(in_ref, tiles):
    index = in_ref[tiles].astype(jnp.int32).astype(jnp.float32)
    scales = jnp.exp2(index * (1.0 / STEPS_PER_OCTAVE))
    return [
        in_ref[first:first + GROUP].astype(jnp.int32).astype(jnp.float32) * scales[g:g + 1][None]
        for g, first in enumerate(range(0, tiles, GROUP))
    ]


def pack_left(info, at, sigma_ref, left_ref, row):
    _, nt, nb, ni, width = sigma_ref.shape
    half = width // 2
    for t in range(nt):
        for b in range(nb):
            live = info[FIRST] + b <= info[at + t]
            ret = jnp.where(live, sigma_ref[0, t, b], jnp.zeros((), jnp.bfloat16))
            less = jnp.where(live, sigma_ref[1, t, b], jnp.zeros((), jnp.bfloat16))
            cols = slice(b * width, (b + 1) * width)
            rows = slice(row + t * ni, row + (t + 1) * ni)
            left_ref[rows, cols] = jnp.concatenate([ret[:, :half], less[:, :half]], axis=1)
            rows = slice(row + (nt + t) * ni, row + (nt + t + 1) * ni)
            left_ref[rows, cols] = jnp.concatenate([ret[:, half:], less[:, half:]], axis=1)


def relative(info, orders, bits):
    spots = [[lax.bitwise_xor(info[BITS[d]], bits[d]) for d in order] for order in orders]
    return [jnp.where(info[CORE] == 0, *pair) for pair in zip(*spots)]


def spots_of(info, orders, nt):
    dims = [order[:3] for order in orders]
    return [[relative(info, dims, {"y": side, "z0": t % 2, "z1": t // 2}) for t in range(nt)] for side in range(2)]


def add_pair(spots, both, pair, term_ref):
    ni, width = term_ref.shape[-2:]
    half_columns = term_ref.shape[3]
    rows = both.shape[0] // 2
    lane = lax.broadcasted_iota(jnp.int32, (rows, width), 1)
    for at in range(2):
        cut = both[:, at * width:(at + 1) * width]
        turned = pltpu.roll(cut[rows:], width // 2, 1)
        value = cut[:rows] + jnp.where(lane < width // 2, -turned, turned)
        side, c = divmod(2 * pair + at, half_columns)
        for t in range(rows // ni):
            term_ref[tuple(spots[side][t]) + (c,)] = value[t * ni:(t + 1) * ni]


def part_kernel(orders, info, *refs):
    n = len(orders)
    sigma_refs, (gless_ref, gadv_ref) = refs[:n], refs[n:n + 2]
    outs, (left_ref, term_ref) = refs[-2 * n - 2:-2], refs[-2:]
    nb, ncol, norb, width = gless_ref.shape
    rows = left_ref.shape[0] // n
    for at, sigma_ref in enumerate(sigma_refs):
        pack_left(info, FIELDS, sigma_ref, left_ref, at * rows)
    spots = [spots_of(info, order, rows // (2 * term_ref.shape[-2])) for order in orders]
    for pair in range(ncol // 2):
        sides = []
        for c in (2 * pair, 2 * pair + 1):
            parts = []
            for b in range(nb):
                parts += [gless_ref[b, c], gadv_ref[b, c]]
            sides.append(jnp.concatenate(parts, axis=0))
        both = jnp.dot(left_ref[...], jnp.concatenate(sides, axis=1), preferred_element_type=jnp.float32)
        for at in range(n):
            add_pair(spots[at], both[at * rows:(at + 1) * rows], pair, term_ref.at[at])
    for at in range(n):
        keep_ref, out_ref = outs[2 * at:2 * at + 2]
        _, n1, n2, half_columns, ni, _ = term_ref.shape[1:]
        keep_ref[0] = term_ref[at, 0]

        def read(first):
            block, c = divmod(first, half_columns)
            a, b = divmod(block, n2)
            return term_ref[at, 1, a, b, c:c + GROUP]

        encode(read, n1 * n2 * half_columns, ni, out_ref)


def fold_kernel(sum_ref, in_ref, *refs):
    keep_ref, out_ref, term_ref = refs[-3:]
    _, nd, nc, ni, width = keep_ref.shape
    tiles = nd * nc
    came = decode(in_ref, 2 * tiles)
    for g, first in enumerate(range(0, tiles, GROUP)):
        d, c = divmod(first, nc)
        keep_ref[0, d, c:c + GROUP] = sum_ref[0, 0, d, c:c + GROUP] + came[g]
        term_ref[first:first + GROUP] = sum_ref[0, 1, d, c:c + GROUP] + came[g + tiles // GROUP]
    encode(lambda first: term_ref[first:first + GROUP], tiles, ni, out_ref)


def cross_kernel(sum_ref, in_ref, *refs):
    out_ref, term_ref = refs[-2:]
    _, nd, nc, ni, width = sum_ref.shape
    for g, came in enumerate(decode(in_ref, nd * nc)):
        d, c = divmod(g * GROUP, nc)
        term_ref[g * GROUP:(g + 1) * GROUP] = sum_ref[0, d, c:c + GROUP] + came
    encode(lambda first: term_ref[first:first + GROUP], nd * nc, ni, out_ref)


def final_kernel(mine_ref, other_ref, *refs):
    out_ref = refs[-1]
    nd, nc, ni, width = out_ref.shape
    mine, other = decode(mine_ref, nd * nc), decode(other_ref, nd * nc)
    half = len(mine) // 2
    for g in range(len(mine)):
        d, c = divmod(g * GROUP, nc)
        out_ref[d, c:c + GROUP] = (mine[g] + other[(g + half) % len(mine)]).astype(jnp.bfloat16)


def merge_kernel(mine_ref, other_ref, *refs):
    out_ref = refs[-1]
    out_ref[0] = mine_ref[...]
    out_ref[1] = other_ref[...]


def copy_kernel(in_ref, *refs):
    refs[-1][...] = in_ref[...]


def place_kernel(items, info, *refs):
    blocks, out_ref, sem = refs[:len(items)], refs[-2], refs[-1]
    copies = []
    for block, (chunk, orders, last) in zip(blocks, items):
        nc, ni, _ = block.shape[-3:]
        row = pl.multiple_of(lax.bitwise_xor(info[COL], chunk) * ni, ni)
        for second in range(2):
            for first in range(2):
                places = []
                for order in orders:
                    bits = dict(zip(order[2:], (first, second, last)))
                    places.append([lax.bitwise_xor(info[BITS[d]], bits[d]) for d in ("y", "z0", "z1")])
                y, z0, z1 = (jnp.where(info[CORE] == 0, *pair) for pair in zip(*places))
                target = out_ref.at[2 * z1 + z0, pl.ds(y * nc, nc), pl.ds(row, ni)]
                copies.append(pltpu.make_async_copy(block.at[second, first], target, sem.at[len(copies)]))
    for copy in copies:
        copy.start()
    for copy in copies:
        copy.wait()


def staged(sigma_ret, sigma_less, green_less, green_adv, time_now, col_start, n_hist, n_col):
    nt, nb, ni, width = sigma_ret.shape
    _, ncol, norb, _ = green_less.shape
    nc = ncol // 2
    hist = lax.axis_index("hist")
    col = lax.axis_index("col")
    field = jnp.arange(FIELDS, dtype=jnp.int32)
    bit = lax.shift_right_logical(jnp.where(field == CORE, col << CORE, hist), field) & 1
    own = jnp.where(field == FIRST, hist * nb, jnp.where(field == COL, col, bit))
    info = jnp.concatenate([own, time_now])

    def swap(v, chunk, stage):
        pairs = []
        for h in range(n_hist):
            for c in range(n_col):
                partner = h ^ (1 << BITS[ORDERS[chunk][c % 2][stage]])
                pairs.append((h * n_col + c, partner * n_col + c))
        return lax.ppermute(v, ("hist", "col"), pairs)

    def swap_col(v, k):
        return lax.ppermute(v, "col", [(i, i ^ k) for i in range(n_col)])

    smem = pl.BlockSpec(memory_space=pltpu.SMEM)
    vmem = pl.BlockSpec(memory_space=pltpu.VMEM)
    hbm = pl.BlockSpec(memory_space=pltpu.HBM)

    def codes_of(n):
        return jax.ShapeDtypeStruct((n * nc + 1, ni, width), jnp.int16)

    own_sigma = jnp.stack([sigma_ret, sigma_less])
    tbar = hist * nb + jnp.arange(nb, dtype=jnp.int32)
    after = (tbar[:, None] >= col_start[None, :])[:, :, None, None]
    zero = jnp.zeros((), green_less.dtype)
    masked = [jnp.where(after, green, zero) for green in (green_less, green_adv)]
    near = swap_col(own_sigma, 1)
    far = swap_col(own_sigma, 2)

    def call(kernel, out_shape, args, before, scratch=(), cost=None, specs=()):
        args = list(args) + ([] if before is None else [before])
        many = isinstance(out_shape, list)
        return pl.pallas_call(
            kernel,
            out_shape=out_shape,
            in_specs=list(specs) + [vmem] * (len(args) - len(specs)),
            out_specs=[vmem] * len(out_shape) if many else vmem,
            scratch_shapes=list(scratch),
            compiler_params=PARAMS,
            cost_estimate=cost,
            name=kernel.func.__name__ if isinstance(kernel, functools.partial) else kernel.__name__,
        )(*args)

    def partial(orders, blocks, before):
        n = len(orders)
        rows = 2 * nt * ni
        keep = jax.ShapeDtypeStruct((1, 2, 2, nc, ni, width), jnp.float32)
        flops = 2 * n * rows * 2 * nb * norb * ncol * width
        out = call(
            functools.partial(part_kernel, orders),
            [keep, codes_of(4)] * n,
            [info, *blocks, *masked],
            before,
            [pltpu.VMEM((n * rows, nb * width), jnp.bfloat16),
             pltpu.VMEM((n, 2, 2, 2, nc, ni, width), jnp.float32)],
            pl.CostEstimate(flops=flops, bytes_accessed=green_less.size * 4, transcendentals=0),
            [smem],
        )
        return [out[2 * at:2 * at + 2] for at in range(n)]

    def terms(n):
        return [pltpu.VMEM((n * nc, ni, width), jnp.float32)]

    def fold(state, chunk, before):
        sums, codes = state
        keep = jax.ShapeDtypeStruct((1, 2, nc, ni, width), jnp.float32)
        state = call(fold_kernel, [keep, codes_of(2)], [sums, swap(codes, chunk, 0)], before, terms(2))
        return state, state[1]

    def cross(state, chunk, before):
        sums, codes = state
        codes = call(cross_kernel, codes_of(2), [sums, swap(codes, chunk, 1)], before, terms(2))
        return codes, codes

    def final(codes, chunk, before):
        out = jax.ShapeDtypeStruct((2, nc, ni, width), jnp.bfloat16)
        out = call(final_kernel, out, [codes, swap(codes, chunk, 2)], before)
        return out, out

    def merge(mine, chunk, before):
        out = jax.ShapeDtypeStruct((2,) + mine.shape, mine.dtype)
        out = call(merge_kernel, out, [mine, swap(mine, chunk, 3)], before)
        return out, out

    def put(items, out):
        extra = [] if out is None else [out]
        n = len(items)
        return pl.pallas_call(
            functools.partial(place_kernel, [(k, ORDERS[k], last) for k, last in items]),
            out_shape=jax.ShapeDtypeStruct((nt, ncol, norb, width), jnp.bfloat16),
            in_specs=[smem] + [vmem] * n + [hbm] * len(extra),
            out_specs=hbm,
            scratch_shapes=[pltpu.SemaphoreType.DMA((4 * n,))],
            input_output_aliases={1 + n: 0} if extra else {},
            compiler_params=PARAMS,
            name="place_part",
        )(info, *[blocks[k][last] for k, last in items], *extra)

    state = partial(ORDERS[:2], [own_sigma, near], None)
    passed = call(copy_kernel, jax.ShapeDtypeStruct(far.shape, far.dtype), [far], state[1][1])
    state += partial(ORDERS[2:3], [far], passed)
    state += partial(ORDERS[3:], [swap_col(passed, 1)], state[2][1])
    last = state[3][1]
    todo = [[fold, cross, final, merge] for _ in range(n_col)]
    for k, chained in zip(STEPS, CHAIN):
        state[k], last = todo[k].pop(0)(state[k], k, last if chained else None)
    blocks = [(state[k], swap(state[k], k, 4)) for k in range(n_col)]
    out = None
    for items in PLACES:
        out = put(items, out)
    return out


def plain(sigma_ret, sigma_less, green_less, green_adv, time_now, col_start):
    norb = green_less.shape[2]
    tb_local = green_less.shape[0]
    full_ret = lax.all_gather(sigma_ret, "col", axis=2, tiled=True)
    full_less = lax.all_gather(sigma_less, "col", axis=2, tiled=True)
    tbar = lax.axis_index("hist") * tb_local + jnp.arange(tb_local, dtype=jnp.int32)
    zero = jnp.zeros((), green_less.dtype)
    before = (tbar[None, :] <= time_now[:, None])[:, :, None, None]
    full_ret = jnp.where(before, full_ret, zero)
    full_less = jnp.where(before, full_less, zero)
    after = (tbar[:, None] >= col_start[None, :])[:, :, None, None]
    b_less = jnp.where(after, widen(green_less, norb), zero)
    b_adv = jnp.where(after, widen(green_adv, norb), zero)
    term = jnp.einsum("tbik,bckn->tcin", full_ret, b_less, preferred_element_type=jnp.float32)
    term = term + jnp.einsum("tbik,bckn->tcin", full_less, b_adv, preferred_element_type=jnp.float32)
    return lax.psum(term, "hist").astype(jnp.bfloat16)


def solution(mesh):
    n_hist, n_col = mesh.shape["hist"], mesh.shape["col"]

    def on_device(*args):
        nt, ncol = args[0].shape[0], args[2].shape[1]
        if n_hist == 8 and nt == 4 and n_col == 4 and ncol % 4 == 0 and ncol % (2 * GROUP) == 0:
            return staged(*args, n_hist, n_col)
        return plain(*args)

    return jax.shard_map(
        on_device,
        mesh=mesh,
        in_specs=(
            P(None, "hist", "col", None),
            P(None, "hist", "col", None),
            P("hist", "col", None, None),
            P("hist", "col", None, None),
            P(),
            P("col"),
        ),
        out_specs=P(None, "col", None, None),
        check_vma=False,
    )
```

time: 158 us -> 57.2 us (0.36)
  blocking collectives: 141 us -> 0 us
  starting transfers between devices: 0 us -> 33.2 us
  waiting for transfers between devices: 0 us -> 10.7 us
  Pallas kernels: 0 us -> 9.05 us
  other arithmetic: 12.5 us -> 3.87 us
  local copies, waits for them, and re-layouts: 2.73 us -> 0.01 us
  matrix products: 2.13 us -> 0 us
    psum x1 -> x0, blocking collectives: 128 us -> none  [on_device(): total = lax.psum(term, 'hist')]
    ppermute x0 -> x23, starting transfers between devices: none -> 33.2 us  [the longest x20 29.9 us: swap(): return lax.ppermute(v, ('hist', 'col'), pairs)]
    all_gather x2 -> x0, blocking collectives: 13 us -> none  [the longest x1 7.18 us: on_device(): lax.all_gather(sigma_less, 'col', axis=2, tiled=True)]
    ppermute x0 -> x23, waiting for transfers between devices: none -> 10.7 us  [the longest x20 10.6 us: swap(): return lax.ppermute(v, ('hist', 'col'), pairs)]
    pallas_call x0 -> x22, Pallas kernels: none -> 9.05 us  [the longest x20 5.95 us: call(): pl.pallas_call(kernel, out_shape=out_shape, in_specs=list(specs) + [vmem]...]
    neg x1 -> x0, other arithmetic: 6.97 us -> none  [widen(): lower = jnp.concatenate([-imag_part, real_part], axis=-1)]
    select_n x1 -> x2, other arithmetic: 5.36 us -> 2.18 us  [the longest x1 2.17 us: staged(): jnp.where(after, green, zero)]
    convert_element_type x1 -> x0, local copies, waits for them, and re-layouts: 2.7 us -> none  [on_device(): return total.astype(jnp.bfloat16)]
  transfers between devices with their start and end apart: 0 -> 23, of which waited for: 0 -> 7; matrix products, arithmetic and copies ran while one was open for 0% -> 5% of each run, Pallas kernels for 0% -> 13%
where the time goes in v1:
time: 57.2 us; the launch traced here: 57 us
  starting transfers between devices  33.2 us (58%)
  waiting for transfers between devices  10.7 us (19%)
  Pallas kernels  9.05 us (16%)
  other arithmetic  3.87 us (7%)
    ppermute x20, starting transfers between devices, swap(): return lax.ppermute(v, ('hist', 'col'), pairs)  29.9 us
    ppermute x20, waiting for transfers between devices, swap(): return lax.ppermute(v, ('hist', 'col'), pairs)  10.6 us
    pallas_call x20, Pallas kernels, call(): pl.pallas_call(kernel, out_shape=out_shape, in_specs=list(specs) + [vmem]...  5.95 us
    ppermute x3, starting transfers between devices, swap_col(): return lax.ppermute(v, 'col', [(i, i ^ k) for i in range(n_col)])  3.31 us
    pallas_call x2, Pallas kernels, put(): pl.pallas_call(functools.partial(place_kernel, [(k, ORDERS[k], last) for...  3.1 us
    select_n x1, other arithmetic, staged(): jnp.where(after, green, zero)  2.17 us
  transfers between devices with their start and end apart: 23, of which 7 were waited for; matrix products, arithmetic and copies ran while one was open for 5% of the time, Pallas kernels for 13%

profile of v1, /device:TPU:0, one launch (start us, length us, event | category | flops | bytes accessed | tf_op | source)
XLA Modules:
  0.0 57.0 jit_solution(2315107115451413294)
XLA Ops:
  1.4 2.6 %collective-permute-start = (bf16[2,4,4,16,128]{4,3,2,1,0:T(8,128)(2,1)S(1)}, bf16[2,4,4,16,128]{4,3,2,1,0:T(8,128)(2,1)S(1)}, u32[]{:S(2)}, u32[]{:S(2)}) collective-permute-start(bf16[2,4,4,16,128]{4,3,2,1,0:T(8,128)(2,1)S(1)} %pad_maximum_fusion.refs_0_), channel_id=1, source_target_pairs={{0,2},{1,3},{2,0},{3,1},{4,6},{5,7},{6,4},{7,5},{8,10},{9,11},{10,... | collective-permute-start | bytes 393224 | tf_op jit(solution)/shard_map/ppermute | solution.py:206
  4.7 2.2 %broadcast_select_fusion = (bf16[4,24,64,128]{3,2,1,0:T(8,128)(2,1)S(1)}, bf16[4,24,64,128]{3,2,1,0:T(8,128)(2,1)S(1)}) fusion(bf16[4,24,64,128]{3,2,1,0:T(8,128)(2,1)} %param.9, pred[4,24]{1,0:T(4,128)(4,1)S(1)} %broadcast_compare_fusion, bf16[4,24,64,128]{3,2,1,0:T(8,128)(2,1)} %param.8), kind=kLoop, calls=%fused_computation | loop fusion | flops 1572864 | bytes 6291552 | tf_op jit(solution)/shard_map/jit(_where)/select_n | solution.py:219
  7.0 2.0 %part_kernel.3 = (f32[1,2,2,12,16,128]{5,4,3,2,1,0:T(8,128)S(1)}, s16[49,16,128]{2,1,0:T(8,128)(2,1)S(1)}, f32[1,2,2,12,16,128]{5,4,3,2,1,0:T(8,128)S(1)}, s16[49,16,128]{2,1,0:T(8,128)(2,1)S(1)}) custom-call(s32[12]{0:T(128)S(1)} %pad_add_fusion.info, bf16[2,4,4,16,128]{4,3,2,1,0:T(8,128)(2,1)S(1)} %pad_maximum_fusion.refs_0_, ...), custom_call_target="tpu_custom_call" | custom-call | flops 805306368 | bytes 3145728 | tf_op jit(solution)/shard_map/part_kernel/pallas_call | solution.py:226
  9.2 1.5 %collective-permute-start.4 = (s16[49,16,128]{2,1,0:T(8,128)(2,1)S(1)}, s16[49,16,128]{2,1,0:T(8,128)(2,1)S(1)}, u32[]{:S(2)}, u32[]{:S(2)}) collective-permute-start(s16[49,16,128]{2,1,0:T(8,128)(2,1)S(1)} %get-tuple-element.26), channel_id=1, source_target_pairs={{0,4},{1,9},{2,6},{3,11},{4,0},{5,13},{6,2},{7,15},{8,12},{9,1},{1... | collective-permute-start | bytes 602120 | tf_op jit(solution)/shard_map/ppermute | solution.py:203
  11.3 1.4 %part_kernel.4 = (f32[1,2,2,12,16,128]{5,4,3,2,1,0:T(8,128)S(1)}, s16[49,16,128]{2,1,0:T(8,128)(2,1)S(1)}) custom-call(s32[12]{0:T(128)S(1)} %pad_add_fusion.info, bf16[2,4,4,16,128]{4,3,2,1,0:T(8,128)(2,1)S(1)} %collective-permute-done.in_ref.refs_0_, bf16[4,24,64,128]{3,2,1,0:T(8,128)(2,1)S(1)} %get-tuple-element.38.refs_2_.refs_1_, ...), custom_call_target="tpu_custom_call" | custom-call | flops 402653184 | bytes 3145728 | tf_op jit(solution)/shard_map/part_kernel/pallas_call | solution.py:226
  12.7 1.6 %collective-permute-start.2 = (s16[49,16,128]{2,1,0:T(8,128)(2,1)S(1)}, s16[49,16,128]{2,1,0:T(8,128)(2,1)S(1)}, u32[]{:S(2)}, u32[]{:S(2)}) collective-permute-start(s16[49,16,128]{2,1,0:T(8,128)(2,1)S(1)} %get-tuple-element.23.refs_3_), channel_id=1, source_target_pairs={{0,4},{1,9},{2,6},{3,11},{4,0},{5,13},{6,2},{7,15},{8,12},{9,1},{1... | collective-permute-start | bytes 602120 | tf_op jit(solution)/shard_map/ppermute | solution.py:203
  14.3 1.4 %part_kernel.5 = (f32[1,2,2,12,16,128]{5,4,3,2,1,0:T(8,128)S(1)}, s16[49,16,128]{2,1,0:T(8,128)(2,1)S(1)}) custom-call(s32[12]{0:T(128)S(1)} %pad_add_fusion.info, bf16[2,4,4,16,128]{4,3,2,1,0:T(8,128)(2,1)S(1)} %collective-permute-done.5.refs_0_, bf16[4,24,64,128]{3,2,1,0:T(8,128)(2,1)S(1)} %get-tuple-element.38.refs_2_.refs_1_, ...), custom_call_target="tpu_custom_call" | custom-call | flops 402653184 | bytes 3145728 | tf_op jit(solution)/shard_map/part_kernel/pallas_call | solution.py:226
  15.7 2.7 %collective-permute-start.8 = (s16[49,16,128]{2,1,0:T(8,128)(2,1)S(1)}, s16[49,16,128]{2,1,0:T(8,128)(2,1)S(1)}, u32[]{:S(2)}, u32[]{:S(2)}) collective-permute-start(s16[49,16,128]{2,1,0:T(8,128)(2,1)S(1)} %get-tuple-element.27.refs_0_), channel_id=1, source_target_pairs={{0,16},{1,5},{2,18},{3,7},{4,20},{5,1},{6,22},{7,3},{8,24},{9,13},... | collective-permute-start | bytes 602120 | tf_op jit(solution)/shard_map/ppermute | solution.py:203
  18.5 1.7 %collective-permute-start.9 = (s16[25,16,128]{2,1,0:T(8,128)(2,1)S(1)}, s16[25,16,128]{2,1,0:T(8,128)(2,1)S(1)}, u32[]{:S(2)}, u32[]{:S(2)}) collective-permute-start(s16[25,16,128]{2,1,0:T(8,128)(2,1)S(1)} %get-tuple-element.28.refs_0_), channel_id=1, source_target_pairs={{0,8},{1,5},{2,10},{3,7},{4,12},{5,1},{6,14},{7,3},{8,0},{9,13},{1... | collective-permute-start | bytes 307208 | tf_op jit(solution)/shard_map/ppermute | solution.py:203
  22.0 1.3 %collective-permute-done.9.in_ref = s16[25,16,128]{2,1,0:T(8,128)(2,1)S(1)} collective-permute-done((s16[25,16,128]{2,1,0:T(8,128)(2,1)S(1)}, s16[25,16,128]{2,1,0:T(8,128)(2,1)S(1)}, u32[]{:S(2)}, u32[]{:S(2)}) %collective-permute-start.9) | collective-permute-done | bytes 102432 | tf_op jit(solution)/shard_map/ppermute | solution.py:203
  23.3 2.9 %collective-permute-start.13 = (s16[25,16,128]{2,1,0:T(8,128)(2,1)S(1)}, s16[25,16,128]{2,1,0:T(8,128)(2,1)S(1)}, u32[]{:S(2)}, u32[]{:S(2)}) collective-permute-start(s16[25,16,128]{2,1,0:T(8,128)(2,1)S(1)} %cross_kernel.4.refs_0_.mine_ref), channel_id=1, source_target_pairs={{0,16},{1,17},{2,18},{3,19},{4,20},{5,21},{6,22},{7,23},{8,24},{9,... | collective-permute-start | bytes 307208 | tf_op jit(solution)/shard_map/ppermute | solution.py:203
  26.3 1.6 %collective-permute-start.12 = (s16[25,16,128]{2,1,0:T(8,128)(2,1)S(1)}, s16[25,16,128]{2,1,0:T(8,128)(2,1)S(1)}, u32[]{:S(2)}, u32[]{:S(2)}) collective-permute-start(s16[25,16,128]{2,1,0:T(8,128)(2,1)S(1)} %get-tuple-element.35.refs_0_), channel_id=1, source_target_pairs={{0,4},{1,9},{2,6},{3,11},{4,0},{5,13},{6,2},{7,15},{8,12},{9,1},{1... | collective-permute-start | bytes 307208 | tf_op jit(solution)/shard_map/ppermute | solution.py:203
  29.0 3.7 %collective-permute-start.10 = (s16[25,16,128]{2,1,0:T(8,128)(2,1)S(1)}, s16[25,16,128]{2,1,0:T(8,128)(2,1)S(1)}, u32[]{:S(2)}, u32[]{:S(2)}) collective-permute-start(s16[25,16,128]{2,1,0:T(8,128)(2,1)S(1)} %cross_kernel.6.refs_0_.mine_ref), channel_id=1, source_target_pairs={{0,16},{1,17},{2,18},{3,19},{4,20},{5,21},{6,22},{7,23},{8,24},{9,... | collective-permute-start | bytes 307208 | tf_op jit(solution)/shard_map/ppermute | solution.py:203
  32.8 1.9 %collective-permute-start.15 = (s16[25,16,128]{2,1,0:T(8,128)(2,1)S(1)}, s16[25,16,128]{2,1,0:T(8,128)(2,1)S(1)}, u32[]{:S(2)}, u32[]{:S(2)}) collective-permute-start(s16[25,16,128]{2,1,0:T(8,128)(2,1)S(1)} %cross_kernel.7.refs_0_.mine_ref), channel_id=1, source_target_pairs={{0,8},{1,17},{2,10},{3,19},{4,12},{5,21},{6,14},{7,23},{8,0},{9,25... | collective-permute-start | bytes 307208 | tf_op jit(solution)/shard_map/ppermute | solution.py:203
  35.0 3.5 %collective-permute-done.10.other_ref = s16[25,16,128]{2,1,0:T(8,128)(2,1)S(1)} collective-permute-done((s16[25,16,128]{2,1,0:T(8,128)(2,1)S(1)}, s16[25,16,128]{2,1,0:T(8,128)(2,1)S(1)}, u32[]{:S(2)}, u32[]{:S(2)}) %collective-permute-start.10) | collective-permute-done | bytes 102432 | tf_op jit(solution)/shard_map/ppermute | solution.py:203
  38.9 1.8 %collective-permute-start.18 = (bf16[2,12,16,128]{3,2,1,0:T(8,128)(2,1)S(1)}, bf16[2,12,16,128]{3,2,1,0:T(8,128)(2,1)S(1)}, u32[]{:S(2)}, u32[]{:S(2)}) collective-permute-start(bf16[2,12,16,128]{3,2,1,0:T(8,128)(2,1)S(1)} %final_kernel.5.refs_0_.mine_ref), channel_id=1, source_target_pairs={{0,4},{1,17},{2,6},{3,19},{4,0},{5,21},{6,2},{7,23},{8,12},{9,25},... | collective-permute-start | bytes 294920 | tf_op jit(solution)/shard_map/ppermute | solution.py:203
  40.7 1.3 %collective-permute-done.16.other_ref = bf16[2,12,16,128]{3,2,1,0:T(8,128)(2,1)S(1)} collective-permute-done((bf16[2,12,16,128]{3,2,1,0:T(8,128)(2,1)S(1)}, bf16[2,12,16,128]{3,2,1,0:T(8,128)(2,1)S(1)}, u32[]{:S(2)}, u32[]{:S(2)}) %collective-permute-start.16) | collective-permute-done | bytes 98336 | tf_op jit(solution)/shard_map/ppermute | solution.py:203
  42.0 1.6 %collective-permute-start.20 = (bf16[2,12,16,128]{3,2,1,0:T(8,128)(2,1)S(1)}, bf16[2,12,16,128]{3,2,1,0:T(8,128)(2,1)S(1)}, u32[]{:S(2)}, u32[]{:S(2)}) collective-permute-start(bf16[2,12,16,128]{3,2,1,0:T(8,128)(2,1)S(1)} %final_kernel.7.refs_0_.mine_ref), channel_id=1, source_target_pairs={{0,16},{1,5},{2,18},{3,7},{4,20},{5,1},{6,22},{7,3},{8,24},{9,13},... | collective-permute-start | bytes 294920 | tf_op jit(solution)/shard_map/ppermute | solution.py:203
  44.3 2.5 %collective-permute-start.17 = (bf16[2,2,12,16,128]{4,3,2,1,0:T(8,128)(2,1)S(1)}, bf16[2,2,12,16,128]{4,3,2,1,0:T(8,128)(2,1)S(1)}, u32[]{:S(2)}, u32[]{:S(2)}) collective-permute-start(bf16[2,2,12,16,128]{4,3,2,1,0:T(8,128)(2,1)S(1)} %merge_kernel.5.refs_0_.refs_2_), channel_id=1, source_target_pairs={{0,8},{1,5},{2,10},{3,7},{4,12},{5,1},{6,14},{7,3},{8,0},{9,13},{1... | collective-permute-start | bytes 589832 | tf_op jit(solution)/shard_map/ppermute | solution.py:203
  48.3 1.6 %collective-permute-start.21 = (bf16[2,2,12,16,128]{4,3,2,1,0:T(8,128)(2,1)S(1)}, bf16[2,2,12,16,128]{4,3,2,1,0:T(8,128)(2,1)S(1)}, u32[]{:S(2)}, u32[]{:S(2)}) collective-permute-start(bf16[2,2,12,16,128]{4,3,2,1,0:T(8,128)(2,1)S(1)} %merge_kernel.7.refs_3_), channel_id=1, source_target_pairs={{0,4},{1,9},{2,6},{3,11},{4,0},{5,13},{6,2},{7,15},{8,12},{9,1},{1... | collective-permute-start | bytes 589832 | tf_op jit(solution)/shard_map/ppermute | solution.py:203
  49.8 1.7 %collective-permute-done.22.refs_4_ = bf16[2,2,12,16,128]{4,3,2,1,0:T(8,128)(2,1)S(1)} collective-permute-done((bf16[2,2,12,16,128]{4,3,2,1,0:T(8,128)(2,1)S(1)}, bf16[2,2,12,16,128]{4,3,2,1,0:T(8,128)(2,1)S(1)}, u32[]{:S(2)}, u32[]{:S(2)}) %collective-permute-start.22) | collective-permute-done | bytes 196640 | tf_op jit(solution)/shard_map/ppermute | solution.py:203
  51.5 1.6 %place_part.2.refs_3_ = bf16[4,24,64,128]{3,2,1,0:T(8,128)(2,1)} custom-call(s32[12]{0:T(128)S(1)} %pad_add_fusion.info, bf16[2,2,12,16,128]{4,3,2,1,0:T(8,128)(2,1)S(1)} %merge_kernel.4.refs_0_, bf16[2,2,12,16,128]{4,3,2,1,0:T(8,128)(2,1)S(1)} %merge_kernel.6.refs_0_.refs_1_, bf16[2,2,12,16,128]{4,3,2,1,0:T(8,128)(2,1)S(1)} %merge_kernel.5.refs_0_.refs_2_, ...), custom_call_target="tpu_custom_call" | custom-call | tf_op jit(solution)/shard_map/place_part/pallas_call | solution.py:281
  53.2 2.4 %collective-permute-done.19.refs_1_ = bf16[2,2,12,16,128]{4,3,2,1,0:T(8,128)(2,1)S(1)} collective-permute-done((bf16[2,2,12,16,128]{4,3,2,1,0:T(8,128)(2,1)S(1)}, bf16[2,2,12,16,128]{4,3,2,1,0:T(8,128)(2,1)S(1)}, u32[]{:S(2)}, u32[]{:S(2)}) %collective-permute-start.19) | collective-permute-done | bytes 196640 | tf_op jit(solution)/shard_map/ppermute | solution.py:203
  55.6 1.5 %place_part.3 = bf16[4,24,64,128]{3,2,1,0:T(8,128)(2,1)} custom-call(s32[12]{0:T(128)S(1)} %pad_add_fusion.info, bf16[2,2,12,16,128]{4,3,2,1,0:T(8,128)(2,1)S(1)} %collective-permute-done.17.refs_0_, bf16[2,2,12,16,128]{4,3,2,1,0:T(8,128)(2,1)S(1)} %collective-permute-done.19.refs_1_, ...), custom_call_target="tpu_custom_call", output_to_operand_aliasing={{}: (4, {})} | custom-call | tf_op jit(solution)/shard_map/place_part/pallas_call | solution.py:281
  (52 shorter events, 9.0 us)
Async XLA Ops:
  0.9 6.1 %collective-permute-start.1 = (bf16[2,4,4,16,128]{4,3,2,1,0:T(8,128)(2,1)S(1)}, bf16[2,4,4,16,128]{4,3,2,1,0:T(8,128)(2,1)S(1)}, u32[]{:S(2)}, u32[]{:S(2)}) collective-permute-start(bf16[2,4,4,16,128]{4,3,2,1,0:T(8,128)(2,1)S(1)} %pad_maximum_fusion.refs_0_), channel_id=1, source_target_pairs={{0,1},{1,0},{2,3},{3,2},{4,5},{5,4},{6,7},{7,6},{8,9},{9,8},{10,11... | collective-permute-start | bytes 393224 | tf_op jit(solution)/shard_map/ppermute | solution.py:206
  1.4 7.6 %collective-permute-start = (bf16[2,4,4,16,128]{4,3,2,1,0:T(8,128)(2,1)S(1)}, bf16[2,4,4,16,128]{4,3,2,1,0:T(8,128)(2,1)S(1)}, u32[]{:S(2)}, u32[]{:S(2)}) collective-permute-start(bf16[2,4,4,16,128]{4,3,2,1,0:T(8,128)(2,1)S(1)} %pad_maximum_fusion.refs_0_), channel_id=1, source_target_pairs={{0,2},{1,3},{2,0},{3,1},{4,6},{5,7},{6,4},{7,5},{8,10},{9,11},{10,... | collective-permute-start | bytes 393224 | tf_op jit(solution)/shard_map/ppermute | solution.py:206
  4.7 2.2 %copy-start = (s32[4]{0:T(128)S(1)}, s32[4]{0:T(128)}, u32[]{:S(2)}) copy-start(s32[4]{0:T(128)} %param.10) | copy-start | bytes 52
  9.0 5.3 %collective-permute-start.5 = (bf16[2,4,4,16,128]{4,3,2,1,0:T(8,128)(2,1)S(1)}, bf16[2,4,4,16,128]{4,3,2,1,0:T(8,128)(2,1)S(1)}, u32[]{:S(2)}, u32[]{:S(2)}) collective-permute-start(bf16[2,4,4,16,128]{4,3,2,1,0:T(8,128)(2,1)S(1)} %copy_kernel.1.refs_3_), channel_id=1, source_target_pairs={{0,1},{1,0},{2,3},{3,2},{4,5},{5,4},{6,7},{7,6},{8,9},{9,8},{10,11... | collective-permute-start | bytes 393224 | tf_op jit(solution)/shard_map/ppermute | solution.py:206
  9.2 9.2 %collective-permute-start.4 = (s16[49,16,128]{2,1,0:T(8,128)(2,1)S(1)}, s16[49,16,128]{2,1,0:T(8,128)(2,1)S(1)}, u32[]{:S(2)}, u32[]{:S(2)}) collective-permute-start(s16[49,16,128]{2,1,0:T(8,128)(2,1)S(1)} %get-tuple-element.26), channel_id=1, source_target_pairs={{0,4},{1,9},{2,6},{3,11},{4,0},{5,13},{6,2},{7,15},{8,12},{9,1},{1... | collective-permute-start | bytes 602120 | tf_op jit(solution)/shard_map/ppermute | solution.py:203
  10.8 9.4 %collective-permute-start.3 = (s16[49,16,128]{2,1,0:T(8,128)(2,1)S(1)}, s16[49,16,128]{2,1,0:T(8,128)(2,1)S(1)}, u32[]{:S(2)}, u32[]{:S(2)}) collective-permute-start(s16[49,16,128]{2,1,0:T(8,128)(2,1)S(1)} %get-tuple-element.21.refs_0_), channel_id=1, source_target_pairs={{0,4},{1,17},{2,6},{3,19},{4,0},{5,21},{6,2},{7,23},{8,12},{9,25},... | collective-permute-start | bytes 602120 | tf_op jit(solution)/shard_map/ppermute | solution.py:203
  12.7 8.0 %collective-permute-start.2 = (s16[49,16,128]{2,1,0:T(8,128)(2,1)S(1)}, s16[49,16,128]{2,1,0:T(8,128)(2,1)S(1)}, u32[]{:S(2)}, u32[]{:S(2)}) collective-permute-start(s16[49,16,128]{2,1,0:T(8,128)(2,1)S(1)} %get-tuple-element.23.refs_3_), channel_id=1, source_target_pairs={{0,4},{1,9},{2,6},{3,11},{4,0},{5,13},{6,2},{7,15},{8,12},{9,1},{1... | collective-permute-start | bytes 602120 | tf_op jit(solution)/shard_map/ppermute | solution.py:203
  15.7 10.5 %collective-permute-start.8 = (s16[49,16,128]{2,1,0:T(8,128)(2,1)S(1)}, s16[49,16,128]{2,1,0:T(8,128)(2,1)S(1)}, u32[]{:S(2)}, u32[]{:S(2)}) collective-permute-start(s16[49,16,128]{2,1,0:T(8,128)(2,1)S(1)} %get-tuple-element.27.refs_0_), channel_id=1, source_target_pairs={{0,16},{1,5},{2,18},{3,7},{4,20},{5,1},{6,22},{7,3},{8,24},{9,13},... | collective-permute-start | bytes 602120 | tf_op jit(solution)/shard_map/ppermute | solution.py:203
  18.5 4.7 %collective-permute-start.9 = (s16[25,16,128]{2,1,0:T(8,128)(2,1)S(1)}, s16[25,16,128]{2,1,0:T(8,128)(2,1)S(1)}, u32[]{:S(2)}, u32[]{:S(2)}) collective-permute-start(s16[25,16,128]{2,1,0:T(8,128)(2,1)S(1)} %get-tuple-element.28.refs_0_), channel_id=1, source_target_pairs={{0,8},{1,5},{2,10},{3,7},{4,12},{5,1},{6,14},{7,3},{8,0},{9,13},{1... | collective-permute-start | bytes 307208 | tf_op jit(solution)/shard_map/ppermute | solution.py:203
  20.3 7.7 %collective-permute-start.7 = (s16[25,16,128]{2,1,0:T(8,128)(2,1)S(1)}, s16[25,16,128]{2,1,0:T(8,128)(2,1)S(1)}, u32[]{:S(2)}, u32[]{:S(2)}) collective-permute-start(s16[25,16,128]{2,1,0:T(8,128)(2,1)S(1)} %get-tuple-element.29.refs_0_), channel_id=1, source_target_pairs={{0,16},{1,5},{2,18},{3,7},{4,20},{5,1},{6,22},{7,3},{8,24},{9,13},... | collective-permute-start | bytes 307208 | tf_op jit(solution)/shard_map/ppermute | solution.py:203
  20.8 8.1 %collective-permute-start.6 = (s16[25,16,128]{2,1,0:T(8,128)(2,1)S(1)}, s16[25,16,128]{2,1,0:T(8,128)(2,1)S(1)}, u32[]{:S(2)}, u32[]{:S(2)}) collective-permute-start(s16[25,16,128]{2,1,0:T(8,128)(2,1)S(1)} %get-tuple-element.31.refs_0_), channel_id=1, source_target_pairs={{0,8},{1,5},{2,10},{3,7},{4,12},{5,1},{6,14},{7,3},{8,0},{9,13},{1... | collective-permute-start | bytes 307208 | tf_op jit(solution)/shard_map/ppermute | solution.py:203
  23.3 9.3 %collective-permute-start.13 = (s16[25,16,128]{2,1,0:T(8,128)(2,1)S(1)}, s16[25,16,128]{2,1,0:T(8,128)(2,1)S(1)}, u32[]{:S(2)}, u32[]{:S(2)}) collective-permute-start(s16[25,16,128]{2,1,0:T(8,128)(2,1)S(1)} %cross_kernel.4.refs_0_.mine_ref), channel_id=1, source_target_pairs={{0,16},{1,17},{2,18},{3,19},{4,20},{5,21},{6,22},{7,23},{8,24},{9,... | collective-permute-start | bytes 307208 | tf_op jit(solution)/shard_map/ppermute | solution.py:203
  26.3 6.4 %collective-permute-start.12 = (s16[25,16,128]{2,1,0:T(8,128)(2,1)S(1)}, s16[25,16,128]{2,1,0:T(8,128)(2,1)S(1)}, u32[]{:S(2)}, u32[]{:S(2)}) collective-permute-start(s16[25,16,128]{2,1,0:T(8,128)(2,1)S(1)} %get-tuple-element.35.refs_0_), channel_id=1, source_target_pairs={{0,4},{1,9},{2,6},{3,11},{4,0},{5,13},{6,2},{7,15},{8,12},{9,1},{1... | collective-permute-start | bytes 307208 | tf_op jit(solution)/shard_map/ppermute | solution.py:203
  28.1 6.8 %collective-permute-start.11 = (s16[25,16,128]{2,1,0:T(8,128)(2,1)S(1)}, s16[25,16,128]{2,1,0:T(8,128)(2,1)S(1)}, u32[]{:S(2)}, u32[]{:S(2)}) collective-permute-start(s16[25,16,128]{2,1,0:T(8,128)(2,1)S(1)} %cross_kernel.5.refs_0_.mine_ref), channel_id=1, source_target_pairs={{0,8},{1,9},{2,10},{3,11},{4,12},{5,13},{6,14},{7,15},{8,0},{9,1},... | collective-permute-start | bytes 307208 | tf_op jit(solution)/shard_map/ppermute | solution.py:203
  29.0 9.6 %collective-permute-start.10 = (s16[25,16,128]{2,1,0:T(8,128)(2,1)S(1)}, s16[25,16,128]{2,1,0:T(8,128)(2,1)S(1)}, u32[]{:S(2)}, u32[]{:S(2)}) collective-permute-start(s16[25,16,128]{2,1,0:T(8,128)(2,1)S(1)} %cross_kernel.6.refs_0_.mine_ref), channel_id=1, source_target_pairs={{0,16},{1,17},{2,18},{3,19},{4,20},{5,21},{6,22},{7,23},{8,24},{9,... | collective-permute-start | bytes 307208 | tf_op jit(solution)/shard_map/ppermute | solution.py:203
  32.8 9.1 %collective-permute-start.15 = (s16[25,16,128]{2,1,0:T(8,128)(2,1)S(1)}, s16[25,16,128]{2,1,0:T(8,128)(2,1)S(1)}, u32[]{:S(2)}, u32[]{:S(2)}) collective-permute-start(s16[25,16,128]{2,1,0:T(8,128)(2,1)S(1)} %cross_kernel.7.refs_0_.mine_ref), channel_id=1, source_target_pairs={{0,8},{1,17},{2,10},{3,19},{4,12},{5,21},{6,14},{7,23},{8,0},{9,25... | collective-permute-start | bytes 307208 | tf_op jit(solution)/shard_map/ppermute | solution.py:203
  34.7 7.2 %collective-permute-start.16 = (bf16[2,12,16,128]{3,2,1,0:T(8,128)(2,1)S(1)}, bf16[2,12,16,128]{3,2,1,0:T(8,128)(2,1)S(1)}, u32[]{:S(2)}, u32[]{:S(2)}) collective-permute-start(bf16[2,12,16,128]{3,2,1,0:T(8,128)(2,1)S(1)} %final_kernel.4.refs_0_.mine_ref), channel_id=1, source_target_pairs={{0,8},{1,9},{2,10},{3,11},{4,12},{5,13},{6,14},{7,15},{8,0},{9,1},... | collective-permute-start | bytes 294920 | tf_op jit(solution)/shard_map/ppermute | solution.py:203
  38.6 5.7 %collective-permute-start.14 = (bf16[2,12,16,128]{3,2,1,0:T(8,128)(2,1)S(1)}, bf16[2,12,16,128]{3,2,1,0:T(8,128)(2,1)S(1)}, u32[]{:S(2)}, u32[]{:S(2)}) collective-permute-start(bf16[2,12,16,128]{3,2,1,0:T(8,128)(2,1)S(1)} %final_kernel.6.refs_0_.mine_ref), channel_id=1, source_target_pairs={{0,4},{1,9},{2,6},{3,11},{4,0},{5,13},{6,2},{7,15},{8,12},{9,1},{1... | collective-permute-start | bytes 294920 | tf_op jit(solution)/shard_map/ppermute | solution.py:203
  38.9 7.9 %collective-permute-start.18 = (bf16[2,12,16,128]{3,2,1,0:T(8,128)(2,1)S(1)}, bf16[2,12,16,128]{3,2,1,0:T(8,128)(2,1)S(1)}, u32[]{:S(2)}, u32[]{:S(2)}) collective-permute-start(bf16[2,12,16,128]{3,2,1,0:T(8,128)(2,1)S(1)} %final_kernel.5.refs_0_.mine_ref), channel_id=1, source_target_pairs={{0,4},{1,17},{2,6},{3,19},{4,0},{5,21},{6,2},{7,23},{8,12},{9,25},... | collective-permute-start | bytes 294920 | tf_op jit(solution)/shard_map/ppermute | solution.py:203
  42.0 6.2 %collective-permute-start.20 = (bf16[2,12,16,128]{3,2,1,0:T(8,128)(2,1)S(1)}, bf16[2,12,16,128]{3,2,1,0:T(8,128)(2,1)S(1)}, u32[]{:S(2)}, u32[]{:S(2)}) collective-permute-start(bf16[2,12,16,128]{3,2,1,0:T(8,128)(2,1)S(1)} %final_kernel.7.refs_0_.mine_ref), channel_id=1, source_target_pairs={{0,16},{1,5},{2,18},{3,7},{4,20},{5,1},{6,22},{7,3},{8,24},{9,13},... | collective-permute-start | bytes 294920 | tf_op jit(solution)/shard_map/ppermute | solution.py:203
  43.7 7.8 %collective-permute-start.22 = (bf16[2,2,12,16,128]{4,3,2,1,0:T(8,128)(2,1)S(1)}, bf16[2,2,12,16,128]{4,3,2,1,0:T(8,128)(2,1)S(1)}, u32[]{:S(2)}, u32[]{:S(2)}) collective-permute-start(bf16[2,2,12,16,128]{4,3,2,1,0:T(8,128)(2,1)S(1)} %merge_kernel.4.refs_0_), channel_id=1, source_target_pairs={{0,4},{1,5},{2,6},{3,7},{4,0},{5,1},{6,2},{7,3},{8,12},{9,13},{10,... | collective-permute-start | bytes 589832 | tf_op jit(solution)/shard_map/ppermute | solution.py:203
  44.3 11.2 %collective-permute-start.17 = (bf16[2,2,12,16,128]{4,3,2,1,0:T(8,128)(2,1)S(1)}, bf16[2,2,12,16,128]{4,3,2,1,0:T(8,128)(2,1)S(1)}, u32[]{:S(2)}, u32[]{:S(2)}) collective-permute-start(bf16[2,2,12,16,128]{4,3,2,1,0:T(8,128)(2,1)S(1)} %merge_kernel.5.refs_0_.refs_2_), channel_id=1, source_target_pairs={{0,8},{1,5},{2,10},{3,7},{4,12},{5,1},{6,14},{7,3},{8,0},{9,13},{1... | collective-permute-start | bytes 589832 | tf_op jit(solution)/shard_map/ppermute | solution.py:203
  46.8 8.7 %collective-permute-start.19 = (bf16[2,2,12,16,128]{4,3,2,1,0:T(8,128)(2,1)S(1)}, bf16[2,2,12,16,128]{4,3,2,1,0:T(8,128)(2,1)S(1)}, u32[]{:S(2)}, u32[]{:S(2)}) collective-permute-start(bf16[2,2,12,16,128]{4,3,2,1,0:T(8,128)(2,1)S(1)} %merge_kernel.6.refs_0_.refs_1_), channel_id=1, source_target_pairs={{0,16},{1,5},{2,18},{3,7},{4,20},{5,1},{6,22},{7,3},{8,24},{9,13},... | collective-permute-start | bytes 589832 | tf_op jit(solution)/shard_map/ppermute | solution.py:203
  48.3 7.3 %collective-permute-start.21 = (bf16[2,2,12,16,128]{4,3,2,1,0:T(8,128)(2,1)S(1)}, bf16[2,2,12,16,128]{4,3,2,1,0:T(8,128)(2,1)S(1)}, u32[]{:S(2)}, u32[]{:S(2)}) collective-permute-start(bf16[2,2,12,16,128]{4,3,2,1,0:T(8,128)(2,1)S(1)} %merge_kernel.7.refs_3_), channel_id=1, source_target_pairs={{0,4},{1,9},{2,6},{3,11},{4,0},{5,13},{6,2},{7,15},{8,12},{9,1},{1... | collective-permute-start | bytes 589832 | tf_op jit(solution)/shard_map/ppermute | solution.py:203

commit v2 on v1

--- a/solution.py
+++ b/solution.py
@@ -8,11 +8,9 @@
 from jax.sharding import PartitionSpec as P
 
 BITS = {"y": 0, "z0": 1, "z1": 2}
-ORDERS = ((("y", "z0", "z1", "z0", "y"), ("z0", "y", "z1", "z0", "y")), (("y", "z1", "z0", "y", "z1"), ("z1", "y", "z0", "z1", "y")), (("y", "z0", "z1", "y", "z0"), ("z0", "y", "z1", "z0", "y")), (("z1", "y", "z0", "z1", "y"), ("y", "z0", "z1", "y", "z0")))
-STEPS = (0, 1, 2, 0, 3, 1, 2, 0, 3, 1, 2, 0, 3, 2, 1, 3)
-PLACES = (((0, 0), (1, 0), (2, 0), (3, 0), (0, 1)), ((2, 1), (1, 1), (3, 1)))
-CHAIN = (1, 1, 1, 1, 1, 1, 1, 1, 1, 1, 1, 1, 1, 1, 1, 1)
-FIRST, COL, CORE, FIELDS = 4, 5, 6, 8
+ORDERS = ((("y", "z0", "z1", "y", "z0"), ("y", "z0", "z1", "y", "z0")), (("z1", "y", "z0", "z1", "y"), ("z1", "y", "z0", "z1", "y")), (("y", "z0", "z1", "z0", "y"), ("y", "z0", "z1", "z0", "y")), (("y", "z0", "z1", "y", "z0"), ("y", "z0", "z1", "y", "z0")))
+STEPS = (0, 2, 0, 1, 3, 2, 1, 0, 3, 2, 1, 0, 3, 2, 1, 3)
+PLACES = (((0, 0), (1, 0), (2, 0), (3, 0), (0, 1)), ((1, 1), (2, 1), (3, 1)))
 GROUP = 3
 STEPS_PER_OCTAVE = 128.0
 TOP = 32512.0
@@ -50,14 +48,13 @@
     ]
 
 
-def pack_left(info, at, sigma_ref, left_ref, row):
+def pack_left(sigma_ref, keep_ref, left_ref, row):
     _, nt, nb, ni, width = sigma_ref.shape
     half = width // 2
     for t in range(nt):
         for b in range(nb):
-            live = info[FIRST] + b <= info[at + t]
-            ret = jnp.where(live, sigma_ref[0, t, b], jnp.zeros((), jnp.bfloat16))
-            less = jnp.where(live, sigma_ref[1, t, b], jnp.zeros((), jnp.bfloat16))
+            ret = sigma_ref[0, t, b] * keep_ref[t, b]
+            less = sigma_ref[1, t, b] * keep_ref[t, b]
             cols = slice(b * width, (b + 1) * width)
             rows = slice(row + t * ni, row + (t + 1) * ni)
             left_ref[rows, cols] = jnp.concatenate([ret[:, :half], less[:, :half]], axis=1)
@@ -65,14 +62,21 @@
             left_ref[rows, cols] = jnp.concatenate([ret[:, half:], less[:, half:]], axis=1)
 
 
-def relative(info, orders, bits):
-    spots = [[lax.bitwise_xor(info[BITS[d]], bits[d]) for d in order] for order in orders]
-    return [jnp.where(info[CORE] == 0, *pair) for pair in zip(*spots)]
-
-
-def spots_of(info, orders, nt):
+def own_bits():
+    hist = lax.axis_index("hist")
+    bits = {d: lax.shift_right_logical(hist, at) & 1 for d, at in BITS.items()}
+    return bits, lax.axis_index("col") & 1
+
+
+def relative(own, core, orders, bits):
+    spots = [[lax.bitwise_xor(own[d], bits[d]) for d in order] for order in orders]
+    return [one if one is two else jnp.where(core == 0, one, two) for one, two in zip(*spots)]
+
+
+def spots_of(orders, nt):
+    own, core = own_bits()
     dims = [order[:3] for order in orders]
-    return [[relative(info, dims, {"y": side, "z0": t % 2, "z1": t // 2}) for t in range(nt)] for side in range(2)]
+    return [[relative(own, core, dims, {"y": side, "z0": t % 2, "z1": t // 2}) for t in range(nt)] for side in range(2)]
 
 
 def add_pair(spots, both, pair, term_ref):
@@ -89,15 +93,15 @@
             term_ref[tuple(spots[side][t]) + (c,)] = value[t * ni:(t + 1) * ni]
 
 
-def part_kernel(orders, info, *refs):
+def part_kernel(orders, keep_ref, *refs):
     n = len(orders)
     sigma_refs, (gless_ref, gadv_ref) = refs[:n], refs[n:n + 2]
     outs, (left_ref, term_ref) = refs[-2 * n - 2:-2], refs[-2:]
     nb, ncol, norb, width = gless_ref.shape
     rows = left_ref.shape[0] // n
     for at, sigma_ref in enumerate(sigma_refs):
-        pack_left(info, FIELDS, sigma_ref, left_ref, at * rows)
-    spots = [spots_of(info, order, rows // (2 * term_ref.shape[-2])) for order in orders]
+        pack_left(sigma_ref, keep_ref, left_ref, at * rows)
+    spots = [spots_of(order, rows // (2 * term_ref.shape[-2])) for order in orders]
     for pair in range(ncol // 2):
         sides = []
         for c in (2 * pair, 2 * pair + 1):
@@ -109,9 +113,9 @@
         for at in range(n):
             add_pair(spots[at], both[at * rows:(at + 1) * rows], pair, term_ref.at[at])
     for at in range(n):
-        keep_ref, out_ref = outs[2 * at:2 * at + 2]
+        kept_ref, out_ref = outs[2 * at:2 * at + 2]
         _, n1, n2, half_columns, ni, _ = term_ref.shape[1:]
-        keep_ref[0] = term_ref[at, 0]
+        kept_ref[0] = term_ref[at, 0]
 
         def read(first):
             block, c = divmod(first, half_columns)
@@ -162,19 +166,20 @@
     refs[-1][...] = in_ref[...]
 
 
-def place_kernel(items, info, *refs):
+def place_kernel(items, *refs):
     blocks, out_ref, sem = refs[:len(items)], refs[-2], refs[-1]
+    own, core = own_bits()
     copies = []
     for block, (chunk, orders, last) in zip(blocks, items):
         nc, ni, _ = block.shape[-3:]
-        row = pl.multiple_of(lax.bitwise_xor(info[COL], chunk) * ni, ni)
+        row = pl.multiple_of(lax.bitwise_xor(lax.axis_index("col"), chunk) * ni, ni)
         for second in range(2):
             for first in range(2):
                 places = []
                 for order in orders:
                     bits = dict(zip(order[2:], (first, second, last)))
-                    places.append([lax.bitwise_xor(info[BITS[d]], bits[d]) for d in ("y", "z0", "z1")])
-                y, z0, z1 = (jnp.where(info[CORE] == 0, *pair) for pair in zip(*places))
+                    places.append([lax.bitwise_xor(own[d], bits[d]) for d in ("y", "z0", "z1")])
+                y, z0, z1 = (jnp.where(core == 0, *pair) for pair in zip(*places))
                 target = out_ref.at[2 * z1 + z0, pl.ds(y * nc, nc), pl.ds(row, ni)]
                 copies.append(pltpu.make_async_copy(block.at[second, first], target, sem.at[len(copies)]))
     for copy in copies:
@@ -188,12 +193,6 @@
     _, ncol, norb, _ = green_less.shape
     nc = ncol // 2
     hist = lax.axis_index("hist")
-    col = lax.axis_index("col")
-    field = jnp.arange(FIELDS, dtype=jnp.int32)
-    bit = lax.shift_right_logical(jnp.where(field == CORE, col << CORE, hist), field) & 1
-    own = jnp.where(field == FIRST, hist * nb, jnp.where(field == COL, col, bit))
-    info = jnp.concatenate([own, time_now])
-
     def swap(v, chunk, stage):
         pairs = []
         for h in range(n_hist):
@@ -205,7 +204,6 @@
     def swap_col(v, k):
         return lax.ppermute(v, "col", [(i, i ^ k) for i in range(n_col)])
 
-    smem = pl.BlockSpec(memory_space=pltpu.SMEM)
     vmem = pl.BlockSpec(memory_space=pltpu.VMEM)
     hbm = pl.BlockSpec(memory_space=pltpu.HBM)
 
@@ -216,17 +214,19 @@
     tbar = hist * nb + jnp.arange(nb, dtype=jnp.int32)
     after = (tbar[:, None] >= col_start[None, :])[:, :, None, None]
     zero = jnp.zeros((), green_less.dtype)
+    before = (tbar[None, :] <= time_now[:, None]).astype(sigma_ret.dtype)
+    keep = jnp.broadcast_to(before[:, :, None, None], sigma_ret.shape)
     masked = [jnp.where(after, green, zero) for green in (green_less, green_adv)]
     near = swap_col(own_sigma, 1)
     far = swap_col(own_sigma, 2)
 
-    def call(kernel, out_shape, args, before, scratch=(), cost=None, specs=()):
+    def call(kernel, out_shape, args, before, scratch=(), cost=None):
         args = list(args) + ([] if before is None else [before])
         many = isinstance(out_shape, list)
         return pl.pallas_call(
             kernel,
             out_shape=out_shape,
-            in_specs=list(specs) + [vmem] * (len(args) - len(specs)),
+            in_specs=[vmem] * len(args),
             out_specs=[vmem] * len(out_shape) if many else vmem,
             scratch_shapes=list(scratch),
             compiler_params=PARAMS,
@@ -237,17 +237,16 @@
     def partial(orders, blocks, before):
         n = len(orders)
         rows = 2 * nt * ni
-        keep = jax.ShapeDtypeStruct((1, 2, 2, nc, ni, width), jnp.float32)
+        kept = jax.ShapeDtypeStruct((1, 2, 2, nc, ni, width), jnp.float32)
         flops = 2 * n * rows * 2 * nb * norb * ncol * width
         out = call(
             functools.partial(part_kernel, orders),
-            [keep, codes_of(4)] * n,
-            [info, *blocks, *masked],
+            [kept, codes_of(4)] * n,
+            [keep, *blocks, *masked],
             before,
             [pltpu.VMEM((n * rows, nb * width), jnp.bfloat16),
              pltpu.VMEM((n, 2, 2, 2, nc, ni, width), jnp.float32)],
             pl.CostEstimate(flops=flops, bytes_accessed=green_less.size * 4, transcendentals=0),
-            [smem],
         )
         return [out[2 * at:2 * at + 2] for at in range(n)]
 
@@ -281,13 +280,13 @@
         return pl.pallas_call(
             functools.partial(place_kernel, [(k, ORDERS[k], last) for k, last in items]),
             out_shape=jax.ShapeDtypeStruct((nt, ncol, norb, width), jnp.bfloat16),
-            in_specs=[smem] + [vmem] * n + [hbm] * len(extra),
+            in_specs=[vmem] * n + [hbm] * len(extra),
             out_specs=hbm,
             scratch_shapes=[pltpu.SemaphoreType.DMA((4 * n,))],
-            input_output_aliases={1 + n: 0} if extra else {},
+            input_output_aliases={n: 0} if extra else {},
             compiler_params=PARAMS,
             name="place_part",
-        )(info, *[blocks[k][last] for k, last in items], *extra)
+        )(*[blocks[k][last] for k, last in items], *extra)
 
     state = partial(ORDERS[:2], [own_sigma, near], None)
     passed = call(copy_kernel, jax.ShapeDtypeStruct(far.shape, far.dtype), [far], state[1][1])
@@ -295,8 +294,8 @@
     state += partial(ORDERS[3:], [swap_col(passed, 1)], state[2][1])
     last = state[3][1]
     todo = [[fold, cross, final, merge] for _ in range(n_col)]
-    for k, chained in zip(STEPS, CHAIN):
-        state[k], last = todo[k].pop(0)(state[k], k, last if chained else None)
+    for k in STEPS:
+        state[k], last = todo[k].pop(0)(state[k], k, last)
     blocks = [(state[k], swap(state[k], k, 4)) for k in range(n_col)]
     out = None
     for items in PLACES:

time: 57.2 us -> 56.6 us (0.990)
  waiting for transfers between devices: 10.7 us -> 17.6 us
  starting transfers between devices: 33.2 us -> 28.4 us
  Pallas kernels: 9.05 us -> 6.22 us
    ppermute x20, waiting for transfers between devices: 10.6 us -> 17.6 us  [swap(): return lax.ppermute(v, ('hist', 'col'), pairs)]
    ppermute x20, starting transfers between devices: 29.9 us -> 24.9 us  [swap(): return lax.ppermute(v, ('hist', 'col'), pairs)]
    pallas_call x20, Pallas kernels: 5.95 us -> 4.23 us  [call(): pl.pallas_call(kernel, out_shape=out_shape, in_specs=[vmem] * len(args),...]
    pallas_call x2, Pallas kernels: 3.1 us -> 2 us  [put(): pl.pallas_call(functools.partial(place_kernel, [(k, ORDERS[k], last) for...]
  transfers between devices with their start and end apart: 23 -> 23, of which waited for: 7 -> 11; matrix products, arithmetic and copies ran while one was open for 5% -> 5% of each run, Pallas kernels for 13% -> 9%
where the time goes in v2:
time: 56.6 us; the launch traced here: 56.4 us
  starting transfers between devices  28.4 us (50%)
  waiting for transfers between devices  17.6 us (31%)
  Pallas kernels  6.22 us (11%)
  other arithmetic  3.86 us (7%)
    ppermute x20, starting transfers between devices, swap(): return lax.ppermute(v, ('hist', 'col'), pairs)  24.9 us
    ppermute x20, waiting for transfers between devices, swap(): return lax.ppermute(v, ('hist', 'col'), pairs)  17.6 us
    pallas_call x20, Pallas kernels, call(): pl.pallas_call(kernel, out_shape=out_shape, in_specs=[vmem] * len(args),...  4.23 us
    ppermute x3, starting transfers between devices, swap_col(): return lax.ppermute(v, 'col', [(i, i ^ k) for i in range(n_col)])  3.58 us
    select_n x1, other arithmetic, staged(): jnp.where(after, green, zero)  2.17 us
    pallas_call x2, Pallas kernels, put(): pl.pallas_call(functools.partial(place_kernel, [(k, ORDERS[k], last) for...  2 us
  transfers between devices with their start and end apart: 23, of which 11 were waited for; matrix products, arithmetic and copies ran while one was open for 5% of the time, Pallas kernels for 9%

profile of v2, /device:TPU:0, one launch (start us, length us, event | category | flops | bytes accessed | tf_op | source)
XLA Modules:
  0.0 56.4 jit_solution(8835376170297459437)
XLA Ops:
  0.9 3.0 %collective-permute-start.3 = (bf16[2,4,4,16,128]{4,3,2,1,0:T(8,128)(2,1)S(1)}, bf16[2,4,4,16,128]{4,3,2,1,0:T(8,128)(2,1)S(1)}, u32[]{:S(2)}, u32[]{:S(2)}) collective-permute-start(bf16[2,4,4,16,128]{4,3,2,1,0:T(8,128)(2,1)S(1)} %pad_maximum_fusion.refs_0_), channel_id=1, source_target_pairs={{0,2},{1,3},{2,0},{3,1},{4,6},{5,7},{6,4},{7,5},{8,10},{9,11},{10,... | collective-permute-start | bytes 393224 | tf_op jit(solution)/shard_map/ppermute | solution.py:205
  4.6 2.2 %broadcast_select_fusion = (bf16[4,24,64,128]{3,2,1,0:T(8,128)(2,1)S(1)}, bf16[4,24,64,128]{3,2,1,0:T(8,128)(2,1)S(1)}) fusion(bf16[4,24,64,128]{3,2,1,0:T(8,128)(2,1)} %param.9, pred[4,24]{1,0:T(4,128)(4,1)S(1)} %broadcast_compare_fusion, bf16[4,24,64,128]{3,2,1,0:T(8,128)(2,1)} %param.8), kind=kLoop, calls=%fused_computation | loop fusion | flops 1572864 | bytes 6291552 | tf_op jit(solution)/shard_map/jit(_where)/select_n | solution.py:219
  7.0 1.4 %part_kernel.3 = (f32[1,2,2,12,16,128]{5,4,3,2,1,0:T(8,128)S(1)}, s16[49,16,128]{2,1,0:T(8,128)(2,1)S(1)}, f32[1,2,2,12,16,128]{5,4,3,2,1,0:T(8,128)S(1)}, s16[49,16,128]{2,1,0:T(8,128)(2,1)S(1)}) custom-call(bf16[4,4,16,128]{3,2,1,0:T(8,128)(2,1)S(1)} %broadcast_in_dim.27.keep_ref, bf16[2,4,4,16,128]{4,3,2,1,0:T(8,128)(2,1)S(1)} %pad_maximum_fusion.refs_0_, ...), custom_call_target="tpu_custom_call" | custom-call | flops 805306368 | bytes 3145728 | tf_op jit(solution)/shard_map/part_kernel/pallas_call | solution.py:226
  9.0 1.5 %collective-permute-start.2 = (s16[49,16,128]{2,1,0:T(8,128)(2,1)S(1)}, s16[49,16,128]{2,1,0:T(8,128)(2,1)S(1)}, u32[]{:S(2)}, u32[]{:S(2)}) collective-permute-start(s16[49,16,128]{2,1,0:T(8,128)(2,1)S(1)} %get-tuple-element.24), channel_id=1, source_target_pairs={{0,4},{1,5},{2,6},{3,7},{4,0},{5,1},{6,2},{7,3},{8,12},{9,13},{10,... | collective-permute-start | bytes 602120 | tf_op jit(solution)/shard_map/ppermute | solution.py:202
  10.5 2.6 %collective-permute-start.1 = (s16[49,16,128]{2,1,0:T(8,128)(2,1)S(1)}, s16[49,16,128]{2,1,0:T(8,128)(2,1)S(1)}, u32[]{:S(2)}, u32[]{:S(2)}) collective-permute-start(s16[49,16,128]{2,1,0:T(8,128)(2,1)S(1)} %get-tuple-element.22.refs_0_), channel_id=1, source_target_pairs={{0,16},{1,17},{2,18},{3,19},{4,20},{5,21},{6,22},{7,23},{8,24},{9,... | collective-permute-start | bytes 602120 | tf_op jit(solution)/shard_map/ppermute | solution.py:202
  15.4 1.6 %collective-permute-start.9 = (s16[49,16,128]{2,1,0:T(8,128)(2,1)S(1)}, s16[49,16,128]{2,1,0:T(8,128)(2,1)S(1)}, u32[]{:S(2)}, u32[]{:S(2)}) collective-permute-start(s16[49,16,128]{2,1,0:T(8,128)(2,1)S(1)} %get-tuple-element.26.refs_0_), channel_id=1, source_target_pairs={{0,4},{1,5},{2,6},{3,7},{4,0},{5,1},{6,2},{7,3},{8,12},{9,13},{10,... | collective-permute-start | bytes 602120 | tf_op jit(solution)/shard_map/ppermute | solution.py:202
  17.1 1.6 %collective-permute-start.5 = (s16[25,16,128]{2,1,0:T(8,128)(2,1)S(1)}, s16[25,16,128]{2,1,0:T(8,128)(2,1)S(1)}, u32[]{:S(2)}, u32[]{:S(2)}) collective-permute-start(s16[25,16,128]{2,1,0:T(8,128)(2,1)S(1)} %get-tuple-element.28.refs_0_), channel_id=1, source_target_pairs={{0,8},{1,9},{2,10},{3,11},{4,12},{5,13},{6,14},{7,15},{8,0},{9,1},... | collective-permute-start | bytes 307208 | tf_op jit(solution)/shard_map/ppermute | solution.py:202
  18.8 3.2 %collective-permute-done.6.in_ref = s16[49,16,128]{2,1,0:T(8,128)(2,1)S(1)} collective-permute-done((s16[49,16,128]{2,1,0:T(8,128)(2,1)S(1)}, s16[49,16,128]{2,1,0:T(8,128)(2,1)S(1)}, u32[]{:S(2)}, u32[]{:S(2)}) %collective-permute-start.6) | collective-permute-done | bytes 200736 | tf_op jit(solution)/shard_map/ppermute | solution.py:202
  22.1 1.6 %collective-permute-start.8 = (s16[25,16,128]{2,1,0:T(8,128)(2,1)S(1)}, s16[25,16,128]{2,1,0:T(8,128)(2,1)S(1)}, u32[]{:S(2)}, u32[]{:S(2)}) collective-permute-start(s16[25,16,128]{2,1,0:T(8,128)(2,1)S(1)} %get-tuple-element.30.refs_0_), channel_id=1, source_target_pairs={{0,8},{1,9},{2,10},{3,11},{4,12},{5,13},{6,14},{7,15},{8,0},{9,1},... | collective-permute-start | bytes 307208 | tf_op jit(solution)/shard_map/ppermute | solution.py:202
  25.5 1.8 %collective-permute-start.13 = (s16[25,16,128]{2,1,0:T(8,128)(2,1)S(1)}, s16[25,16,128]{2,1,0:T(8,128)(2,1)S(1)}, u32[]{:S(2)}, u32[]{:S(2)}) collective-permute-start(s16[25,16,128]{2,1,0:T(8,128)(2,1)S(1)} %cross_kernel.4.refs_0_.mine_ref), channel_id=1, source_target_pairs={{0,16},{1,17},{2,18},{3,19},{4,20},{5,21},{6,22},{7,23},{8,24},{9,... | collective-permute-start | bytes 307208 | tf_op jit(solution)/shard_map/ppermute | solution.py:202
  27.4 2.3 %collective-permute-start.12 = (s16[25,16,128]{2,1,0:T(8,128)(2,1)S(1)}, s16[25,16,128]{2,1,0:T(8,128)(2,1)S(1)}, u32[]{:S(2)}, u32[]{:S(2)}) collective-permute-start(s16[25,16,128]{2,1,0:T(8,128)(2,1)S(1)} %get-tuple-element.35.refs_0_), channel_id=1, source_target_pairs={{0,8},{1,9},{2,10},{3,11},{4,12},{5,13},{6,14},{7,15},{8,0},{9,1},... | collective-permute-start | bytes 307208 | tf_op jit(solution)/shard_map/ppermute | solution.py:202
  30.0 1.0 %collective-permute-start.10 = (s16[25,16,128]{2,1,0:T(8,128)(2,1)S(1)}, s16[25,16,128]{2,1,0:T(8,128)(2,1)S(1)}, u32[]{:S(2)}, u32[]{:S(2)}) collective-permute-start(s16[25,16,128]{2,1,0:T(8,128)(2,1)S(1)} %cross_kernel.6.refs_0_.mine_ref), channel_id=1, source_target_pairs={{0,8},{1,9},{2,10},{3,11},{4,12},{5,13},{6,14},{7,15},{8,0},{9,1},... | collective-permute-start | bytes 307208 | tf_op jit(solution)/shard_map/ppermute | solution.py:202
  31.0 1.9 %collective-permute-done.13.other_ref = s16[25,16,128]{2,1,0:T(8,128)(2,1)S(1)} collective-permute-done((s16[25,16,128]{2,1,0:T(8,128)(2,1)S(1)}, s16[25,16,128]{2,1,0:T(8,128)(2,1)S(1)}, u32[]{:S(2)}, u32[]{:S(2)}) %collective-permute-start.13) | collective-permute-done | bytes 102432 | tf_op jit(solution)/shard_map/ppermute | solution.py:202
  33.0 2.5 %collective-permute-done.12.in_ref = s16[25,16,128]{2,1,0:T(8,128)(2,1)S(1)} collective-permute-done((s16[25,16,128]{2,1,0:T(8,128)(2,1)S(1)}, s16[25,16,128]{2,1,0:T(8,128)(2,1)S(1)}, u32[]{:S(2)}, u32[]{:S(2)}) %collective-permute-start.12) | collective-permute-done | bytes 102432 | tf_op jit(solution)/shard_map/ppermute | solution.py:202
  35.7 1.8 %collective-permute-start.17 = (bf16[2,12,16,128]{3,2,1,0:T(8,128)(2,1)S(1)}, bf16[2,12,16,128]{3,2,1,0:T(8,128)(2,1)S(1)}, u32[]{:S(2)}, u32[]{:S(2)}) collective-permute-start(bf16[2,12,16,128]{3,2,1,0:T(8,128)(2,1)S(1)} %final_kernel.4.refs_0_.mine_ref), channel_id=1, source_target_pairs={{0,4},{1,5},{2,6},{3,7},{4,0},{5,1},{6,2},{7,3},{8,12},{9,13},{10,... | collective-permute-start | bytes 294920 | tf_op jit(solution)/shard_map/ppermute | solution.py:202
  37.5 1.3 %collective-permute-done.11.other_ref = s16[25,16,128]{2,1,0:T(8,128)(2,1)S(1)} collective-permute-done((s16[25,16,128]{2,1,0:T(8,128)(2,1)S(1)}, s16[25,16,128]{2,1,0:T(8,128)(2,1)S(1)}, u32[]{:S(2)}, u32[]{:S(2)}) %collective-permute-start.11) | collective-permute-done | bytes 102432 | tf_op jit(solution)/shard_map/ppermute | solution.py:202
  39.6 2.8 %collective-permute-start.14 = (bf16[2,12,16,128]{3,2,1,0:T(8,128)(2,1)S(1)}, bf16[2,12,16,128]{3,2,1,0:T(8,128)(2,1)S(1)}, u32[]{:S(2)}, u32[]{:S(2)}) collective-permute-start(bf16[2,12,16,128]{3,2,1,0:T(8,128)(2,1)S(1)} %final_kernel.6.refs_0_.mine_ref), channel_id=1, source_target_pairs={{0,16},{1,17},{2,18},{3,19},{4,20},{5,21},{6,22},{7,23},{8,24},{9,... | collective-permute-start | bytes 294920 | tf_op jit(solution)/shard_map/ppermute | solution.py:202
  42.4 1.6 %collective-permute-done.16.other_ref = s16[25,16,128]{2,1,0:T(8,128)(2,1)S(1)} collective-permute-done((s16[25,16,128]{2,1,0:T(8,128)(2,1)S(1)}, s16[25,16,128]{2,1,0:T(8,128)(2,1)S(1)}, u32[]{:S(2)}, u32[]{:S(2)}) %collective-permute-start.16) | collective-permute-done | bytes 102432 | tf_op jit(solution)/shard_map/ppermute | solution.py:202
  44.1 1.8 %collective-permute-start.20 = (bf16[2,12,16,128]{3,2,1,0:T(8,128)(2,1)S(1)}, bf16[2,12,16,128]{3,2,1,0:T(8,128)(2,1)S(1)}, u32[]{:S(2)}, u32[]{:S(2)}) collective-permute-start(bf16[2,12,16,128]{3,2,1,0:T(8,128)(2,1)S(1)} %final_kernel.7.refs_0_.mine_ref), channel_id=1, source_target_pairs={{0,4},{1,5},{2,6},{3,7},{4,0},{5,1},{6,2},{7,3},{8,12},{9,13},{10,... | collective-permute-start | bytes 294920 | tf_op jit(solution)/shard_map/ppermute | solution.py:202
  46.6 1.3 %collective-permute-start.19 = (bf16[2,2,12,16,128]{4,3,2,1,0:T(8,128)(2,1)S(1)}, bf16[2,2,12,16,128]{4,3,2,1,0:T(8,128)(2,1)S(1)}, u32[]{:S(2)}, u32[]{:S(2)}) collective-permute-start(bf16[2,2,12,16,128]{4,3,2,1,0:T(8,128)(2,1)S(1)} %merge_kernel.5.refs_0_.refs_2_), channel_id=1, source_target_pairs={{0,4},{1,5},{2,6},{3,7},{4,0},{5,1},{6,2},{7,3},{8,12},{9,13},{10,... | collective-permute-start | bytes 589832 | tf_op jit(solution)/shard_map/ppermute | solution.py:202
  50.1 2.1 %collective-permute-done.22.refs_4_ = bf16[2,2,12,16,128]{4,3,2,1,0:T(8,128)(2,1)S(1)} collective-permute-done((bf16[2,2,12,16,128]{4,3,2,1,0:T(8,128)(2,1)S(1)}, bf16[2,2,12,16,128]{4,3,2,1,0:T(8,128)(2,1)S(1)}, u32[]{:S(2)}, u32[]{:S(2)}) %collective-permute-start.22) | collective-permute-done | bytes 196640 | tf_op jit(solution)/shard_map/ppermute | solution.py:202
  52.2 1.1 %place_part.2.refs_3_ = bf16[4,24,64,128]{3,2,1,0:T(8,128)(2,1)} custom-call(bf16[2,2,12,16,128]{4,3,2,1,0:T(8,128)(2,1)S(1)} %merge_kernel.4.refs_0_, bf16[2,2,12,16,128]{4,3,2,1,0:T(8,128)(2,1)S(1)} %merge_kernel.6.refs_0_.refs_1_, bf16[2,2,12,16,128]{4,3,2,1,0:T(8,128)(2,1)S(1)} %merge_kernel.5.refs_0_.refs_2_, ...), custom_call_target="tpu_custom_call" | custom-call | tf_op jit(solution)/shard_map/place_part/pallas_call | solution.py:280
  53.4 1.1 %collective-permute-done.18.refs_0_ = bf16[2,2,12,16,128]{4,3,2,1,0:T(8,128)(2,1)S(1)} collective-permute-done((bf16[2,2,12,16,128]{4,3,2,1,0:T(8,128)(2,1)S(1)}, bf16[2,2,12,16,128]{4,3,2,1,0:T(8,128)(2,1)S(1)}, u32[]{:S(2)}, u32[]{:S(2)}) %collective-permute-start.18) | collective-permute-done | bytes 196640 | tf_op jit(solution)/shard_map/ppermute | solution.py:202
  54.5 1.1 %collective-permute-done.21.refs_2_ = bf16[2,2,12,16,128]{4,3,2,1,0:T(8,128)(2,1)S(1)} collective-permute-done((bf16[2,2,12,16,128]{4,3,2,1,0:T(8,128)(2,1)S(1)}, bf16[2,2,12,16,128]{4,3,2,1,0:T(8,128)(2,1)S(1)}, u32[]{:S(2)}, u32[]{:S(2)}) %collective-permute-start.21) | collective-permute-done | bytes 196640 | tf_op jit(solution)/shard_map/ppermute | solution.py:202
  (52 shorter events, 11.9 us)
Async XLA Ops:
  0.9 7.5 %collective-permute-start.3 = (bf16[2,4,4,16,128]{4,3,2,1,0:T(8,128)(2,1)S(1)}, bf16[2,4,4,16,128]{4,3,2,1,0:T(8,128)(2,1)S(1)}, u32[]{:S(2)}, u32[]{:S(2)}) collective-permute-start(bf16[2,4,4,16,128]{4,3,2,1,0:T(8,128)(2,1)S(1)} %pad_maximum_fusion.refs_0_), channel_id=1, source_target_pairs={{0,2},{1,3},{2,0},{3,1},{4,6},{5,7},{6,4},{7,5},{8,10},{9,11},{10,... | collective-permute-start | bytes 393224 | tf_op jit(solution)/shard_map/ppermute | solution.py:205
  3.9 3.0 %collective-permute-start = (bf16[2,4,4,16,128]{4,3,2,1,0:T(8,128)(2,1)S(1)}, bf16[2,4,4,16,128]{4,3,2,1,0:T(8,128)(2,1)S(1)}, u32[]{:S(2)}, u32[]{:S(2)}) collective-permute-start(bf16[2,4,4,16,128]{4,3,2,1,0:T(8,128)(2,1)S(1)} %pad_maximum_fusion.refs_0_), channel_id=1, source_target_pairs={{0,1},{1,0},{2,3},{3,2},{4,5},{5,4},{6,7},{7,6},{8,9},{9,8},{10,11... | collective-permute-start | bytes 393224 | tf_op jit(solution)/shard_map/ppermute | solution.py:205
  4.6 2.2 %copy-start = (s32[4]{0:T(128)S(1)}, s32[4]{0:T(128)}, u32[]{:S(2)}) copy-start(s32[4]{0:T(128)} %param.10) | copy-start | bytes 52
  8.4 6.1 %collective-permute-start.4 = (bf16[2,4,4,16,128]{4,3,2,1,0:T(8,128)(2,1)S(1)}, bf16[2,4,4,16,128]{4,3,2,1,0:T(8,128)(2,1)S(1)}, u32[]{:S(2)}, u32[]{:S(2)}) collective-permute-start(bf16[2,4,4,16,128]{4,3,2,1,0:T(8,128)(2,1)S(1)} %copy_kernel.1.refs_3_), channel_id=1, source_target_pairs={{0,1},{1,0},{2,3},{3,2},{4,5},{5,4},{6,7},{7,6},{8,9},{9,8},{10,11... | collective-permute-start | bytes 393224 | tf_op jit(solution)/shard_map/ppermute | solution.py:205
  9.0 8.0 %collective-permute-start.2 = (s16[49,16,128]{2,1,0:T(8,128)(2,1)S(1)}, s16[49,16,128]{2,1,0:T(8,128)(2,1)S(1)}, u32[]{:S(2)}, u32[]{:S(2)}) collective-permute-start(s16[49,16,128]{2,1,0:T(8,128)(2,1)S(1)} %get-tuple-element.24), channel_id=1, source_target_pairs={{0,4},{1,5},{2,6},{3,7},{4,0},{5,1},{6,2},{7,3},{8,12},{9,13},{10,... | collective-permute-start | bytes 602120 | tf_op jit(solution)/shard_map/ppermute | solution.py:202
  10.5 14.3 %collective-permute-start.1 = (s16[49,16,128]{2,1,0:T(8,128)(2,1)S(1)}, s16[49,16,128]{2,1,0:T(8,128)(2,1)S(1)}, u32[]{:S(2)}, u32[]{:S(2)}) collective-permute-start(s16[49,16,128]{2,1,0:T(8,128)(2,1)S(1)} %get-tuple-element.22.refs_0_), channel_id=1, source_target_pairs={{0,16},{1,17},{2,18},{3,19},{4,20},{5,21},{6,22},{7,23},{8,24},{9,... | collective-permute-start | bytes 602120 | tf_op jit(solution)/shard_map/ppermute | solution.py:202
  14.0 8.0 %collective-permute-start.6 = (s16[49,16,128]{2,1,0:T(8,128)(2,1)S(1)}, s16[49,16,128]{2,1,0:T(8,128)(2,1)S(1)}, u32[]{:S(2)}, u32[]{:S(2)}) collective-permute-start(s16[49,16,128]{2,1,0:T(8,128)(2,1)S(1)} %get-tuple-element.25.refs_3_), channel_id=1, source_target_pairs={{0,4},{1,5},{2,6},{3,7},{4,0},{5,1},{6,2},{7,3},{8,12},{9,13},{10,... | collective-permute-start | bytes 602120 | tf_op jit(solution)/shard_map/ppermute | solution.py:202
  15.4 11.9 %collective-permute-start.9 = (s16[49,16,128]{2,1,0:T(8,128)(2,1)S(1)}, s16[49,16,128]{2,1,0:T(8,128)(2,1)S(1)}, u32[]{:S(2)}, u32[]{:S(2)}) collective-permute-start(s16[49,16,128]{2,1,0:T(8,128)(2,1)S(1)} %get-tuple-element.26.refs_0_), channel_id=1, source_target_pairs={{0,4},{1,5},{2,6},{3,7},{4,0},{5,1},{6,2},{7,3},{8,12},{9,13},{10,... | collective-permute-start | bytes 602120 | tf_op jit(solution)/shard_map/ppermute | solution.py:202
  17.1 7.6 %collective-permute-start.5 = (s16[25,16,128]{2,1,0:T(8,128)(2,1)S(1)}, s16[25,16,128]{2,1,0:T(8,128)(2,1)S(1)}, u32[]{:S(2)}, u32[]{:S(2)}) collective-permute-start(s16[25,16,128]{2,1,0:T(8,128)(2,1)S(1)} %get-tuple-element.28.refs_0_), channel_id=1, source_target_pairs={{0,8},{1,9},{2,10},{3,11},{4,12},{5,13},{6,14},{7,15},{8,0},{9,1},... | collective-permute-start | bytes 307208 | tf_op jit(solution)/shard_map/ppermute | solution.py:202
  22.1 7.6 %collective-permute-start.8 = (s16[25,16,128]{2,1,0:T(8,128)(2,1)S(1)}, s16[25,16,128]{2,1,0:T(8,128)(2,1)S(1)}, u32[]{:S(2)}, u32[]{:S(2)}) collective-permute-start(s16[25,16,128]{2,1,0:T(8,128)(2,1)S(1)} %get-tuple-element.30.refs_0_), channel_id=1, source_target_pairs={{0,8},{1,9},{2,10},{3,11},{4,12},{5,13},{6,14},{7,15},{8,0},{9,1},... | collective-permute-start | bytes 307208 | tf_op jit(solution)/shard_map/ppermute | solution.py:202
  25.0 4.9 %collective-permute-start.7 = (s16[25,16,128]{2,1,0:T(8,128)(2,1)S(1)}, s16[25,16,128]{2,1,0:T(8,128)(2,1)S(1)}, u32[]{:S(2)}, u32[]{:S(2)}) collective-permute-start(s16[25,16,128]{2,1,0:T(8,128)(2,1)S(1)} %get-tuple-element.32.refs_0_), channel_id=1, source_target_pairs={{0,4},{1,5},{2,6},{3,7},{4,0},{5,1},{6,2},{7,3},{8,12},{9,13},{10,... | collective-permute-start | bytes 307208 | tf_op jit(solution)/shard_map/ppermute | solution.py:202
  25.5 7.5 %collective-permute-start.13 = (s16[25,16,128]{2,1,0:T(8,128)(2,1)S(1)}, s16[25,16,128]{2,1,0:T(8,128)(2,1)S(1)}, u32[]{:S(2)}, u32[]{:S(2)}) collective-permute-start(s16[25,16,128]{2,1,0:T(8,128)(2,1)S(1)} %cross_kernel.4.refs_0_.mine_ref), channel_id=1, source_target_pairs={{0,16},{1,17},{2,18},{3,19},{4,20},{5,21},{6,22},{7,23},{8,24},{9,... | collective-permute-start | bytes 307208 | tf_op jit(solution)/shard_map/ppermute | solution.py:202
  27.4 8.2 %collective-permute-start.12 = (s16[25,16,128]{2,1,0:T(8,128)(2,1)S(1)}, s16[25,16,128]{2,1,0:T(8,128)(2,1)S(1)}, u32[]{:S(2)}, u32[]{:S(2)}) collective-permute-start(s16[25,16,128]{2,1,0:T(8,128)(2,1)S(1)} %get-tuple-element.35.refs_0_), channel_id=1, source_target_pairs={{0,8},{1,9},{2,10},{3,11},{4,12},{5,13},{6,14},{7,15},{8,0},{9,1},... | collective-permute-start | bytes 307208 | tf_op jit(solution)/shard_map/ppermute | solution.py:202
  29.8 9.0 %collective-permute-start.11 = (s16[25,16,128]{2,1,0:T(8,128)(2,1)S(1)}, s16[25,16,128]{2,1,0:T(8,128)(2,1)S(1)}, u32[]{:S(2)}, u32[]{:S(2)}) collective-permute-start(s16[25,16,128]{2,1,0:T(8,128)(2,1)S(1)} %cross_kernel.5.refs_0_.mine_ref), channel_id=1, source_target_pairs={{0,16},{1,17},{2,18},{3,19},{4,20},{5,21},{6,22},{7,23},{8,24},{9,... | collective-permute-start | bytes 307208 | tf_op jit(solution)/shard_map/ppermute | solution.py:202
  30.0 9.5 %collective-permute-start.10 = (s16[25,16,128]{2,1,0:T(8,128)(2,1)S(1)}, s16[25,16,128]{2,1,0:T(8,128)(2,1)S(1)}, u32[]{:S(2)}, u32[]{:S(2)}) collective-permute-start(s16[25,16,128]{2,1,0:T(8,128)(2,1)S(1)} %cross_kernel.6.refs_0_.mine_ref), channel_id=1, source_target_pairs={{0,8},{1,9},{2,10},{3,11},{4,12},{5,13},{6,14},{7,15},{8,0},{9,1},... | collective-permute-start | bytes 307208 | tf_op jit(solution)/shard_map/ppermute | solution.py:202
  35.6 8.3 %collective-permute-start.16 = (s16[25,16,128]{2,1,0:T(8,128)(2,1)S(1)}, s16[25,16,128]{2,1,0:T(8,128)(2,1)S(1)}, u32[]{:S(2)}, u32[]{:S(2)}) collective-permute-start(s16[25,16,128]{2,1,0:T(8,128)(2,1)S(1)} %cross_kernel.7.refs_0_.mine_ref), channel_id=1, source_target_pairs={{0,16},{1,17},{2,18},{3,19},{4,20},{5,21},{6,22},{7,23},{8,24},{9,... | collective-permute-start | bytes 307208 | tf_op jit(solution)/shard_map/ppermute | solution.py:202
  35.7 6.7 %collective-permute-start.17 = (bf16[2,12,16,128]{3,2,1,0:T(8,128)(2,1)S(1)}, bf16[2,12,16,128]{3,2,1,0:T(8,128)(2,1)S(1)}, u32[]{:S(2)}, u32[]{:S(2)}) collective-permute-start(bf16[2,12,16,128]{3,2,1,0:T(8,128)(2,1)S(1)} %final_kernel.4.refs_0_.mine_ref), channel_id=1, source_target_pairs={{0,4},{1,5},{2,6},{3,7},{4,0},{5,1},{6,2},{7,3},{8,12},{9,13},{10,... | collective-permute-start | bytes 294920 | tf_op jit(solution)/shard_map/ppermute | solution.py:202
  38.9 7.7 %collective-permute-start.15 = (bf16[2,12,16,128]{3,2,1,0:T(8,128)(2,1)S(1)}, bf16[2,12,16,128]{3,2,1,0:T(8,128)(2,1)S(1)}, u32[]{:S(2)}, u32[]{:S(2)}) collective-permute-start(bf16[2,12,16,128]{3,2,1,0:T(8,128)(2,1)S(1)} %final_kernel.5.refs_0_.mine_ref), channel_id=1, source_target_pairs={{0,8},{1,9},{2,10},{3,11},{4,12},{5,13},{6,14},{7,15},{8,0},{9,1},... | collective-permute-start | bytes 294920 | tf_op jit(solution)/shard_map/ppermute | solution.py:202
  39.6 8.4 %collective-permute-start.14 = (bf16[2,12,16,128]{3,2,1,0:T(8,128)(2,1)S(1)}, bf16[2,12,16,128]{3,2,1,0:T(8,128)(2,1)S(1)}, u32[]{:S(2)}, u32[]{:S(2)}) collective-permute-start(bf16[2,12,16,128]{3,2,1,0:T(8,128)(2,1)S(1)} %final_kernel.6.refs_0_.mine_ref), channel_id=1, source_target_pairs={{0,16},{1,17},{2,18},{3,19},{4,20},{5,21},{6,22},{7,23},{8,24},{9,... | collective-permute-start | bytes 294920 | tf_op jit(solution)/shard_map/ppermute | solution.py:202
  44.1 5.7 %collective-permute-start.20 = (bf16[2,12,16,128]{3,2,1,0:T(8,128)(2,1)S(1)}, bf16[2,12,16,128]{3,2,1,0:T(8,128)(2,1)S(1)}, u32[]{:S(2)}, u32[]{:S(2)}) collective-permute-start(bf16[2,12,16,128]{3,2,1,0:T(8,128)(2,1)S(1)} %final_kernel.7.refs_0_.mine_ref), channel_id=1, source_target_pairs={{0,4},{1,5},{2,6},{3,7},{4,0},{5,1},{6,2},{7,3},{8,12},{9,13},{10,... | collective-permute-start | bytes 294920 | tf_op jit(solution)/shard_map/ppermute | solution.py:202
  45.8 6.4 %collective-permute-start.22 = (bf16[2,2,12,16,128]{4,3,2,1,0:T(8,128)(2,1)S(1)}, bf16[2,2,12,16,128]{4,3,2,1,0:T(8,128)(2,1)S(1)}, u32[]{:S(2)}, u32[]{:S(2)}) collective-permute-start(bf16[2,2,12,16,128]{4,3,2,1,0:T(8,128)(2,1)S(1)} %merge_kernel.4.refs_0_), channel_id=1, source_target_pairs={{0,8},{1,9},{2,10},{3,11},{4,12},{5,13},{6,14},{7,15},{8,0},{9,1},... | collective-permute-start | bytes 589832 | tf_op jit(solution)/shard_map/ppermute | solution.py:202
  46.6 6.7 %collective-permute-start.19 = (bf16[2,2,12,16,128]{4,3,2,1,0:T(8,128)(2,1)S(1)}, bf16[2,2,12,16,128]{4,3,2,1,0:T(8,128)(2,1)S(1)}, u32[]{:S(2)}, u32[]{:S(2)}) collective-permute-start(bf16[2,2,12,16,128]{4,3,2,1,0:T(8,128)(2,1)S(1)} %merge_kernel.5.refs_0_.refs_2_), channel_id=1, source_target_pairs={{0,4},{1,5},{2,6},{3,7},{4,0},{5,1},{6,2},{7,3},{8,12},{9,13},{10,... | collective-permute-start | bytes 589832 | tf_op jit(solution)/shard_map/ppermute | solution.py:202
  48.0 6.5 %collective-permute-start.18 = (bf16[2,2,12,16,128]{4,3,2,1,0:T(8,128)(2,1)S(1)}, bf16[2,2,12,16,128]{4,3,2,1,0:T(8,128)(2,1)S(1)}, u32[]{:S(2)}, u32[]{:S(2)}) collective-permute-start(bf16[2,2,12,16,128]{4,3,2,1,0:T(8,128)(2,1)S(1)} %merge_kernel.6.refs_0_.refs_1_), channel_id=1, source_target_pairs={{0,4},{1,5},{2,6},{3,7},{4,0},{5,1},{6,2},{7,3},{8,12},{9,13},{10,... | collective-permute-start | bytes 589832 | tf_op jit(solution)/shard_map/ppermute | solution.py:202
  49.8 5.7 %collective-permute-start.21 = (bf16[2,2,12,16,128]{4,3,2,1,0:T(8,128)(2,1)S(1)}, bf16[2,2,12,16,128]{4,3,2,1,0:T(8,128)(2,1)S(1)}, u32[]{:S(2)}, u32[]{:S(2)}) collective-permute-start(bf16[2,2,12,16,128]{4,3,2,1,0:T(8,128)(2,1)S(1)} %merge_kernel.7.refs_3_), channel_id=1, source_target_pairs={{0,8},{1,9},{2,10},{3,11},{4,12},{5,13},{6,14},{7,15},{8,0},{9,1},... | collective-permute-start | bytes 589832 | tf_op jit(solution)/shard_map/ppermute | solution.py:202

commit v3 on v2

--- a/solution.py
+++ b/solution.py
@@ -8,9 +8,9 @@
 from jax.sharding import PartitionSpec as P
 
 BITS = {"y": 0, "z0": 1, "z1": 2}
-ORDERS = ((("y", "z0", "z1", "y", "z0"), ("y", "z0", "z1", "y", "z0")), (("z1", "y", "z0", "z1", "y"), ("z1", "y", "z0", "z1", "y")), (("y", "z0", "z1", "z0", "y"), ("y", "z0", "z1", "z0", "y")), (("y", "z0", "z1", "y", "z0"), ("y", "z0", "z1", "y", "z0")))
-STEPS = (0, 2, 0, 1, 3, 2, 1, 0, 3, 2, 1, 0, 3, 2, 1, 3)
-PLACES = (((0, 0), (1, 0), (2, 0), (3, 0), (0, 1)), ((1, 1), (2, 1), (3, 1)))
+ORDERS = ((("y", "z0", "z1", "z0", "y"), ("z0", "y", "z1", "z0", "y")), (("y", "z1", "z0", "y", "z1"), ("z1", "y", "z0", "z1", "y")), (("y", "z0", "z1", "y", "z0"), ("z0", "y", "z1", "y", "z0")), (("z1", "y", "z0", "z1", "y"), ("y", "z0", "z1", "y", "z0")))
+STEPS = (0, 1, 2, 0, 3, 1, 2, 0, 3, 1, 2, 0, 3, 2, 1, 3)
+PLACES = (((0, 0), (1, 0), (2, 0), (3, 0), (0, 1)), ((2, 1), (1, 1), (3, 1)))
 GROUP = 3
 STEPS_PER_OCTAVE = 128.0
 TOP = 32512.0

time: 56.6 us -> 56.7 us (level)
  starting transfers between devices: 28.4 us -> 38.7 us
  waiting for transfers between devices: 17.6 us -> 7.47 us
    ppermute x20, starting transfers between devices: 24.9 us -> 35.4 us  [swap(): return lax.ppermute(v, ('hist', 'col'), pairs)]
    ppermute x20, waiting for transfers between devices: 17.6 us -> 7.47 us  [swap(): return lax.ppermute(v, ('hist', 'col'), pairs)]
  transfers between devices with their start and end apart: 23 -> 23, of which waited for: 11 -> 3; matrix products, arithmetic and copies ran while one was open for 5% -> 5% of each run, Pallas kernels for 9% -> 9%
where the time goes in v3:
time: 56.7 us; the launch traced here: 56.5 us
  starting transfers between devices  38.7 us (68%)
  waiting for transfers between devices  7.47 us (13%)
  Pallas kernels  6.23 us (11%)
  other arithmetic  3.86 us (7%)
    ppermute x20, starting transfers between devices, swap(): return lax.ppermute(v, ('hist', 'col'), pairs)  35.4 us
    ppermute x20, waiting for transfers between devices, swap(): return lax.ppermute(v, ('hist', 'col'), pairs)  7.47 us
    pallas_call x20, Pallas kernels, call(): pl.pallas_call(kernel, out_shape=out_shape, in_specs=[vmem] * len(args),...  4.23 us
    ppermute x3, starting transfers between devices, swap_col(): return lax.ppermute(v, 'col', [(i, i ^ k) for i in range(n_col)])  3.31 us
    select_n x1, other arithmetic, staged(): jnp.where(after, green, zero)  2.17 us
    pallas_call x2, Pallas kernels, put(): pl.pallas_call(functools.partial(place_kernel, [(k, ORDERS[k], last) for...  2 us
  transfers between devices with their start and end apart: 23, of which 3 were waited for; matrix products, arithmetic and copies ran while one was open for 5% of the time, Pallas kernels for 9%

profile of v3, /device:TPU:0, one launch (start us, length us, event | category | flops | bytes accessed | tf_op | source)
XLA Modules:
  0.0 56.5 jit_solution(11956712919115908022)
XLA Ops:
  1.4 2.6 %collective-permute-start = (bf16[2,4,4,16,128]{4,3,2,1,0:T(8,128)(2,1)S(1)}, bf16[2,4,4,16,128]{4,3,2,1,0:T(8,128)(2,1)S(1)}, u32[]{:S(2)}, u32[]{:S(2)}) collective-permute-start(bf16[2,4,4,16,128]{4,3,2,1,0:T(8,128)(2,1)S(1)} %pad_maximum_fusion.refs_0_), channel_id=1, source_target_pairs={{0,2},{1,3},{2,0},{3,1},{4,6},{5,7},{6,4},{7,5},{8,10},{9,11},{10,... | collective-permute-start | bytes 393224 | tf_op jit(solution)/shard_map/ppermute | solution.py:205
  4.7 2.2 %broadcast_select_fusion = (bf16[4,24,64,128]{3,2,1,0:T(8,128)(2,1)S(1)}, bf16[4,24,64,128]{3,2,1,0:T(8,128)(2,1)S(1)}) fusion(bf16[4,24,64,128]{3,2,1,0:T(8,128)(2,1)} %param.9, pred[4,24]{1,0:T(4,128)(4,1)S(1)} %broadcast_compare_fusion, bf16[4,24,64,128]{3,2,1,0:T(8,128)(2,1)} %param.8), kind=kLoop, calls=%fused_computation | loop fusion | flops 1572864 | bytes 6291552 | tf_op jit(solution)/shard_map/jit(_where)/select_n | solution.py:219
  7.1 1.4 %part_kernel.3 = (f32[1,2,2,12,16,128]{5,4,3,2,1,0:T(8,128)S(1)}, s16[49,16,128]{2,1,0:T(8,128)(2,1)S(1)}, f32[1,2,2,12,16,128]{5,4,3,2,1,0:T(8,128)S(1)}, s16[49,16,128]{2,1,0:T(8,128)(2,1)S(1)}) custom-call(bf16[4,4,16,128]{3,2,1,0:T(8,128)(2,1)S(1)} %broadcast_in_dim.27.keep_ref, bf16[2,4,4,16,128]{4,3,2,1,0:T(8,128)(2,1)S(1)} %pad_maximum_fusion.refs_0_, ...), custom_call_target="tpu_custom_call" | custom-call | flops 805306368 | bytes 3145728 | tf_op jit(solution)/shard_map/part_kernel/pallas_call | solution.py:226
  8.7 1.5 %collective-permute-start.4 = (s16[49,16,128]{2,1,0:T(8,128)(2,1)S(1)}, s16[49,16,128]{2,1,0:T(8,128)(2,1)S(1)}, u32[]{:S(2)}, u32[]{:S(2)}) collective-permute-start(s16[49,16,128]{2,1,0:T(8,128)(2,1)S(1)} %get-tuple-element.26), channel_id=1, source_target_pairs={{0,4},{1,9},{2,6},{3,11},{4,0},{5,13},{6,2},{7,15},{8,12},{9,1},{1... | collective-permute-start | bytes 602120 | tf_op jit(solution)/shard_map/ppermute | solution.py:202
  11.6 1.6 %collective-permute-start.2 = (s16[49,16,128]{2,1,0:T(8,128)(2,1)S(1)}, s16[49,16,128]{2,1,0:T(8,128)(2,1)S(1)}, u32[]{:S(2)}, u32[]{:S(2)}) collective-permute-start(s16[49,16,128]{2,1,0:T(8,128)(2,1)S(1)} %get-tuple-element.23.refs_3_), channel_id=1, source_target_pairs={{0,4},{1,9},{2,6},{3,11},{4,0},{5,13},{6,2},{7,15},{8,12},{9,1},{1... | collective-permute-start | bytes 602120 | tf_op jit(solution)/shard_map/ppermute | solution.py:202
  14.1 2.6 %collective-permute-start.8 = (s16[49,16,128]{2,1,0:T(8,128)(2,1)S(1)}, s16[49,16,128]{2,1,0:T(8,128)(2,1)S(1)}, u32[]{:S(2)}, u32[]{:S(2)}) collective-permute-start(s16[49,16,128]{2,1,0:T(8,128)(2,1)S(1)} %get-tuple-element.27.refs_0_), channel_id=1, source_target_pairs={{0,16},{1,5},{2,18},{3,7},{4,20},{5,1},{6,22},{7,3},{8,24},{9,13},... | collective-permute-start | bytes 602120 | tf_op jit(solution)/shard_map/ppermute | solution.py:202
  16.9 1.7 %collective-permute-start.9 = (s16[25,16,128]{2,1,0:T(8,128)(2,1)S(1)}, s16[25,16,128]{2,1,0:T(8,128)(2,1)S(1)}, u32[]{:S(2)}, u32[]{:S(2)}) collective-permute-start(s16[25,16,128]{2,1,0:T(8,128)(2,1)S(1)} %get-tuple-element.28.refs_0_), channel_id=1, source_target_pairs={{0,8},{1,5},{2,10},{3,7},{4,12},{5,1},{6,14},{7,3},{8,0},{9,13},{1... | collective-permute-start | bytes 307208 | tf_op jit(solution)/shard_map/ppermute | solution.py:202
  18.6 2.1 %collective-permute-start.7 = (s16[25,16,128]{2,1,0:T(8,128)(2,1)S(1)}, s16[25,16,128]{2,1,0:T(8,128)(2,1)S(1)}, u32[]{:S(2)}, u32[]{:S(2)}) collective-permute-start(s16[25,16,128]{2,1,0:T(8,128)(2,1)S(1)} %get-tuple-element.29.refs_0_), channel_id=1, source_target_pairs={{0,16},{1,5},{2,18},{3,7},{4,20},{5,1},{6,22},{7,3},{8,24},{9,13},... | collective-permute-start | bytes 307208 | tf_op jit(solution)/shard_map/ppermute | solution.py:202
  20.9 1.6 %collective-permute-start.6 = (s16[25,16,128]{2,1,0:T(8,128)(2,1)S(1)}, s16[25,16,128]{2,1,0:T(8,128)(2,1)S(1)}, u32[]{:S(2)}, u32[]{:S(2)}) collective-permute-start(s16[25,16,128]{2,1,0:T(8,128)(2,1)S(1)} %get-tuple-element.31.refs_0_), channel_id=1, source_target_pairs={{0,8},{1,5},{2,10},{3,7},{4,12},{5,1},{6,14},{7,3},{8,0},{9,13},{1... | collective-permute-start | bytes 307208 | tf_op jit(solution)/shard_map/ppermute | solution.py:202
  22.6 4.2 %collective-permute-start.13 = (s16[25,16,128]{2,1,0:T(8,128)(2,1)S(1)}, s16[25,16,128]{2,1,0:T(8,128)(2,1)S(1)}, u32[]{:S(2)}, u32[]{:S(2)}) collective-permute-start(s16[25,16,128]{2,1,0:T(8,128)(2,1)S(1)} %cross_kernel.4.refs_0_.mine_ref), channel_id=1, source_target_pairs={{0,16},{1,17},{2,18},{3,19},{4,20},{5,21},{6,22},{7,23},{8,24},{9,... | collective-permute-start | bytes 307208 | tf_op jit(solution)/shard_map/ppermute | solution.py:202
  26.9 1.6 %collective-permute-start.12 = (s16[25,16,128]{2,1,0:T(8,128)(2,1)S(1)}, s16[25,16,128]{2,1,0:T(8,128)(2,1)S(1)}, u32[]{:S(2)}, u32[]{:S(2)}) collective-permute-start(s16[25,16,128]{2,1,0:T(8,128)(2,1)S(1)} %get-tuple-element.35.refs_0_), channel_id=1, source_target_pairs={{0,4},{1,9},{2,6},{3,11},{4,0},{5,13},{6,2},{7,15},{8,12},{9,1},{1... | collective-permute-start | bytes 307208 | tf_op jit(solution)/shard_map/ppermute | solution.py:202
  29.2 3.3 %collective-permute-start.10 = (s16[25,16,128]{2,1,0:T(8,128)(2,1)S(1)}, s16[25,16,128]{2,1,0:T(8,128)(2,1)S(1)}, u32[]{:S(2)}, u32[]{:S(2)}) collective-permute-start(s16[25,16,128]{2,1,0:T(8,128)(2,1)S(1)} %cross_kernel.6.refs_0_.mine_ref), channel_id=1, source_target_pairs={{0,16},{1,17},{2,18},{3,19},{4,20},{5,21},{6,22},{7,23},{8,24},{9,... | collective-permute-start | bytes 307208 | tf_op jit(solution)/shard_map/ppermute | solution.py:202
  32.6 2.5 %collective-permute-start.15 = (s16[25,16,128]{2,1,0:T(8,128)(2,1)S(1)}, s16[25,16,128]{2,1,0:T(8,128)(2,1)S(1)}, u32[]{:S(2)}, u32[]{:S(2)}) collective-permute-start(s16[25,16,128]{2,1,0:T(8,128)(2,1)S(1)} %cross_kernel.7.refs_0_.mine_ref), channel_id=1, source_target_pairs={{0,8},{1,17},{2,10},{3,19},{4,12},{5,21},{6,14},{7,23},{8,0},{9,25... | collective-permute-start | bytes 307208 | tf_op jit(solution)/shard_map/ppermute | solution.py:202
  35.3 3.2 %collective-permute-done.10.other_ref = s16[25,16,128]{2,1,0:T(8,128)(2,1)S(1)} collective-permute-done((s16[25,16,128]{2,1,0:T(8,128)(2,1)S(1)}, s16[25,16,128]{2,1,0:T(8,128)(2,1)S(1)}, u32[]{:S(2)}, u32[]{:S(2)}) %collective-permute-start.10) | collective-permute-done | bytes 102432 | tf_op jit(solution)/shard_map/ppermute | solution.py:202
  38.6 1.0 %collective-permute-start.14 = (bf16[2,12,16,128]{3,2,1,0:T(8,128)(2,1)S(1)}, bf16[2,12,16,128]{3,2,1,0:T(8,128)(2,1)S(1)}, u32[]{:S(2)}, u32[]{:S(2)}) collective-permute-start(bf16[2,12,16,128]{3,2,1,0:T(8,128)(2,1)S(1)} %final_kernel.6.refs_0_.mine_ref), channel_id=1, source_target_pairs={{0,4},{1,5},{2,6},{3,7},{4,0},{5,1},{6,2},{7,3},{8,12},{9,13},{10,... | collective-permute-start | bytes 294920 | tf_op jit(solution)/shard_map/ppermute | solution.py:202
  39.6 1.1 %collective-permute-start.18 = (bf16[2,12,16,128]{3,2,1,0:T(8,128)(2,1)S(1)}, bf16[2,12,16,128]{3,2,1,0:T(8,128)(2,1)S(1)}, u32[]{:S(2)}, u32[]{:S(2)}) collective-permute-start(bf16[2,12,16,128]{3,2,1,0:T(8,128)(2,1)S(1)} %final_kernel.5.refs_0_.mine_ref), channel_id=1, source_target_pairs={{0,4},{1,17},{2,6},{3,19},{4,0},{5,21},{6,2},{7,23},{8,12},{9,25},... | collective-permute-start | bytes 294920 | tf_op jit(solution)/shard_map/ppermute | solution.py:202
  40.8 1.6 %collective-permute-start.20 = (bf16[2,12,16,128]{3,2,1,0:T(8,128)(2,1)S(1)}, bf16[2,12,16,128]{3,2,1,0:T(8,128)(2,1)S(1)}, u32[]{:S(2)}, u32[]{:S(2)}) collective-permute-start(bf16[2,12,16,128]{3,2,1,0:T(8,128)(2,1)S(1)} %final_kernel.7.refs_0_.mine_ref), channel_id=1, source_target_pairs={{0,16},{1,5},{2,18},{3,7},{4,20},{5,1},{6,22},{7,3},{8,24},{9,13},... | collective-permute-start | bytes 294920 | tf_op jit(solution)/shard_map/ppermute | solution.py:202
  42.4 1.8 %collective-permute-start.22 = (bf16[2,2,12,16,128]{4,3,2,1,0:T(8,128)(2,1)S(1)}, bf16[2,2,12,16,128]{4,3,2,1,0:T(8,128)(2,1)S(1)}, u32[]{:S(2)}, u32[]{:S(2)}) collective-permute-start(bf16[2,2,12,16,128]{4,3,2,1,0:T(8,128)(2,1)S(1)} %merge_kernel.4.refs_0_), channel_id=1, source_target_pairs={{0,4},{1,5},{2,6},{3,7},{4,0},{5,1},{6,2},{7,3},{8,12},{9,13},{10,... | collective-permute-start | bytes 589832 | tf_op jit(solution)/shard_map/ppermute | solution.py:202
  44.4 2.4 %collective-permute-start.17 = (bf16[2,2,12,16,128]{4,3,2,1,0:T(8,128)(2,1)S(1)}, bf16[2,2,12,16,128]{4,3,2,1,0:T(8,128)(2,1)S(1)}, u32[]{:S(2)}, u32[]{:S(2)}) collective-permute-start(bf16[2,2,12,16,128]{4,3,2,1,0:T(8,128)(2,1)S(1)} %merge_kernel.5.refs_0_.refs_2_), channel_id=1, source_target_pairs={{0,8},{1,9},{2,10},{3,11},{4,12},{5,13},{6,14},{7,15},{8,0},{9,1},... | collective-permute-start | bytes 589832 | tf_op jit(solution)/shard_map/ppermute | solution.py:202
  46.9 1.5 %collective-permute-start.19 = (bf16[2,2,12,16,128]{4,3,2,1,0:T(8,128)(2,1)S(1)}, bf16[2,2,12,16,128]{4,3,2,1,0:T(8,128)(2,1)S(1)}, u32[]{:S(2)}, u32[]{:S(2)}) collective-permute-start(bf16[2,2,12,16,128]{4,3,2,1,0:T(8,128)(2,1)S(1)} %merge_kernel.6.refs_0_.refs_1_), channel_id=1, source_target_pairs={{0,16},{1,5},{2,18},{3,7},{4,20},{5,1},{6,22},{7,3},{8,24},{9,13},... | collective-permute-start | bytes 589832 | tf_op jit(solution)/shard_map/ppermute | solution.py:202
  48.4 2.1 %collective-permute-start.21 = (bf16[2,2,12,16,128]{4,3,2,1,0:T(8,128)(2,1)S(1)}, bf16[2,2,12,16,128]{4,3,2,1,0:T(8,128)(2,1)S(1)}, u32[]{:S(2)}, u32[]{:S(2)}) collective-permute-start(bf16[2,2,12,16,128]{4,3,2,1,0:T(8,128)(2,1)S(1)} %merge_kernel.7.refs_3_), channel_id=1, source_target_pairs={{0,4},{1,9},{2,6},{3,11},{4,0},{5,13},{6,2},{7,15},{8,12},{9,1},{1... | collective-permute-start | bytes 589832 | tf_op jit(solution)/shard_map/ppermute | solution.py:202
  50.5 1.1 %place_part.2.refs_3_ = bf16[4,24,64,128]{3,2,1,0:T(8,128)(2,1)} custom-call(bf16[2,2,12,16,128]{4,3,2,1,0:T(8,128)(2,1)S(1)} %merge_kernel.4.refs_0_, bf16[2,2,12,16,128]{4,3,2,1,0:T(8,128)(2,1)S(1)} %merge_kernel.6.refs_0_.refs_1_, bf16[2,2,12,16,128]{4,3,2,1,0:T(8,128)(2,1)S(1)} %merge_kernel.5.refs_0_.refs_2_, ...), custom_call_target="tpu_custom_call" | custom-call | tf_op jit(solution)/shard_map/place_part/pallas_call | solution.py:280
  51.6 4.0 %collective-permute-done.19.refs_1_ = bf16[2,2,12,16,128]{4,3,2,1,0:T(8,128)(2,1)S(1)} collective-permute-done((bf16[2,2,12,16,128]{4,3,2,1,0:T(8,128)(2,1)S(1)}, bf16[2,2,12,16,128]{4,3,2,1,0:T(8,128)(2,1)S(1)}, u32[]{:S(2)}, u32[]{:S(2)}) %collective-permute-start.19) | collective-permute-done | bytes 196640 | tf_op jit(solution)/shard_map/ppermute | solution.py:202
  55.6 0.9 %place_part.3 = bf16[4,24,64,128]{3,2,1,0:T(8,128)(2,1)} custom-call(bf16[2,2,12,16,128]{4,3,2,1,0:T(8,128)(2,1)S(1)} %collective-permute-done.17.refs_0_, bf16[2,2,12,16,128]{4,3,2,1,0:T(8,128)(2,1)S(1)} %collective-permute-done.19.refs_1_, bf16[2,2,12,16,128]{4,3,2,1,0:T(8,128)(2,1)S(1)} %collective-permute-done.21.refs_2_, ...), custom_call_target="tpu_custom_call", output_to_operand_aliasing={{}: (3, {})} | custom-call | tf_op jit(solution)/shard_map/place_part/pallas_call | solution.py:280
  (52 shorter events, 6.8 us)
Async XLA Ops:
  0.9 6.1 %collective-permute-start.1 = (bf16[2,4,4,16,128]{4,3,2,1,0:T(8,128)(2,1)S(1)}, bf16[2,4,4,16,128]{4,3,2,1,0:T(8,128)(2,1)S(1)}, u32[]{:S(2)}, u32[]{:S(2)}) collective-permute-start(bf16[2,4,4,16,128]{4,3,2,1,0:T(8,128)(2,1)S(1)} %pad_maximum_fusion.refs_0_), channel_id=1, source_target_pairs={{0,1},{1,0},{2,3},{3,2},{4,5},{5,4},{6,7},{7,6},{8,9},{9,8},{10,11... | collective-permute-start | bytes 393224 | tf_op jit(solution)/shard_map/ppermute | solution.py:205
  1.4 7.0 %collective-permute-start = (bf16[2,4,4,16,128]{4,3,2,1,0:T(8,128)(2,1)S(1)}, bf16[2,4,4,16,128]{4,3,2,1,0:T(8,128)(2,1)S(1)}, u32[]{:S(2)}, u32[]{:S(2)}) collective-permute-start(bf16[2,4,4,16,128]{4,3,2,1,0:T(8,128)(2,1)S(1)} %pad_maximum_fusion.refs_0_), channel_id=1, source_target_pairs={{0,2},{1,3},{2,0},{3,1},{4,6},{5,7},{6,4},{7,5},{8,10},{9,11},{10,... | collective-permute-start | bytes 393224 | tf_op jit(solution)/shard_map/ppermute | solution.py:205
  4.7 2.2 %copy-start = (s32[4]{0:T(128)S(1)}, s32[4]{0:T(128)}, u32[]{:S(2)}) copy-start(s32[4]{0:T(128)} %param.10) | copy-start | bytes 52
  8.5 4.7 %collective-permute-start.5 = (bf16[2,4,4,16,128]{4,3,2,1,0:T(8,128)(2,1)S(1)}, bf16[2,4,4,16,128]{4,3,2,1,0:T(8,128)(2,1)S(1)}, u32[]{:S(2)}, u32[]{:S(2)}) collective-permute-start(bf16[2,4,4,16,128]{4,3,2,1,0:T(8,128)(2,1)S(1)} %copy_kernel.1.refs_3_), channel_id=1, source_target_pairs={{0,1},{1,0},{2,3},{3,2},{4,5},{5,4},{6,7},{7,6},{8,9},{9,8},{10,11... | collective-permute-start | bytes 393224 | tf_op jit(solution)/shard_map/ppermute | solution.py:205
  8.7 8.0 %collective-permute-start.4 = (s16[49,16,128]{2,1,0:T(8,128)(2,1)S(1)}, s16[49,16,128]{2,1,0:T(8,128)(2,1)S(1)}, u32[]{:S(2)}, u32[]{:S(2)}) collective-permute-start(s16[49,16,128]{2,1,0:T(8,128)(2,1)S(1)} %get-tuple-element.26), channel_id=1, source_target_pairs={{0,4},{1,9},{2,6},{3,11},{4,0},{5,13},{6,2},{7,15},{8,12},{9,1},{1... | collective-permute-start | bytes 602120 | tf_op jit(solution)/shard_map/ppermute | solution.py:202
  10.2 8.3 %collective-permute-start.3 = (s16[49,16,128]{2,1,0:T(8,128)(2,1)S(1)}, s16[49,16,128]{2,1,0:T(8,128)(2,1)S(1)}, u32[]{:S(2)}, u32[]{:S(2)}) collective-permute-start(s16[49,16,128]{2,1,0:T(8,128)(2,1)S(1)} %get-tuple-element.21.refs_0_), channel_id=1, source_target_pairs={{0,4},{1,17},{2,6},{3,19},{4,0},{5,21},{6,2},{7,23},{8,12},{9,25},... | collective-permute-start | bytes 602120 | tf_op jit(solution)/shard_map/ppermute | solution.py:202
  11.6 9.2 %collective-permute-start.2 = (s16[49,16,128]{2,1,0:T(8,128)(2,1)S(1)}, s16[49,16,128]{2,1,0:T(8,128)(2,1)S(1)}, u32[]{:S(2)}, u32[]{:S(2)}) collective-permute-start(s16[49,16,128]{2,1,0:T(8,128)(2,1)S(1)} %get-tuple-element.23.refs_3_), channel_id=1, source_target_pairs={{0,4},{1,9},{2,6},{3,11},{4,0},{5,13},{6,2},{7,15},{8,12},{9,1},{1... | collective-permute-start | bytes 602120 | tf_op jit(solution)/shard_map/ppermute | solution.py:202
  14.1 12.7 %collective-permute-start.8 = (s16[49,16,128]{2,1,0:T(8,128)(2,1)S(1)}, s16[49,16,128]{2,1,0:T(8,128)(2,1)S(1)}, u32[]{:S(2)}, u32[]{:S(2)}) collective-permute-start(s16[49,16,128]{2,1,0:T(8,128)(2,1)S(1)} %get-tuple-element.27.refs_0_), channel_id=1, source_target_pairs={{0,16},{1,5},{2,18},{3,7},{4,20},{5,1},{6,22},{7,3},{8,24},{9,13},... | collective-permute-start | bytes 602120 | tf_op jit(solution)/shard_map/ppermute | solution.py:202
  16.9 5.7 %collective-permute-start.9 = (s16[25,16,128]{2,1,0:T(8,128)(2,1)S(1)}, s16[25,16,128]{2,1,0:T(8,128)(2,1)S(1)}, u32[]{:S(2)}, u32[]{:S(2)}) collective-permute-start(s16[25,16,128]{2,1,0:T(8,128)(2,1)S(1)} %get-tuple-element.28.refs_0_), channel_id=1, source_target_pairs={{0,8},{1,5},{2,10},{3,7},{4,12},{5,1},{6,14},{7,3},{8,0},{9,13},{1... | collective-permute-start | bytes 307208 | tf_op jit(solution)/shard_map/ppermute | solution.py:202
  18.6 9.9 %collective-permute-start.7 = (s16[25,16,128]{2,1,0:T(8,128)(2,1)S(1)}, s16[25,16,128]{2,1,0:T(8,128)(2,1)S(1)}, u32[]{:S(2)}, u32[]{:S(2)}) collective-permute-start(s16[25,16,128]{2,1,0:T(8,128)(2,1)S(1)} %get-tuple-element.29.refs_0_), channel_id=1, source_target_pairs={{0,16},{1,5},{2,18},{3,7},{4,20},{5,1},{6,22},{7,3},{8,24},{9,13},... | collective-permute-start | bytes 307208 | tf_op jit(solution)/shard_map/ppermute | solution.py:202
  20.9 8.2 %collective-permute-start.6 = (s16[25,16,128]{2,1,0:T(8,128)(2,1)S(1)}, s16[25,16,128]{2,1,0:T(8,128)(2,1)S(1)}, u32[]{:S(2)}, u32[]{:S(2)}) collective-permute-start(s16[25,16,128]{2,1,0:T(8,128)(2,1)S(1)} %get-tuple-element.31.refs_0_), channel_id=1, source_target_pairs={{0,8},{1,5},{2,10},{3,7},{4,12},{5,1},{6,14},{7,3},{8,0},{9,13},{1... | collective-permute-start | bytes 307208 | tf_op jit(solution)/shard_map/ppermute | solution.py:202
  22.6 9.8 %collective-permute-start.13 = (s16[25,16,128]{2,1,0:T(8,128)(2,1)S(1)}, s16[25,16,128]{2,1,0:T(8,128)(2,1)S(1)}, u32[]{:S(2)}, u32[]{:S(2)}) collective-permute-start(s16[25,16,128]{2,1,0:T(8,128)(2,1)S(1)} %cross_kernel.4.refs_0_.mine_ref), channel_id=1, source_target_pairs={{0,16},{1,17},{2,18},{3,19},{4,20},{5,21},{6,22},{7,23},{8,24},{9,... | collective-permute-start | bytes 307208 | tf_op jit(solution)/shard_map/ppermute | solution.py:202
  26.9 5.6 %collective-permute-start.12 = (s16[25,16,128]{2,1,0:T(8,128)(2,1)S(1)}, s16[25,16,128]{2,1,0:T(8,128)(2,1)S(1)}, u32[]{:S(2)}, u32[]{:S(2)}) collective-permute-start(s16[25,16,128]{2,1,0:T(8,128)(2,1)S(1)} %get-tuple-element.35.refs_0_), channel_id=1, source_target_pairs={{0,4},{1,9},{2,6},{3,11},{4,0},{5,13},{6,2},{7,15},{8,12},{9,1},{1... | collective-permute-start | bytes 307208 | tf_op jit(solution)/shard_map/ppermute | solution.py:202
  28.6 6.7 %collective-permute-start.11 = (s16[25,16,128]{2,1,0:T(8,128)(2,1)S(1)}, s16[25,16,128]{2,1,0:T(8,128)(2,1)S(1)}, u32[]{:S(2)}, u32[]{:S(2)}) collective-permute-start(s16[25,16,128]{2,1,0:T(8,128)(2,1)S(1)} %cross_kernel.5.refs_0_.mine_ref), channel_id=1, source_target_pairs={{0,8},{1,9},{2,10},{3,11},{4,12},{5,13},{6,14},{7,15},{8,0},{9,1},... | collective-permute-start | bytes 307208 | tf_op jit(solution)/shard_map/ppermute | solution.py:202
  29.2 9.4 %collective-permute-start.10 = (s16[25,16,128]{2,1,0:T(8,128)(2,1)S(1)}, s16[25,16,128]{2,1,0:T(8,128)(2,1)S(1)}, u32[]{:S(2)}, u32[]{:S(2)}) collective-permute-start(s16[25,16,128]{2,1,0:T(8,128)(2,1)S(1)} %cross_kernel.6.refs_0_.mine_ref), channel_id=1, source_target_pairs={{0,16},{1,17},{2,18},{3,19},{4,20},{5,21},{6,22},{7,23},{8,24},{9,... | collective-permute-start | bytes 307208 | tf_op jit(solution)/shard_map/ppermute | solution.py:202
  32.6 8.1 %collective-permute-start.15 = (s16[25,16,128]{2,1,0:T(8,128)(2,1)S(1)}, s16[25,16,128]{2,1,0:T(8,128)(2,1)S(1)}, u32[]{:S(2)}, u32[]{:S(2)}) collective-permute-start(s16[25,16,128]{2,1,0:T(8,128)(2,1)S(1)} %cross_kernel.7.refs_0_.mine_ref), channel_id=1, source_target_pairs={{0,8},{1,17},{2,10},{3,19},{4,12},{5,21},{6,14},{7,23},{8,0},{9,25... | collective-permute-start | bytes 307208 | tf_op jit(solution)/shard_map/ppermute | solution.py:202
  35.2 5.5 %collective-permute-start.16 = (bf16[2,12,16,128]{3,2,1,0:T(8,128)(2,1)S(1)}, bf16[2,12,16,128]{3,2,1,0:T(8,128)(2,1)S(1)}, u32[]{:S(2)}, u32[]{:S(2)}) collective-permute-start(bf16[2,12,16,128]{3,2,1,0:T(8,128)(2,1)S(1)} %final_kernel.4.refs_0_.mine_ref), channel_id=1, source_target_pairs={{0,8},{1,9},{2,10},{3,11},{4,12},{5,13},{6,14},{7,15},{8,0},{9,1},... | collective-permute-start | bytes 294920 | tf_op jit(solution)/shard_map/ppermute | solution.py:202
  38.6 5.8 %collective-permute-start.14 = (bf16[2,12,16,128]{3,2,1,0:T(8,128)(2,1)S(1)}, bf16[2,12,16,128]{3,2,1,0:T(8,128)(2,1)S(1)}, u32[]{:S(2)}, u32[]{:S(2)}) collective-permute-start(bf16[2,12,16,128]{3,2,1,0:T(8,128)(2,1)S(1)} %final_kernel.6.refs_0_.mine_ref), channel_id=1, source_target_pairs={{0,4},{1,5},{2,6},{3,7},{4,0},{5,1},{6,2},{7,3},{8,12},{9,13},{10,... | collective-permute-start | bytes 294920 | tf_op jit(solution)/shard_map/ppermute | solution.py:202
  39.6 7.3 %collective-permute-start.18 = (bf16[2,12,16,128]{3,2,1,0:T(8,128)(2,1)S(1)}, bf16[2,12,16,128]{3,2,1,0:T(8,128)(2,1)S(1)}, u32[]{:S(2)}, u32[]{:S(2)}) collective-permute-start(bf16[2,12,16,128]{3,2,1,0:T(8,128)(2,1)S(1)} %final_kernel.5.refs_0_.mine_ref), channel_id=1, source_target_pairs={{0,4},{1,17},{2,6},{3,19},{4,0},{5,21},{6,2},{7,23},{8,12},{9,25},... | collective-permute-start | bytes 294920 | tf_op jit(solution)/shard_map/ppermute | solution.py:202
  40.8 7.6 %collective-permute-start.20 = (bf16[2,12,16,128]{3,2,1,0:T(8,128)(2,1)S(1)}, bf16[2,12,16,128]{3,2,1,0:T(8,128)(2,1)S(1)}, u32[]{:S(2)}, u32[]{:S(2)}) collective-permute-start(bf16[2,12,16,128]{3,2,1,0:T(8,128)(2,1)S(1)} %final_kernel.7.refs_0_.mine_ref), channel_id=1, source_target_pairs={{0,16},{1,5},{2,18},{3,7},{4,20},{5,1},{6,22},{7,3},{8,24},{9,13},... | collective-permute-start | bytes 294920 | tf_op jit(solution)/shard_map/ppermute | solution.py:202
  42.4 8.1 %collective-permute-start.22 = (bf16[2,2,12,16,128]{4,3,2,1,0:T(8,128)(2,1)S(1)}, bf16[2,2,12,16,128]{4,3,2,1,0:T(8,128)(2,1)S(1)}, u32[]{:S(2)}, u32[]{:S(2)}) collective-permute-start(bf16[2,2,12,16,128]{4,3,2,1,0:T(8,128)(2,1)S(1)} %merge_kernel.4.refs_0_), channel_id=1, source_target_pairs={{0,4},{1,5},{2,6},{3,7},{4,0},{5,1},{6,2},{7,3},{8,12},{9,13},{10,... | collective-permute-start | bytes 589832 | tf_op jit(solution)/shard_map/ppermute | solution.py:202
  44.4 11.2 %collective-permute-start.17 = (bf16[2,2,12,16,128]{4,3,2,1,0:T(8,128)(2,1)S(1)}, bf16[2,2,12,16,128]{4,3,2,1,0:T(8,128)(2,1)S(1)}, u32[]{:S(2)}, u32[]{:S(2)}) collective-permute-start(bf16[2,2,12,16,128]{4,3,2,1,0:T(8,128)(2,1)S(1)} %merge_kernel.5.refs_0_.refs_2_), channel_id=1, source_target_pairs={{0,8},{1,9},{2,10},{3,11},{4,12},{5,13},{6,14},{7,15},{8,0},{9,1},... | collective-permute-start | bytes 589832 | tf_op jit(solution)/shard_map/ppermute | solution.py:202
  46.9 8.7 %collective-permute-start.19 = (bf16[2,2,12,16,128]{4,3,2,1,0:T(8,128)(2,1)S(1)}, bf16[2,2,12,16,128]{4,3,2,1,0:T(8,128)(2,1)S(1)}, u32[]{:S(2)}, u32[]{:S(2)}) collective-permute-start(bf16[2,2,12,16,128]{4,3,2,1,0:T(8,128)(2,1)S(1)} %merge_kernel.6.refs_0_.refs_1_), channel_id=1, source_target_pairs={{0,16},{1,5},{2,18},{3,7},{4,20},{5,1},{6,22},{7,3},{8,24},{9,13},... | collective-permute-start | bytes 589832 | tf_op jit(solution)/shard_map/ppermute | solution.py:202
  48.4 7.2 %collective-permute-start.21 = (bf16[2,2,12,16,128]{4,3,2,1,0:T(8,128)(2,1)S(1)}, bf16[2,2,12,16,128]{4,3,2,1,0:T(8,128)(2,1)S(1)}, u32[]{:S(2)}, u32[]{:S(2)}) collective-permute-start(bf16[2,2,12,16,128]{4,3,2,1,0:T(8,128)(2,1)S(1)} %merge_kernel.7.refs_3_), channel_id=1, source_target_pairs={{0,4},{1,9},{2,6},{3,11},{4,0},{5,13},{6,2},{7,15},{8,12},{9,1},{1... | collective-permute-start | bytes 589832 | tf_op jit(solution)/shard_map/ppermute | solution.py:202

commit v4 on v3

--- a/solution.py
+++ b/solution.py
@@ -8,7 +8,7 @@
 from jax.sharding import PartitionSpec as P
 
 BITS = {"y": 0, "z0": 1, "z1": 2}
-ORDERS = ((("y", "z0", "z1", "z0", "y"), ("z0", "y", "z1", "z0", "y")), (("y", "z1", "z0", "y", "z1"), ("z1", "y", "z0", "z1", "y")), (("y", "z0", "z1", "y", "z0"), ("z0", "y", "z1", "y", "z0")), (("z1", "y", "z0", "z1", "y"), ("y", "z0", "z1", "y", "z0")))
+ORDERS = ((("y", "z0", "z1", "z0", "y"), ("z0", "y", "z1", "z0", "y")), (("y", "z1", "z0", "z1", "y"), ("z1", "y", "z0", "y", "z1")), (("y", "z0", "z1", "y", "z0"), ("z0", "y", "z1", "y", "z0")), (("z1", "y", "z0", "z1", "y"), ("y", "z0", "z1", "y", "z0")))
 STEPS = (0, 1, 2, 0, 3, 1, 2, 0, 3, 1, 2, 0, 3, 2, 1, 3)
 PLACES = (((0, 0), (1, 0), (2, 0), (3, 0), (0, 1)), ((2, 1), (1, 1), (3, 1)))
 GROUP = 3

time: 56.7 us -> 58 us (1.023)
  waiting for transfers between devices: 7.47 us -> 11.5 us
  starting transfers between devices: 38.7 us -> 35.9 us
    ppermute x20, waiting for transfers between devices: 7.47 us -> 11.5 us  [swap(): return lax.ppermute(v, ('hist', 'col'), pairs)]
    ppermute x20, starting transfers between devices: 35.4 us -> 32.6 us  [swap(): return lax.ppermute(v, ('hist', 'col'), pairs)]
  transfers between devices with their start and end apart: 23 -> 23, of which waited for: 3 -> 6; matrix products, arithmetic and copies ran while one was open for 5% -> 5% of each run, Pallas kernels for 9% -> 9%
where the time goes in v4:
time: 58 us; the launch traced here: 57.8 us
  starting transfers between devices  35.9 us (62%)
  waiting for transfers between devices  11.5 us (20%)
  Pallas kernels  6.22 us (11%)
  other arithmetic  3.86 us (7%)
    ppermute x20, starting transfers between devices, swap(): return lax.ppermute(v, ('hist', 'col'), pairs)  32.6 us
    ppermute x20, waiting for transfers between devices, swap(): return lax.ppermute(v, ('hist', 'col'), pairs)  11.5 us
    pallas_call x20, Pallas kernels, call(): pl.pallas_call(kernel, out_shape=out_shape, in_specs=[vmem] * len(args),...  4.23 us
    ppermute x3, starting transfers between devices, swap_col(): return lax.ppermute(v, 'col', [(i, i ^ k) for i in range(n_col)])  3.31 us
    select_n x1, other arithmetic, staged(): jnp.where(after, green, zero)  2.17 us
    pallas_call x2, Pallas kernels, put(): pl.pallas_call(functools.partial(place_kernel, [(k, ORDERS[k], last) for...  2 us
  transfers between devices with their start and end apart: 23, of which 6 were waited for; matrix products, arithmetic and copies ran while one was open for 5% of the time, Pallas kernels for 9%

profile of v4, /device:TPU:0, one launch (start us, length us, event | category | flops | bytes accessed | tf_op | source)
XLA Modules:
  0.0 57.8 jit_solution(13717841486216064053)
XLA Ops:
  1.4 2.6 %collective-permute-start = (bf16[2,4,4,16,128]{4,3,2,1,0:T(8,128)(2,1)S(1)}, bf16[2,4,4,16,128]{4,3,2,1,0:T(8,128)(2,1)S(1)}, u32[]{:S(2)}, u32[]{:S(2)}) collective-permute-start(bf16[2,4,4,16,128]{4,3,2,1,0:T(8,128)(2,1)S(1)} %pad_maximum_fusion.refs_0_), channel_id=1, source_target_pairs={{0,2},{1,3},{2,0},{3,1},{4,6},{5,7},{6,4},{7,5},{8,10},{9,11},{10,... | collective-permute-start | bytes 393224 | tf_op jit(solution)/shard_map/ppermute | solution.py:205
  4.7 2.2 %broadcast_select_fusion = (bf16[4,24,64,128]{3,2,1,0:T(8,128)(2,1)S(1)}, bf16[4,24,64,128]{3,2,1,0:T(8,128)(2,1)S(1)}) fusion(bf16[4,24,64,128]{3,2,1,0:T(8,128)(2,1)} %param.9, pred[4,24]{1,0:T(4,128)(4,1)S(1)} %broadcast_compare_fusion, bf16[4,24,64,128]{3,2,1,0:T(8,128)(2,1)} %param.8), kind=kLoop, calls=%fused_computation | loop fusion | flops 1572864 | bytes 6291552 | tf_op jit(solution)/shard_map/jit(_where)/select_n | solution.py:219
  7.1 1.4 %part_kernel.3 = (f32[1,2,2,12,16,128]{5,4,3,2,1,0:T(8,128)S(1)}, s16[49,16,128]{2,1,0:T(8,128)(2,1)S(1)}, f32[1,2,2,12,16,128]{5,4,3,2,1,0:T(8,128)S(1)}, s16[49,16,128]{2,1,0:T(8,128)(2,1)S(1)}) custom-call(bf16[4,4,16,128]{3,2,1,0:T(8,128)(2,1)S(1)} %broadcast_in_dim.27.keep_ref, bf16[2,4,4,16,128]{4,3,2,1,0:T(8,128)(2,1)S(1)} %pad_maximum_fusion.refs_0_, ...), custom_call_target="tpu_custom_call" | custom-call | flops 805306368 | bytes 3145728 | tf_op jit(solution)/shard_map/part_kernel/pallas_call | solution.py:226
  8.7 1.5 %collective-permute-start.4 = (s16[49,16,128]{2,1,0:T(8,128)(2,1)S(1)}, s16[49,16,128]{2,1,0:T(8,128)(2,1)S(1)}, u32[]{:S(2)}, u32[]{:S(2)}) collective-permute-start(s16[49,16,128]{2,1,0:T(8,128)(2,1)S(1)} %get-tuple-element.26), channel_id=1, source_target_pairs={{0,4},{1,9},{2,6},{3,11},{4,0},{5,13},{6,2},{7,15},{8,12},{9,1},{1... | collective-permute-start | bytes 602120 | tf_op jit(solution)/shard_map/ppermute | solution.py:202
  11.6 1.6 %collective-permute-start.2 = (s16[49,16,128]{2,1,0:T(8,128)(2,1)S(1)}, s16[49,16,128]{2,1,0:T(8,128)(2,1)S(1)}, u32[]{:S(2)}, u32[]{:S(2)}) collective-permute-start(s16[49,16,128]{2,1,0:T(8,128)(2,1)S(1)} %get-tuple-element.23.refs_3_), channel_id=1, source_target_pairs={{0,4},{1,9},{2,6},{3,11},{4,0},{5,13},{6,2},{7,15},{8,12},{9,1},{1... | collective-permute-start | bytes 602120 | tf_op jit(solution)/shard_map/ppermute | solution.py:202
  14.1 2.6 %collective-permute-start.8 = (s16[49,16,128]{2,1,0:T(8,128)(2,1)S(1)}, s16[49,16,128]{2,1,0:T(8,128)(2,1)S(1)}, u32[]{:S(2)}, u32[]{:S(2)}) collective-permute-start(s16[49,16,128]{2,1,0:T(8,128)(2,1)S(1)} %get-tuple-element.27.refs_0_), channel_id=1, source_target_pairs={{0,16},{1,5},{2,18},{3,7},{4,20},{5,1},{6,22},{7,3},{8,24},{9,13},... | collective-permute-start | bytes 602120 | tf_op jit(solution)/shard_map/ppermute | solution.py:202
  16.9 1.7 %collective-permute-start.9 = (s16[25,16,128]{2,1,0:T(8,128)(2,1)S(1)}, s16[25,16,128]{2,1,0:T(8,128)(2,1)S(1)}, u32[]{:S(2)}, u32[]{:S(2)}) collective-permute-start(s16[25,16,128]{2,1,0:T(8,128)(2,1)S(1)} %get-tuple-element.28.refs_0_), channel_id=1, source_target_pairs={{0,8},{1,5},{2,10},{3,7},{4,12},{5,1},{6,14},{7,3},{8,0},{9,13},{1... | collective-permute-start | bytes 307208 | tf_op jit(solution)/shard_map/ppermute | solution.py:202
  18.6 2.1 %collective-permute-start.7 = (s16[25,16,128]{2,1,0:T(8,128)(2,1)S(1)}, s16[25,16,128]{2,1,0:T(8,128)(2,1)S(1)}, u32[]{:S(2)}, u32[]{:S(2)}) collective-permute-start(s16[25,16,128]{2,1,0:T(8,128)(2,1)S(1)} %get-tuple-element.29.refs_0_), channel_id=1, source_target_pairs={{0,16},{1,5},{2,18},{3,7},{4,20},{5,1},{6,22},{7,3},{8,24},{9,13},... | collective-permute-start | bytes 307208 | tf_op jit(solution)/shard_map/ppermute | solution.py:202
  20.9 1.6 %collective-permute-start.6 = (s16[25,16,128]{2,1,0:T(8,128)(2,1)S(1)}, s16[25,16,128]{2,1,0:T(8,128)(2,1)S(1)}, u32[]{:S(2)}, u32[]{:S(2)}) collective-permute-start(s16[25,16,128]{2,1,0:T(8,128)(2,1)S(1)} %get-tuple-element.31.refs_0_), channel_id=1, source_target_pairs={{0,8},{1,5},{2,10},{3,7},{4,12},{5,1},{6,14},{7,3},{8,0},{9,13},{1... | collective-permute-start | bytes 307208 | tf_op jit(solution)/shard_map/ppermute | solution.py:202
  22.6 4.2 %collective-permute-start.13 = (s16[25,16,128]{2,1,0:T(8,128)(2,1)S(1)}, s16[25,16,128]{2,1,0:T(8,128)(2,1)S(1)}, u32[]{:S(2)}, u32[]{:S(2)}) collective-permute-start(s16[25,16,128]{2,1,0:T(8,128)(2,1)S(1)} %cross_kernel.4.refs_0_.mine_ref), channel_id=1, source_target_pairs={{0,16},{1,17},{2,18},{3,19},{4,20},{5,21},{6,22},{7,23},{8,24},{9,... | collective-permute-start | bytes 307208 | tf_op jit(solution)/shard_map/ppermute | solution.py:202
  26.9 1.6 %collective-permute-start.12 = (s16[25,16,128]{2,1,0:T(8,128)(2,1)S(1)}, s16[25,16,128]{2,1,0:T(8,128)(2,1)S(1)}, u32[]{:S(2)}, u32[]{:S(2)}) collective-permute-start(s16[25,16,128]{2,1,0:T(8,128)(2,1)S(1)} %get-tuple-element.35.refs_0_), channel_id=1, source_target_pairs={{0,4},{1,9},{2,6},{3,11},{4,0},{5,13},{6,2},{7,15},{8,12},{9,1},{1... | collective-permute-start | bytes 307208 | tf_op jit(solution)/shard_map/ppermute | solution.py:202
  29.2 3.3 %collective-permute-start.10 = (s16[25,16,128]{2,1,0:T(8,128)(2,1)S(1)}, s16[25,16,128]{2,1,0:T(8,128)(2,1)S(1)}, u32[]{:S(2)}, u32[]{:S(2)}) collective-permute-start(s16[25,16,128]{2,1,0:T(8,128)(2,1)S(1)} %cross_kernel.6.refs_0_.mine_ref), channel_id=1, source_target_pairs={{0,16},{1,17},{2,18},{3,19},{4,20},{5,21},{6,22},{7,23},{8,24},{9,... | collective-permute-start | bytes 307208 | tf_op jit(solution)/shard_map/ppermute | solution.py:202
  32.6 2.5 %collective-permute-start.15 = (s16[25,16,128]{2,1,0:T(8,128)(2,1)S(1)}, s16[25,16,128]{2,1,0:T(8,128)(2,1)S(1)}, u32[]{:S(2)}, u32[]{:S(2)}) collective-permute-start(s16[25,16,128]{2,1,0:T(8,128)(2,1)S(1)} %cross_kernel.7.refs_0_.mine_ref), channel_id=1, source_target_pairs={{0,8},{1,17},{2,10},{3,19},{4,12},{5,21},{6,14},{7,23},{8,0},{9,25... | collective-permute-start | bytes 307208 | tf_op jit(solution)/shard_map/ppermute | solution.py:202
  35.3 2.9 %collective-permute-done.10.other_ref = s16[25,16,128]{2,1,0:T(8,128)(2,1)S(1)} collective-permute-done((s16[25,16,128]{2,1,0:T(8,128)(2,1)S(1)}, s16[25,16,128]{2,1,0:T(8,128)(2,1)S(1)}, u32[]{:S(2)}, u32[]{:S(2)}) %collective-permute-start.10) | collective-permute-done | bytes 102432 | tf_op jit(solution)/shard_map/ppermute | solution.py:202
  38.4 1.6 %collective-permute-start.18 = (bf16[2,12,16,128]{3,2,1,0:T(8,128)(2,1)S(1)}, bf16[2,12,16,128]{3,2,1,0:T(8,128)(2,1)S(1)}, u32[]{:S(2)}, u32[]{:S(2)}) collective-permute-start(bf16[2,12,16,128]{3,2,1,0:T(8,128)(2,1)S(1)} %final_kernel.5.refs_0_.mine_ref), channel_id=1, source_target_pairs={{0,16},{1,5},{2,18},{3,7},{4,20},{5,1},{6,22},{7,3},{8,24},{9,13},... | collective-permute-start | bytes 294920 | tf_op jit(solution)/shard_map/ppermute | solution.py:202
  40.0 1.5 %collective-permute-start.20 = (bf16[2,12,16,128]{3,2,1,0:T(8,128)(2,1)S(1)}, bf16[2,12,16,128]{3,2,1,0:T(8,128)(2,1)S(1)}, u32[]{:S(2)}, u32[]{:S(2)}) collective-permute-start(bf16[2,12,16,128]{3,2,1,0:T(8,128)(2,1)S(1)} %final_kernel.7.refs_0_.mine_ref), channel_id=1, source_target_pairs={{0,16},{1,5},{2,18},{3,7},{4,20},{5,1},{6,22},{7,3},{8,24},{9,13},... | collective-permute-start | bytes 294920 | tf_op jit(solution)/shard_map/ppermute | solution.py:202
  41.5 1.9 %collective-permute-start.22 = (bf16[2,2,12,16,128]{4,3,2,1,0:T(8,128)(2,1)S(1)}, bf16[2,2,12,16,128]{4,3,2,1,0:T(8,128)(2,1)S(1)}, u32[]{:S(2)}, u32[]{:S(2)}) collective-permute-start(bf16[2,2,12,16,128]{4,3,2,1,0:T(8,128)(2,1)S(1)} %merge_kernel.4.refs_0_), channel_id=1, source_target_pairs={{0,4},{1,5},{2,6},{3,7},{4,0},{5,1},{6,2},{7,3},{8,12},{9,13},{10,... | collective-permute-start | bytes 589832 | tf_op jit(solution)/shard_map/ppermute | solution.py:202
  44.7 4.3 %collective-permute-done.18.other_ref = bf16[2,12,16,128]{3,2,1,0:T(8,128)(2,1)S(1)} collective-permute-done((bf16[2,12,16,128]{3,2,1,0:T(8,128)(2,1)S(1)}, bf16[2,12,16,128]{3,2,1,0:T(8,128)(2,1)S(1)}, u32[]{:S(2)}, u32[]{:S(2)}) %collective-permute-start.18) | collective-permute-done | bytes 98336 | tf_op jit(solution)/shard_map/ppermute | solution.py:202
  49.0 2.0 %collective-permute-start.19 = (bf16[2,2,12,16,128]{4,3,2,1,0:T(8,128)(2,1)S(1)}, bf16[2,2,12,16,128]{4,3,2,1,0:T(8,128)(2,1)S(1)}, u32[]{:S(2)}, u32[]{:S(2)}) collective-permute-start(bf16[2,2,12,16,128]{4,3,2,1,0:T(8,128)(2,1)S(1)} %merge_kernel.6.refs_0_.refs_1_), channel_id=1, source_target_pairs={{0,4},{1,17},{2,6},{3,19},{4,0},{5,21},{6,2},{7,23},{8,12},{9,25},... | collective-permute-start | bytes 589832 | tf_op jit(solution)/shard_map/ppermute | solution.py:202
  51.1 1.0 %collective-permute-start.21 = (bf16[2,2,12,16,128]{4,3,2,1,0:T(8,128)(2,1)S(1)}, bf16[2,2,12,16,128]{4,3,2,1,0:T(8,128)(2,1)S(1)}, u32[]{:S(2)}, u32[]{:S(2)}) collective-permute-start(bf16[2,2,12,16,128]{4,3,2,1,0:T(8,128)(2,1)S(1)} %merge_kernel.7.refs_3_), channel_id=1, source_target_pairs={{0,4},{1,9},{2,6},{3,11},{4,0},{5,13},{6,2},{7,15},{8,12},{9,1},{1... | collective-permute-start | bytes 589832 | tf_op jit(solution)/shard_map/ppermute | solution.py:202
  52.1 1.1 %place_part.2.refs_3_ = bf16[4,24,64,128]{3,2,1,0:T(8,128)(2,1)} custom-call(bf16[2,2,12,16,128]{4,3,2,1,0:T(8,128)(2,1)S(1)} %merge_kernel.4.refs_0_, bf16[2,2,12,16,128]{4,3,2,1,0:T(8,128)(2,1)S(1)} %merge_kernel.6.refs_0_.refs_1_, bf16[2,2,12,16,128]{4,3,2,1,0:T(8,128)(2,1)S(1)} %merge_kernel.5.refs_0_.refs_2_, ...), custom_call_target="tpu_custom_call" | custom-call | tf_op jit(solution)/shard_map/place_part/pallas_call | solution.py:280
  53.2 1.5 %collective-permute-done.19.refs_1_ = bf16[2,2,12,16,128]{4,3,2,1,0:T(8,128)(2,1)S(1)} collective-permute-done((bf16[2,2,12,16,128]{4,3,2,1,0:T(8,128)(2,1)S(1)}, bf16[2,2,12,16,128]{4,3,2,1,0:T(8,128)(2,1)S(1)}, u32[]{:S(2)}, u32[]{:S(2)}) %collective-permute-start.19) | collective-permute-done | bytes 196640 | tf_op jit(solution)/shard_map/ppermute | solution.py:202
  54.8 2.1 %collective-permute-done.21.refs_2_ = bf16[2,2,12,16,128]{4,3,2,1,0:T(8,128)(2,1)S(1)} collective-permute-done((bf16[2,2,12,16,128]{4,3,2,1,0:T(8,128)(2,1)S(1)}, bf16[2,2,12,16,128]{4,3,2,1,0:T(8,128)(2,1)S(1)}, u32[]{:S(2)}, u32[]{:S(2)}) %collective-permute-start.21) | collective-permute-done | bytes 196640 | tf_op jit(solution)/shard_map/ppermute | solution.py:202
  56.9 0.9 %place_part.3 = bf16[4,24,64,128]{3,2,1,0:T(8,128)(2,1)} custom-call(bf16[2,2,12,16,128]{4,3,2,1,0:T(8,128)(2,1)S(1)} %collective-permute-done.17.refs_0_, bf16[2,2,12,16,128]{4,3,2,1,0:T(8,128)(2,1)S(1)} %collective-permute-done.19.refs_1_, bf16[2,2,12,16,128]{4,3,2,1,0:T(8,128)(2,1)S(1)} %collective-permute-done.21.refs_2_, ...), custom_call_target="tpu_custom_call", output_to_operand_aliasing={{}: (3, {})} | custom-call | tf_op jit(solution)/shard_map/place_part/pallas_call | solution.py:280
  (52 shorter events, 7.9 us)
Async XLA Ops:
  0.9 6.1 %collective-permute-start.1 = (bf16[2,4,4,16,128]{4,3,2,1,0:T(8,128)(2,1)S(1)}, bf16[2,4,4,16,128]{4,3,2,1,0:T(8,128)(2,1)S(1)}, u32[]{:S(2)}, u32[]{:S(2)}) collective-permute-start(bf16[2,4,4,16,128]{4,3,2,1,0:T(8,128)(2,1)S(1)} %pad_maximum_fusion.refs_0_), channel_id=1, source_target_pairs={{0,1},{1,0},{2,3},{3,2},{4,5},{5,4},{6,7},{7,6},{8,9},{9,8},{10,11... | collective-permute-start | bytes 393224 | tf_op jit(solution)/shard_map/ppermute | solution.py:205
  1.4 7.0 %collective-permute-start = (bf16[2,4,4,16,128]{4,3,2,1,0:T(8,128)(2,1)S(1)}, bf16[2,4,4,16,128]{4,3,2,1,0:T(8,128)(2,1)S(1)}, u32[]{:S(2)}, u32[]{:S(2)}) collective-permute-start(bf16[2,4,4,16,128]{4,3,2,1,0:T(8,128)(2,1)S(1)} %pad_maximum_fusion.refs_0_), channel_id=1, source_target_pairs={{0,2},{1,3},{2,0},{3,1},{4,6},{5,7},{6,4},{7,5},{8,10},{9,11},{10,... | collective-permute-start | bytes 393224 | tf_op jit(solution)/shard_map/ppermute | solution.py:205
  4.7 2.2 %copy-start = (s32[4]{0:T(128)S(1)}, s32[4]{0:T(128)}, u32[]{:S(2)}) copy-start(s32[4]{0:T(128)} %param.10) | copy-start | bytes 52
  8.5 4.7 %collective-permute-start.5 = (bf16[2,4,4,16,128]{4,3,2,1,0:T(8,128)(2,1)S(1)}, bf16[2,4,4,16,128]{4,3,2,1,0:T(8,128)(2,1)S(1)}, u32[]{:S(2)}, u32[]{:S(2)}) collective-permute-start(bf16[2,4,4,16,128]{4,3,2,1,0:T(8,128)(2,1)S(1)} %copy_kernel.1.refs_3_), channel_id=1, source_target_pairs={{0,1},{1,0},{2,3},{3,2},{4,5},{5,4},{6,7},{7,6},{8,9},{9,8},{10,11... | collective-permute-start | bytes 393224 | tf_op jit(solution)/shard_map/ppermute | solution.py:205
  8.7 8.0 %collective-permute-start.4 = (s16[49,16,128]{2,1,0:T(8,128)(2,1)S(1)}, s16[49,16,128]{2,1,0:T(8,128)(2,1)S(1)}, u32[]{:S(2)}, u32[]{:S(2)}) collective-permute-start(s16[49,16,128]{2,1,0:T(8,128)(2,1)S(1)} %get-tuple-element.26), channel_id=1, source_target_pairs={{0,4},{1,9},{2,6},{3,11},{4,0},{5,13},{6,2},{7,15},{8,12},{9,1},{1... | collective-permute-start | bytes 602120 | tf_op jit(solution)/shard_map/ppermute | solution.py:202
  10.2 8.3 %collective-permute-start.3 = (s16[49,16,128]{2,1,0:T(8,128)(2,1)S(1)}, s16[49,16,128]{2,1,0:T(8,128)(2,1)S(1)}, u32[]{:S(2)}, u32[]{:S(2)}) collective-permute-start(s16[49,16,128]{2,1,0:T(8,128)(2,1)S(1)} %get-tuple-element.21.refs_0_), channel_id=1, source_target_pairs={{0,4},{1,17},{2,6},{3,19},{4,0},{5,21},{6,2},{7,23},{8,12},{9,25},... | collective-permute-start | bytes 602120 | tf_op jit(solution)/shard_map/ppermute | solution.py:202
  11.6 9.2 %collective-permute-start.2 = (s16[49,16,128]{2,1,0:T(8,128)(2,1)S(1)}, s16[49,16,128]{2,1,0:T(8,128)(2,1)S(1)}, u32[]{:S(2)}, u32[]{:S(2)}) collective-permute-start(s16[49,16,128]{2,1,0:T(8,128)(2,1)S(1)} %get-tuple-element.23.refs_3_), channel_id=1, source_target_pairs={{0,4},{1,9},{2,6},{3,11},{4,0},{5,13},{6,2},{7,15},{8,12},{9,1},{1... | collective-permute-start | bytes 602120 | tf_op jit(solution)/shard_map/ppermute | solution.py:202
  14.1 12.7 %collective-permute-start.8 = (s16[49,16,128]{2,1,0:T(8,128)(2,1)S(1)}, s16[49,16,128]{2,1,0:T(8,128)(2,1)S(1)}, u32[]{:S(2)}, u32[]{:S(2)}) collective-permute-start(s16[49,16,128]{2,1,0:T(8,128)(2,1)S(1)} %get-tuple-element.27.refs_0_), channel_id=1, source_target_pairs={{0,16},{1,5},{2,18},{3,7},{4,20},{5,1},{6,22},{7,3},{8,24},{9,13},... | collective-permute-start | bytes 602120 | tf_op jit(solution)/shard_map/ppermute | solution.py:202
  16.9 5.7 %collective-permute-start.9 = (s16[25,16,128]{2,1,0:T(8,128)(2,1)S(1)}, s16[25,16,128]{2,1,0:T(8,128)(2,1)S(1)}, u32[]{:S(2)}, u32[]{:S(2)}) collective-permute-start(s16[25,16,128]{2,1,0:T(8,128)(2,1)S(1)} %get-tuple-element.28.refs_0_), channel_id=1, source_target_pairs={{0,8},{1,5},{2,10},{3,7},{4,12},{5,1},{6,14},{7,3},{8,0},{9,13},{1... | collective-permute-start | bytes 307208 | tf_op jit(solution)/shard_map/ppermute | solution.py:202
  18.6 9.9 %collective-permute-start.7 = (s16[25,16,128]{2,1,0:T(8,128)(2,1)S(1)}, s16[25,16,128]{2,1,0:T(8,128)(2,1)S(1)}, u32[]{:S(2)}, u32[]{:S(2)}) collective-permute-start(s16[25,16,128]{2,1,0:T(8,128)(2,1)S(1)} %get-tuple-element.29.refs_0_), channel_id=1, source_target_pairs={{0,16},{1,5},{2,18},{3,7},{4,20},{5,1},{6,22},{7,3},{8,24},{9,13},... | collective-permute-start | bytes 307208 | tf_op jit(solution)/shard_map/ppermute | solution.py:202
  20.9 8.2 %collective-permute-start.6 = (s16[25,16,128]{2,1,0:T(8,128)(2,1)S(1)}, s16[25,16,128]{2,1,0:T(8,128)(2,1)S(1)}, u32[]{:S(2)}, u32[]{:S(2)}) collective-permute-start(s16[25,16,128]{2,1,0:T(8,128)(2,1)S(1)} %get-tuple-element.31.refs_0_), channel_id=1, source_target_pairs={{0,8},{1,5},{2,10},{3,7},{4,12},{5,1},{6,14},{7,3},{8,0},{9,13},{1... | collective-permute-start | bytes 307208 | tf_op jit(solution)/shard_map/ppermute | solution.py:202
  22.6 9.8 %collective-permute-start.13 = (s16[25,16,128]{2,1,0:T(8,128)(2,1)S(1)}, s16[25,16,128]{2,1,0:T(8,128)(2,1)S(1)}, u32[]{:S(2)}, u32[]{:S(2)}) collective-permute-start(s16[25,16,128]{2,1,0:T(8,128)(2,1)S(1)} %cross_kernel.4.refs_0_.mine_ref), channel_id=1, source_target_pairs={{0,16},{1,17},{2,18},{3,19},{4,20},{5,21},{6,22},{7,23},{8,24},{9,... | collective-permute-start | bytes 307208 | tf_op jit(solution)/shard_map/ppermute | solution.py:202
  26.9 5.6 %collective-permute-start.12 = (s16[25,16,128]{2,1,0:T(8,128)(2,1)S(1)}, s16[25,16,128]{2,1,0:T(8,128)(2,1)S(1)}, u32[]{:S(2)}, u32[]{:S(2)}) collective-permute-start(s16[25,16,128]{2,1,0:T(8,128)(2,1)S(1)} %get-tuple-element.35.refs_0_), channel_id=1, source_target_pairs={{0,4},{1,9},{2,6},{3,11},{4,0},{5,13},{6,2},{7,15},{8,12},{9,1},{1... | collective-permute-start | bytes 307208 | tf_op jit(solution)/shard_map/ppermute | solution.py:202
  28.6 6.7 %collective-permute-start.11 = (s16[25,16,128]{2,1,0:T(8,128)(2,1)S(1)}, s16[25,16,128]{2,1,0:T(8,128)(2,1)S(1)}, u32[]{:S(2)}, u32[]{:S(2)}) collective-permute-start(s16[25,16,128]{2,1,0:T(8,128)(2,1)S(1)} %cross_kernel.5.refs_0_.mine_ref), channel_id=1, source_target_pairs={{0,8},{1,9},{2,10},{3,11},{4,12},{5,13},{6,14},{7,15},{8,0},{9,1},... | collective-permute-start | bytes 307208 | tf_op jit(solution)/shard_map/ppermute | solution.py:202
  29.2 9.0 %collective-permute-start.10 = (s16[25,16,128]{2,1,0:T(8,128)(2,1)S(1)}, s16[25,16,128]{2,1,0:T(8,128)(2,1)S(1)}, u32[]{:S(2)}, u32[]{:S(2)}) collective-permute-start(s16[25,16,128]{2,1,0:T(8,128)(2,1)S(1)} %cross_kernel.6.refs_0_.mine_ref), channel_id=1, source_target_pairs={{0,16},{1,17},{2,18},{3,19},{4,20},{5,21},{6,22},{7,23},{8,24},{9,... | collective-permute-start | bytes 307208 | tf_op jit(solution)/shard_map/ppermute | solution.py:202
  32.6 7.3 %collective-permute-start.15 = (s16[25,16,128]{2,1,0:T(8,128)(2,1)S(1)}, s16[25,16,128]{2,1,0:T(8,128)(2,1)S(1)}, u32[]{:S(2)}, u32[]{:S(2)}) collective-permute-start(s16[25,16,128]{2,1,0:T(8,128)(2,1)S(1)} %cross_kernel.7.refs_0_.mine_ref), channel_id=1, source_target_pairs={{0,8},{1,17},{2,10},{3,19},{4,12},{5,21},{6,14},{7,23},{8,0},{9,25... | collective-permute-start | bytes 307208 | tf_op jit(solution)/shard_map/ppermute | solution.py:202
  35.2 4.7 %collective-permute-start.16 = (bf16[2,12,16,128]{3,2,1,0:T(8,128)(2,1)S(1)}, bf16[2,12,16,128]{3,2,1,0:T(8,128)(2,1)S(1)}, u32[]{:S(2)}, u32[]{:S(2)}) collective-permute-start(bf16[2,12,16,128]{3,2,1,0:T(8,128)(2,1)S(1)} %final_kernel.4.refs_0_.mine_ref), channel_id=1, source_target_pairs={{0,8},{1,9},{2,10},{3,11},{4,12},{5,13},{6,14},{7,15},{8,0},{9,1},... | collective-permute-start | bytes 294920 | tf_op jit(solution)/shard_map/ppermute | solution.py:202
  38.3 5.8 %collective-permute-start.14 = (bf16[2,12,16,128]{3,2,1,0:T(8,128)(2,1)S(1)}, bf16[2,12,16,128]{3,2,1,0:T(8,128)(2,1)S(1)}, u32[]{:S(2)}, u32[]{:S(2)}) collective-permute-start(bf16[2,12,16,128]{3,2,1,0:T(8,128)(2,1)S(1)} %final_kernel.6.refs_0_.mine_ref), channel_id=1, source_target_pairs={{0,4},{1,5},{2,6},{3,7},{4,0},{5,1},{6,2},{7,3},{8,12},{9,13},{10,... | collective-permute-start | bytes 294920 | tf_op jit(solution)/shard_map/ppermute | solution.py:202
  38.4 10.7 %collective-permute-start.18 = (bf16[2,12,16,128]{3,2,1,0:T(8,128)(2,1)S(1)}, bf16[2,12,16,128]{3,2,1,0:T(8,128)(2,1)S(1)}, u32[]{:S(2)}, u32[]{:S(2)}) collective-permute-start(bf16[2,12,16,128]{3,2,1,0:T(8,128)(2,1)S(1)} %final_kernel.5.refs_0_.mine_ref), channel_id=1, source_target_pairs={{0,16},{1,5},{2,18},{3,7},{4,20},{5,1},{6,22},{7,3},{8,24},{9,13},... | collective-permute-start | bytes 294920 | tf_op jit(solution)/shard_map/ppermute | solution.py:202
  40.0 11.1 %collective-permute-start.20 = (bf16[2,12,16,128]{3,2,1,0:T(8,128)(2,1)S(1)}, bf16[2,12,16,128]{3,2,1,0:T(8,128)(2,1)S(1)}, u32[]{:S(2)}, u32[]{:S(2)}) collective-permute-start(bf16[2,12,16,128]{3,2,1,0:T(8,128)(2,1)S(1)} %final_kernel.7.refs_0_.mine_ref), channel_id=1, source_target_pairs={{0,16},{1,5},{2,18},{3,7},{4,20},{5,1},{6,22},{7,3},{8,24},{9,13},... | collective-permute-start | bytes 294920 | tf_op jit(solution)/shard_map/ppermute | solution.py:202
  41.5 10.6 %collective-permute-start.22 = (bf16[2,2,12,16,128]{4,3,2,1,0:T(8,128)(2,1)S(1)}, bf16[2,2,12,16,128]{4,3,2,1,0:T(8,128)(2,1)S(1)}, u32[]{:S(2)}, u32[]{:S(2)}) collective-permute-start(bf16[2,2,12,16,128]{4,3,2,1,0:T(8,128)(2,1)S(1)} %merge_kernel.4.refs_0_), channel_id=1, source_target_pairs={{0,4},{1,5},{2,6},{3,7},{4,0},{5,1},{6,2},{7,3},{8,12},{9,13},{10,... | collective-permute-start | bytes 589832 | tf_op jit(solution)/shard_map/ppermute | solution.py:202
  44.1 10.7 %collective-permute-start.17 = (bf16[2,2,12,16,128]{4,3,2,1,0:T(8,128)(2,1)S(1)}, bf16[2,2,12,16,128]{4,3,2,1,0:T(8,128)(2,1)S(1)}, u32[]{:S(2)}, u32[]{:S(2)}) collective-permute-start(bf16[2,2,12,16,128]{4,3,2,1,0:T(8,128)(2,1)S(1)} %merge_kernel.5.refs_0_.refs_2_), channel_id=1, source_target_pairs={{0,8},{1,9},{2,10},{3,11},{4,12},{5,13},{6,14},{7,15},{8,0},{9,1},... | collective-permute-start | bytes 589832 | tf_op jit(solution)/shard_map/ppermute | solution.py:202
  49.0 5.7 %collective-permute-start.19 = (bf16[2,2,12,16,128]{4,3,2,1,0:T(8,128)(2,1)S(1)}, bf16[2,2,12,16,128]{4,3,2,1,0:T(8,128)(2,1)S(1)}, u32[]{:S(2)}, u32[]{:S(2)}) collective-permute-start(bf16[2,2,12,16,128]{4,3,2,1,0:T(8,128)(2,1)S(1)} %merge_kernel.6.refs_0_.refs_1_), channel_id=1, source_target_pairs={{0,4},{1,17},{2,6},{3,19},{4,0},{5,21},{6,2},{7,23},{8,12},{9,25},... | collective-permute-start | bytes 589832 | tf_op jit(solution)/shard_map/ppermute | solution.py:202
  51.1 5.7 %collective-permute-start.21 = (bf16[2,2,12,16,128]{4,3,2,1,0:T(8,128)(2,1)S(1)}, bf16[2,2,12,16,128]{4,3,2,1,0:T(8,128)(2,1)S(1)}, u32[]{:S(2)}, u32[]{:S(2)}) collective-permute-start(bf16[2,2,12,16,128]{4,3,2,1,0:T(8,128)(2,1)S(1)} %merge_kernel.7.refs_3_), channel_id=1, source_target_pairs={{0,4},{1,9},{2,6},{3,11},{4,0},{5,13},{6,2},{7,15},{8,12},{9,1},{1... | collective-permute-start | bytes 589832 | tf_op jit(solution)/shard_map/ppermute | solution.py:202

commit v5 on v2

--- a/solution.py
+++ b/solution.py
@@ -8,8 +8,8 @@
 from jax.sharding import PartitionSpec as P
 
 BITS = {"y": 0, "z0": 1, "z1": 2}
-ORDERS = ((("y", "z0", "z1", "y", "z0"), ("y", "z0", "z1", "y", "z0")), (("z1", "y", "z0", "z1", "y"), ("z1", "y", "z0", "z1", "y")), (("y", "z0", "z1", "z0", "y"), ("y", "z0", "z1", "z0", "y")), (("y", "z0", "z1", "y", "z0"), ("y", "z0", "z1", "y", "z0")))
-STEPS = (0, 2, 0, 1, 3, 2, 1, 0, 3, 2, 1, 0, 3, 2, 1, 3)
+ORDERS = ((("y", "z0", "z1", "z0", "y"), ("z0", "y", "z1", "z0", "y")), (("y", "z1", "z0", "y", "z1"), ("z1", "y", "z0", "z1", "y")), (("y", "z0", "z1", "y", "z0"), ("z0", "y", "z1", "z0", "y")), (("z1", "y", "z0", "z1", "y"), ("y", "z0", "z1", "y", "z0")))
+STEPS = (0, 1, 2, 0, 3, 1, 2, 0, 3, 1, 2, 0, 3, 1, 2, 3)
 PLACES = (((0, 0), (1, 0), (2, 0), (3, 0), (0, 1)), ((1, 1), (2, 1), (3, 1)))
 GROUP = 3
 STEPS_PER_OCTAVE = 128.0

time: 56.6 us -> 54.8 us (0.968)
  waiting for transfers between devices: 17.6 us -> 8.39 us
  starting transfers between devices: 28.4 us -> 35.8 us
    ppermute x20, waiting for transfers between devices: 17.6 us -> 8.38 us  [swap(): return lax.ppermute(v, ('hist', 'col'), pairs)]
    ppermute x20, starting transfers between devices: 24.9 us -> 32.2 us  [swap(): return lax.ppermute(v, ('hist', 'col'), pairs)]
  transfers between devices with their start and end apart: 23 -> 23, of which waited for: 11 -> 6; matrix products, arithmetic and copies ran while one was open for 5% -> 6% of each run, Pallas kernels for 9% -> 10%
where the time goes in v5:
time: 54.8 us; the launch traced here: 54.5 us
  starting transfers between devices  35.8 us (65%)
  waiting for transfers between devices  8.39 us (15%)
  Pallas kernels  6.23 us (11%)
  other arithmetic  3.86 us (7%)
    ppermute x20, starting transfers between devices, swap(): return lax.ppermute(v, ('hist', 'col'), pairs)  32.2 us
    ppermute x20, waiting for transfers between devices, swap(): return lax.ppermute(v, ('hist', 'col'), pairs)  8.38 us
    pallas_call x20, Pallas kernels, call(): pl.pallas_call(kernel, out_shape=out_shape, in_specs=[vmem] * len(args),...  4.23 us
    ppermute x3, starting transfers between devices, swap_col(): return lax.ppermute(v, 'col', [(i, i ^ k) for i in range(n_col)])  3.58 us
    select_n x1, other arithmetic, staged(): jnp.where(after, green, zero)  2.17 us
    pallas_call x2, Pallas kernels, put(): pl.pallas_call(functools.partial(place_kernel, [(k, ORDERS[k], last) for...  2 us
  transfers between devices with their start and end apart: 23, of which 6 were waited for; matrix products, arithmetic and copies ran while one was open for 6% of the time, Pallas kernels for 10%

profile of v5, /device:TPU:0, one launch (start us, length us, event | category | flops | bytes accessed | tf_op | source)
XLA Modules:
  0.0 54.5 jit_solution(7926378284369399763)
XLA Ops:
  0.0 0.9 %pad_maximum_fusion.refs_0_ = bf16[2,4,4,16,128]{4,3,2,1,0:T(8,128)(2,1)S(1)} fusion(bf16[1,4,4,16,128]{4,3,2,1,0:T(8,128)(2,1)} %bitcast.2, bf16[1,4,4,16,128]{4,3,2,1,0:T(8,128)(2,1)} %bitcast.3), kind=kLoop, calls=%fused_computation.2 | loop fusion | flops 65536 | bytes 262144 | tf_op jit(solution)/shard_map/stack | solution.py:213
  0.9 3.0 %collective-permute-start.3 = (bf16[2,4,4,16,128]{4,3,2,1,0:T(8,128)(2,1)S(1)}, bf16[2,4,4,16,128]{4,3,2,1,0:T(8,128)(2,1)S(1)}, u32[]{:S(2)}, u32[]{:S(2)}) collective-permute-start(bf16[2,4,4,16,128]{4,3,2,1,0:T(8,128)(2,1)S(1)} %pad_maximum_fusion.refs_0_), channel_id=1, source_target_pairs={{0,2},{1,3},{2,0},{3,1},{4,6},{5,7},{6,4},{7,5},{8,10},{9,11},{10,... | collective-permute-start | bytes 393224 | tf_op jit(solution)/shard_map/ppermute | solution.py:205
  4.6 2.2 %broadcast_select_fusion = (bf16[4,24,64,128]{3,2,1,0:T(8,128)(2,1)S(1)}, bf16[4,24,64,128]{3,2,1,0:T(8,128)(2,1)S(1)}) fusion(bf16[4,24,64,128]{3,2,1,0:T(8,128)(2,1)} %param.9, pred[4,24]{1,0:T(4,128)(4,1)S(1)} %broadcast_compare_fusion, bf16[4,24,64,128]{3,2,1,0:T(8,128)(2,1)} %param.8), kind=kLoop, calls=%fused_computation | loop fusion | flops 1572864 | bytes 6291552 | tf_op jit(solution)/shard_map/jit(_where)/select_n | solution.py:219
  7.0 1.4 %part_kernel.3 = (f32[1,2,2,12,16,128]{5,4,3,2,1,0:T(8,128)S(1)}, s16[49,16,128]{2,1,0:T(8,128)(2,1)S(1)}, f32[1,2,2,12,16,128]{5,4,3,2,1,0:T(8,128)S(1)}, s16[49,16,128]{2,1,0:T(8,128)(2,1)S(1)}) custom-call(bf16[4,4,16,128]{3,2,1,0:T(8,128)(2,1)S(1)} %broadcast_in_dim.27.keep_ref, bf16[2,4,4,16,128]{4,3,2,1,0:T(8,128)(2,1)S(1)} %pad_maximum_fusion.refs_0_, ...), custom_call_target="tpu_custom_call" | custom-call | flops 805306368 | bytes 3145728 | tf_op jit(solution)/shard_map/part_kernel/pallas_call | solution.py:226
  9.0 1.5 %collective-permute-start.2 = (s16[49,16,128]{2,1,0:T(8,128)(2,1)S(1)}, s16[49,16,128]{2,1,0:T(8,128)(2,1)S(1)}, u32[]{:S(2)}, u32[]{:S(2)}) collective-permute-start(s16[49,16,128]{2,1,0:T(8,128)(2,1)S(1)} %get-tuple-element.24), channel_id=1, source_target_pairs={{0,4},{1,9},{2,6},{3,11},{4,0},{5,13},{6,2},{7,15},{8,12},{9,1},{1... | collective-permute-start | bytes 602120 | tf_op jit(solution)/shard_map/ppermute | solution.py:202
  11.9 1.6 %collective-permute-start.8 = (s16[49,16,128]{2,1,0:T(8,128)(2,1)S(1)}, s16[49,16,128]{2,1,0:T(8,128)(2,1)S(1)}, u32[]{:S(2)}, u32[]{:S(2)}) collective-permute-start(s16[49,16,128]{2,1,0:T(8,128)(2,1)S(1)} %get-tuple-element.25.refs_3_), channel_id=1, source_target_pairs={{0,4},{1,9},{2,6},{3,11},{4,0},{5,13},{6,2},{7,15},{8,12},{9,1},{1... | collective-permute-start | bytes 602120 | tf_op jit(solution)/shard_map/ppermute | solution.py:202
  14.3 2.6 %collective-permute-start.6 = (s16[49,16,128]{2,1,0:T(8,128)(2,1)S(1)}, s16[49,16,128]{2,1,0:T(8,128)(2,1)S(1)}, u32[]{:S(2)}, u32[]{:S(2)}) collective-permute-start(s16[49,16,128]{2,1,0:T(8,128)(2,1)S(1)} %get-tuple-element.26.refs_0_), channel_id=1, source_target_pairs={{0,16},{1,5},{2,18},{3,7},{4,20},{5,1},{6,22},{7,3},{8,24},{9,13},... | collective-permute-start | bytes 602120 | tf_op jit(solution)/shard_map/ppermute | solution.py:202
  17.1 1.6 %collective-permute-start.7 = (s16[25,16,128]{2,1,0:T(8,128)(2,1)S(1)}, s16[25,16,128]{2,1,0:T(8,128)(2,1)S(1)}, u32[]{:S(2)}, u32[]{:S(2)}) collective-permute-start(s16[25,16,128]{2,1,0:T(8,128)(2,1)S(1)} %get-tuple-element.27.refs_0_), channel_id=1, source_target_pairs={{0,8},{1,5},{2,10},{3,7},{4,12},{5,1},{6,14},{7,3},{8,0},{9,13},{1... | collective-permute-start | bytes 307208 | tf_op jit(solution)/shard_map/ppermute | solution.py:202
  18.9 2.4 %collective-permute-start.5 = (s16[25,16,128]{2,1,0:T(8,128)(2,1)S(1)}, s16[25,16,128]{2,1,0:T(8,128)(2,1)S(1)}, u32[]{:S(2)}, u32[]{:S(2)}) collective-permute-start(s16[25,16,128]{2,1,0:T(8,128)(2,1)S(1)} %get-tuple-element.29.refs_0_), channel_id=1, source_target_pairs={{0,16},{1,5},{2,18},{3,7},{4,20},{5,1},{6,22},{7,3},{8,24},{9,13},... | collective-permute-start | bytes 307208 | tf_op jit(solution)/shard_map/ppermute | solution.py:202
  21.4 1.6 %collective-permute-start.12 = (s16[25,16,128]{2,1,0:T(8,128)(2,1)S(1)}, s16[25,16,128]{2,1,0:T(8,128)(2,1)S(1)}, u32[]{:S(2)}, u32[]{:S(2)}) collective-permute-start(s16[25,16,128]{2,1,0:T(8,128)(2,1)S(1)} %get-tuple-element.33.refs_0_), channel_id=1, source_target_pairs={{0,8},{1,5},{2,10},{3,7},{4,12},{5,1},{6,14},{7,3},{8,0},{9,13},{1... | collective-permute-start | bytes 307208 | tf_op jit(solution)/shard_map/ppermute | solution.py:202
  23.1 4.2 %collective-permute-start.11 = (s16[25,16,128]{2,1,0:T(8,128)(2,1)S(1)}, s16[25,16,128]{2,1,0:T(8,128)(2,1)S(1)}, u32[]{:S(2)}, u32[]{:S(2)}) collective-permute-start(s16[25,16,128]{2,1,0:T(8,128)(2,1)S(1)} %cross_kernel.4.refs_0_.mine_ref), channel_id=1, source_target_pairs={{0,16},{1,17},{2,18},{3,19},{4,20},{5,21},{6,22},{7,23},{8,24},{9,... | collective-permute-start | bytes 307208 | tf_op jit(solution)/shard_map/ppermute | solution.py:202
  27.4 1.6 %collective-permute-start.10 = (s16[25,16,128]{2,1,0:T(8,128)(2,1)S(1)}, s16[25,16,128]{2,1,0:T(8,128)(2,1)S(1)}, u32[]{:S(2)}, u32[]{:S(2)}) collective-permute-start(s16[25,16,128]{2,1,0:T(8,128)(2,1)S(1)} %get-tuple-element.34.refs_0_), channel_id=1, source_target_pairs={{0,4},{1,9},{2,6},{3,11},{4,0},{5,13},{6,2},{7,15},{8,12},{9,1},{1... | collective-permute-start | bytes 307208 | tf_op jit(solution)/shard_map/ppermute | solution.py:202
  29.8 2.6 %collective-permute-start.16 = (s16[25,16,128]{2,1,0:T(8,128)(2,1)S(1)}, s16[25,16,128]{2,1,0:T(8,128)(2,1)S(1)}, u32[]{:S(2)}, u32[]{:S(2)}) collective-permute-start(s16[25,16,128]{2,1,0:T(8,128)(2,1)S(1)} %cross_kernel.6.refs_0_.mine_ref), channel_id=1, source_target_pairs={{0,16},{1,17},{2,18},{3,19},{4,20},{5,21},{6,22},{7,23},{8,24},{9,... | collective-permute-start | bytes 307208 | tf_op jit(solution)/shard_map/ppermute | solution.py:202
  32.5 2.5 %collective-permute-start.14 = (s16[25,16,128]{2,1,0:T(8,128)(2,1)S(1)}, s16[25,16,128]{2,1,0:T(8,128)(2,1)S(1)}, u32[]{:S(2)}, u32[]{:S(2)}) collective-permute-start(s16[25,16,128]{2,1,0:T(8,128)(2,1)S(1)} %cross_kernel.7.refs_0_.mine_ref), channel_id=1, source_target_pairs={{0,8},{1,17},{2,10},{3,19},{4,12},{5,21},{6,14},{7,23},{8,0},{9,25... | collective-permute-start | bytes 307208 | tf_op jit(solution)/shard_map/ppermute | solution.py:202
  36.8 3.0 %collective-permute-done.16.other_ref = s16[25,16,128]{2,1,0:T(8,128)(2,1)S(1)} collective-permute-done((s16[25,16,128]{2,1,0:T(8,128)(2,1)S(1)}, s16[25,16,128]{2,1,0:T(8,128)(2,1)S(1)}, u32[]{:S(2)}, u32[]{:S(2)}) %collective-permute-start.16) | collective-permute-done | bytes 102432 | tf_op jit(solution)/shard_map/ppermute | solution.py:202
  39.9 1.1 %collective-permute-start.18 = (bf16[2,12,16,128]{3,2,1,0:T(8,128)(2,1)S(1)}, bf16[2,12,16,128]{3,2,1,0:T(8,128)(2,1)S(1)}, u32[]{:S(2)}, u32[]{:S(2)}) collective-permute-start(bf16[2,12,16,128]{3,2,1,0:T(8,128)(2,1)S(1)} %final_kernel.6.refs_0_.mine_ref), channel_id=1, source_target_pairs={{0,4},{1,9},{2,6},{3,11},{4,0},{5,13},{6,2},{7,15},{8,12},{9,1},{1... | collective-permute-start | bytes 294920 | tf_op jit(solution)/shard_map/ppermute | solution.py:202
  41.6 1.8 %collective-permute-start.20 = (bf16[2,12,16,128]{3,2,1,0:T(8,128)(2,1)S(1)}, bf16[2,12,16,128]{3,2,1,0:T(8,128)(2,1)S(1)}, u32[]{:S(2)}, u32[]{:S(2)}) collective-permute-start(bf16[2,12,16,128]{3,2,1,0:T(8,128)(2,1)S(1)} %final_kernel.7.refs_0_.mine_ref), channel_id=1, source_target_pairs={{0,16},{1,5},{2,18},{3,7},{4,20},{5,1},{6,22},{7,3},{8,24},{9,13},... | collective-permute-start | bytes 294920 | tf_op jit(solution)/shard_map/ppermute | solution.py:202
  43.4 1.5 %collective-permute-start.22 = (bf16[2,2,12,16,128]{4,3,2,1,0:T(8,128)(2,1)S(1)}, bf16[2,2,12,16,128]{4,3,2,1,0:T(8,128)(2,1)S(1)}, u32[]{:S(2)}, u32[]{:S(2)}) collective-permute-start(bf16[2,2,12,16,128]{4,3,2,1,0:T(8,128)(2,1)S(1)} %merge_kernel.4.refs_0_), channel_id=1, source_target_pairs={{0,4},{1,5},{2,6},{3,7},{4,0},{5,1},{6,2},{7,3},{8,12},{9,13},{10,... | collective-permute-start | bytes 589832 | tf_op jit(solution)/shard_map/ppermute | solution.py:202
  44.9 0.9 %collective-permute-start.17 = (bf16[2,2,12,16,128]{4,3,2,1,0:T(8,128)(2,1)S(1)}, bf16[2,2,12,16,128]{4,3,2,1,0:T(8,128)(2,1)S(1)}, u32[]{:S(2)}, u32[]{:S(2)}) collective-permute-start(bf16[2,2,12,16,128]{4,3,2,1,0:T(8,128)(2,1)S(1)} %merge_kernel.5.refs_0_.refs_1_), channel_id=1, source_target_pairs={{0,16},{1,5},{2,18},{3,7},{4,20},{5,1},{6,22},{7,3},{8,24},{9,13},... | collective-permute-start | bytes 589832 | tf_op jit(solution)/shard_map/ppermute | solution.py:202
  45.8 1.8 %collective-permute-start.19 = (bf16[2,2,12,16,128]{4,3,2,1,0:T(8,128)(2,1)S(1)}, bf16[2,2,12,16,128]{4,3,2,1,0:T(8,128)(2,1)S(1)}, u32[]{:S(2)}, u32[]{:S(2)}) collective-permute-start(bf16[2,2,12,16,128]{4,3,2,1,0:T(8,128)(2,1)S(1)} %merge_kernel.6.refs_0_.refs_2_), channel_id=1, source_target_pairs={{0,8},{1,5},{2,10},{3,7},{4,12},{5,1},{6,14},{7,3},{8,0},{9,13},{1... | collective-permute-start | bytes 589832 | tf_op jit(solution)/shard_map/ppermute | solution.py:202
  48.5 2.6 %collective-permute-done.22.refs_4_ = bf16[2,2,12,16,128]{4,3,2,1,0:T(8,128)(2,1)S(1)} collective-permute-done((bf16[2,2,12,16,128]{4,3,2,1,0:T(8,128)(2,1)S(1)}, bf16[2,2,12,16,128]{4,3,2,1,0:T(8,128)(2,1)S(1)}, u32[]{:S(2)}, u32[]{:S(2)}) %collective-permute-start.22) | collective-permute-done | bytes 196640 | tf_op jit(solution)/shard_map/ppermute | solution.py:202
  51.0 1.1 %place_part.2.refs_3_ = bf16[4,24,64,128]{3,2,1,0:T(8,128)(2,1)} custom-call(bf16[2,2,12,16,128]{4,3,2,1,0:T(8,128)(2,1)S(1)} %merge_kernel.4.refs_0_, bf16[2,2,12,16,128]{4,3,2,1,0:T(8,128)(2,1)S(1)} %merge_kernel.5.refs_0_.refs_1_, bf16[2,2,12,16,128]{4,3,2,1,0:T(8,128)(2,1)S(1)} %merge_kernel.6.refs_0_.refs_2_, ...), custom_call_target="tpu_custom_call" | custom-call | tf_op jit(solution)/shard_map/place_part/pallas_call | solution.py:280
  52.1 1.3 %collective-permute-done.19.refs_1_ = bf16[2,2,12,16,128]{4,3,2,1,0:T(8,128)(2,1)S(1)} collective-permute-done((bf16[2,2,12,16,128]{4,3,2,1,0:T(8,128)(2,1)S(1)}, bf16[2,2,12,16,128]{4,3,2,1,0:T(8,128)(2,1)S(1)}, u32[]{:S(2)}, u32[]{:S(2)}) %collective-permute-start.19) | collective-permute-done | bytes 196640 | tf_op jit(solution)/shard_map/ppermute | solution.py:202
  53.6 0.9 %place_part.3 = bf16[4,24,64,128]{3,2,1,0:T(8,128)(2,1)} custom-call(bf16[2,2,12,16,128]{4,3,2,1,0:T(8,128)(2,1)S(1)} %collective-permute-done.17.refs_0_, bf16[2,2,12,16,128]{4,3,2,1,0:T(8,128)(2,1)S(1)} %collective-permute-done.19.refs_1_, bf16[2,2,12,16,128]{4,3,2,1,0:T(8,128)(2,1)S(1)} %collective-permute-done.21.refs_2_, ...), custom_call_target="tpu_custom_call", output_to_operand_aliasing={{}: (3, {})} | custom-call | tf_op jit(solution)/shard_map/place_part/pallas_call | solution.py:280
  (52 shorter events, 8.6 us)
Async XLA Ops:
  0.9 7.5 %collective-permute-start.3 = (bf16[2,4,4,16,128]{4,3,2,1,0:T(8,128)(2,1)S(1)}, bf16[2,4,4,16,128]{4,3,2,1,0:T(8,128)(2,1)S(1)}, u32[]{:S(2)}, u32[]{:S(2)}) collective-permute-start(bf16[2,4,4,16,128]{4,3,2,1,0:T(8,128)(2,1)S(1)} %pad_maximum_fusion.refs_0_), channel_id=1, source_target_pairs={{0,2},{1,3},{2,0},{3,1},{4,6},{5,7},{6,4},{7,5},{8,10},{9,11},{10,... | collective-permute-start | bytes 393224 | tf_op jit(solution)/shard_map/ppermute | solution.py:205
  3.9 3.0 %collective-permute-start = (bf16[2,4,4,16,128]{4,3,2,1,0:T(8,128)(2,1)S(1)}, bf16[2,4,4,16,128]{4,3,2,1,0:T(8,128)(2,1)S(1)}, u32[]{:S(2)}, u32[]{:S(2)}) collective-permute-start(bf16[2,4,4,16,128]{4,3,2,1,0:T(8,128)(2,1)S(1)} %pad_maximum_fusion.refs_0_), channel_id=1, source_target_pairs={{0,1},{1,0},{2,3},{3,2},{4,5},{5,4},{6,7},{7,6},{8,9},{9,8},{10,11... | collective-permute-start | bytes 393224 | tf_op jit(solution)/shard_map/ppermute | solution.py:205
  4.6 2.2 %copy-start = (s32[4]{0:T(128)S(1)}, s32[4]{0:T(128)}, u32[]{:S(2)}) copy-start(s32[4]{0:T(128)} %param.10) | copy-start | bytes 52
  8.4 5.1 %collective-permute-start.4 = (bf16[2,4,4,16,128]{4,3,2,1,0:T(8,128)(2,1)S(1)}, bf16[2,4,4,16,128]{4,3,2,1,0:T(8,128)(2,1)S(1)}, u32[]{:S(2)}, u32[]{:S(2)}) collective-permute-start(bf16[2,4,4,16,128]{4,3,2,1,0:T(8,128)(2,1)S(1)} %copy_kernel.1.refs_3_), channel_id=1, source_target_pairs={{0,1},{1,0},{2,3},{3,2},{4,5},{5,4},{6,7},{7,6},{8,9},{9,8},{10,11... | collective-permute-start | bytes 393224 | tf_op jit(solution)/shard_map/ppermute | solution.py:205
  9.0 8.0 %collective-permute-start.2 = (s16[49,16,128]{2,1,0:T(8,128)(2,1)S(1)}, s16[49,16,128]{2,1,0:T(8,128)(2,1)S(1)}, u32[]{:S(2)}, u32[]{:S(2)}) collective-permute-start(s16[49,16,128]{2,1,0:T(8,128)(2,1)S(1)} %get-tuple-element.24), channel_id=1, source_target_pairs={{0,4},{1,9},{2,6},{3,11},{4,0},{5,13},{6,2},{7,15},{8,12},{9,1},{1... | collective-permute-start | bytes 602120 | tf_op jit(solution)/shard_map/ppermute | solution.py:202
  10.5 8.3 %collective-permute-start.1 = (s16[49,16,128]{2,1,0:T(8,128)(2,1)S(1)}, s16[49,16,128]{2,1,0:T(8,128)(2,1)S(1)}, u32[]{:S(2)}, u32[]{:S(2)}) collective-permute-start(s16[49,16,128]{2,1,0:T(8,128)(2,1)S(1)} %get-tuple-element.22.refs_0_), channel_id=1, source_target_pairs={{0,4},{1,17},{2,6},{3,19},{4,0},{5,21},{6,2},{7,23},{8,12},{9,25},... | collective-permute-start | bytes 602120 | tf_op jit(solution)/shard_map/ppermute | solution.py:202
  11.9 9.4 %collective-permute-start.8 = (s16[49,16,128]{2,1,0:T(8,128)(2,1)S(1)}, s16[49,16,128]{2,1,0:T(8,128)(2,1)S(1)}, u32[]{:S(2)}, u32[]{:S(2)}) collective-permute-start(s16[49,16,128]{2,1,0:T(8,128)(2,1)S(1)} %get-tuple-element.25.refs_3_), channel_id=1, source_target_pairs={{0,4},{1,9},{2,6},{3,11},{4,0},{5,13},{6,2},{7,15},{8,12},{9,1},{1... | collective-permute-start | bytes 602120 | tf_op jit(solution)/shard_map/ppermute | solution.py:202
  14.3 13.0 %collective-permute-start.6 = (s16[49,16,128]{2,1,0:T(8,128)(2,1)S(1)}, s16[49,16,128]{2,1,0:T(8,128)(2,1)S(1)}, u32[]{:S(2)}, u32[]{:S(2)}) collective-permute-start(s16[49,16,128]{2,1,0:T(8,128)(2,1)S(1)} %get-tuple-element.26.refs_0_), channel_id=1, source_target_pairs={{0,16},{1,5},{2,18},{3,7},{4,20},{5,1},{6,22},{7,3},{8,24},{9,13},... | collective-permute-start | bytes 602120 | tf_op jit(solution)/shard_map/ppermute | solution.py:202
  17.1 5.9 %collective-permute-start.7 = (s16[25,16,128]{2,1,0:T(8,128)(2,1)S(1)}, s16[25,16,128]{2,1,0:T(8,128)(2,1)S(1)}, u32[]{:S(2)}, u32[]{:S(2)}) collective-permute-start(s16[25,16,128]{2,1,0:T(8,128)(2,1)S(1)} %get-tuple-element.27.refs_0_), channel_id=1, source_target_pairs={{0,8},{1,5},{2,10},{3,7},{4,12},{5,1},{6,14},{7,3},{8,0},{9,13},{1... | collective-permute-start | bytes 307208 | tf_op jit(solution)/shard_map/ppermute | solution.py:202
  18.9 10.2 %collective-permute-start.5 = (s16[25,16,128]{2,1,0:T(8,128)(2,1)S(1)}, s16[25,16,128]{2,1,0:T(8,128)(2,1)S(1)}, u32[]{:S(2)}, u32[]{:S(2)}) collective-permute-start(s16[25,16,128]{2,1,0:T(8,128)(2,1)S(1)} %get-tuple-element.29.refs_0_), channel_id=1, source_target_pairs={{0,16},{1,5},{2,18},{3,7},{4,20},{5,1},{6,22},{7,3},{8,24},{9,13},... | collective-permute-start | bytes 307208 | tf_op jit(solution)/shard_map/ppermute | solution.py:202
  21.4 8.2 %collective-permute-start.12 = (s16[25,16,128]{2,1,0:T(8,128)(2,1)S(1)}, s16[25,16,128]{2,1,0:T(8,128)(2,1)S(1)}, u32[]{:S(2)}, u32[]{:S(2)}) collective-permute-start(s16[25,16,128]{2,1,0:T(8,128)(2,1)S(1)} %get-tuple-element.33.refs_0_), channel_id=1, source_target_pairs={{0,8},{1,5},{2,10},{3,7},{4,12},{5,1},{6,14},{7,3},{8,0},{9,13},{1... | collective-permute-start | bytes 307208 | tf_op jit(solution)/shard_map/ppermute | solution.py:202
  23.1 9.2 %collective-permute-start.11 = (s16[25,16,128]{2,1,0:T(8,128)(2,1)S(1)}, s16[25,16,128]{2,1,0:T(8,128)(2,1)S(1)}, u32[]{:S(2)}, u32[]{:S(2)}) collective-permute-start(s16[25,16,128]{2,1,0:T(8,128)(2,1)S(1)} %cross_kernel.4.refs_0_.mine_ref), channel_id=1, source_target_pairs={{0,16},{1,17},{2,18},{3,19},{4,20},{5,21},{6,22},{7,23},{8,24},{9,... | collective-permute-start | bytes 307208 | tf_op jit(solution)/shard_map/ppermute | solution.py:202
  27.4 4.9 %collective-permute-start.10 = (s16[25,16,128]{2,1,0:T(8,128)(2,1)S(1)}, s16[25,16,128]{2,1,0:T(8,128)(2,1)S(1)}, u32[]{:S(2)}, u32[]{:S(2)}) collective-permute-start(s16[25,16,128]{2,1,0:T(8,128)(2,1)S(1)} %get-tuple-element.34.refs_0_), channel_id=1, source_target_pairs={{0,4},{1,9},{2,6},{3,11},{4,0},{5,13},{6,2},{7,15},{8,12},{9,1},{1... | collective-permute-start | bytes 307208 | tf_op jit(solution)/shard_map/ppermute | solution.py:202
  29.1 6.7 %collective-permute-start.9 = (s16[25,16,128]{2,1,0:T(8,128)(2,1)S(1)}, s16[25,16,128]{2,1,0:T(8,128)(2,1)S(1)}, u32[]{:S(2)}, u32[]{:S(2)}) collective-permute-start(s16[25,16,128]{2,1,0:T(8,128)(2,1)S(1)} %cross_kernel.5.refs_0_.mine_ref), channel_id=1, source_target_pairs={{0,8},{1,9},{2,10},{3,11},{4,12},{5,13},{6,14},{7,15},{8,0},{9,1},... | collective-permute-start | bytes 307208 | tf_op jit(solution)/shard_map/ppermute | solution.py:202
  29.8 10.1 %collective-permute-start.16 = (s16[25,16,128]{2,1,0:T(8,128)(2,1)S(1)}, s16[25,16,128]{2,1,0:T(8,128)(2,1)S(1)}, u32[]{:S(2)}, u32[]{:S(2)}) collective-permute-start(s16[25,16,128]{2,1,0:T(8,128)(2,1)S(1)} %cross_kernel.6.refs_0_.mine_ref), channel_id=1, source_target_pairs={{0,16},{1,17},{2,18},{3,19},{4,20},{5,21},{6,22},{7,23},{8,24},{9,... | collective-permute-start | bytes 307208 | tf_op jit(solution)/shard_map/ppermute | solution.py:202
  32.5 9.0 %collective-permute-start.14 = (s16[25,16,128]{2,1,0:T(8,128)(2,1)S(1)}, s16[25,16,128]{2,1,0:T(8,128)(2,1)S(1)}, u32[]{:S(2)}, u32[]{:S(2)}) collective-permute-start(s16[25,16,128]{2,1,0:T(8,128)(2,1)S(1)} %cross_kernel.7.refs_0_.mine_ref), channel_id=1, source_target_pairs={{0,8},{1,17},{2,10},{3,19},{4,12},{5,21},{6,14},{7,23},{8,0},{9,25... | collective-permute-start | bytes 307208 | tf_op jit(solution)/shard_map/ppermute | solution.py:202
  35.0 6.4 %collective-permute-start.15 = (bf16[2,12,16,128]{3,2,1,0:T(8,128)(2,1)S(1)}, bf16[2,12,16,128]{3,2,1,0:T(8,128)(2,1)S(1)}, u32[]{:S(2)}, u32[]{:S(2)}) collective-permute-start(bf16[2,12,16,128]{3,2,1,0:T(8,128)(2,1)S(1)} %final_kernel.4.refs_0_.mine_ref), channel_id=1, source_target_pairs={{0,8},{1,9},{2,10},{3,11},{4,12},{5,13},{6,14},{7,15},{8,0},{9,1},... | collective-permute-start | bytes 294920 | tf_op jit(solution)/shard_map/ppermute | solution.py:202
  35.9 8.9 %collective-permute-start.13 = (bf16[2,12,16,128]{3,2,1,0:T(8,128)(2,1)S(1)}, bf16[2,12,16,128]{3,2,1,0:T(8,128)(2,1)S(1)}, u32[]{:S(2)}, u32[]{:S(2)}) collective-permute-start(bf16[2,12,16,128]{3,2,1,0:T(8,128)(2,1)S(1)} %final_kernel.5.refs_0_.mine_ref), channel_id=1, source_target_pairs={{0,4},{1,17},{2,6},{3,19},{4,0},{5,21},{6,2},{7,23},{8,12},{9,25},... | collective-permute-start | bytes 294920 | tf_op jit(solution)/shard_map/ppermute | solution.py:202
  39.9 5.9 %collective-permute-start.18 = (bf16[2,12,16,128]{3,2,1,0:T(8,128)(2,1)S(1)}, bf16[2,12,16,128]{3,2,1,0:T(8,128)(2,1)S(1)}, u32[]{:S(2)}, u32[]{:S(2)}) collective-permute-start(bf16[2,12,16,128]{3,2,1,0:T(8,128)(2,1)S(1)} %final_kernel.6.refs_0_.mine_ref), channel_id=1, source_target_pairs={{0,4},{1,9},{2,6},{3,11},{4,0},{5,13},{6,2},{7,15},{8,12},{9,1},{1... | collective-permute-start | bytes 294920 | tf_op jit(solution)/shard_map/ppermute | solution.py:202
  41.6 6.0 %collective-permute-start.20 = (bf16[2,12,16,128]{3,2,1,0:T(8,128)(2,1)S(1)}, bf16[2,12,16,128]{3,2,1,0:T(8,128)(2,1)S(1)}, u32[]{:S(2)}, u32[]{:S(2)}) collective-permute-start(bf16[2,12,16,128]{3,2,1,0:T(8,128)(2,1)S(1)} %final_kernel.7.refs_0_.mine_ref), channel_id=1, source_target_pairs={{0,16},{1,5},{2,18},{3,7},{4,20},{5,1},{6,22},{7,3},{8,24},{9,13},... | collective-permute-start | bytes 294920 | tf_op jit(solution)/shard_map/ppermute | solution.py:202
  43.4 7.7 %collective-permute-start.22 = (bf16[2,2,12,16,128]{4,3,2,1,0:T(8,128)(2,1)S(1)}, bf16[2,2,12,16,128]{4,3,2,1,0:T(8,128)(2,1)S(1)}, u32[]{:S(2)}, u32[]{:S(2)}) collective-permute-start(bf16[2,2,12,16,128]{4,3,2,1,0:T(8,128)(2,1)S(1)} %merge_kernel.4.refs_0_), channel_id=1, source_target_pairs={{0,4},{1,5},{2,6},{3,7},{4,0},{5,1},{6,2},{7,3},{8,12},{9,13},{10,... | collective-permute-start | bytes 589832 | tf_op jit(solution)/shard_map/ppermute | solution.py:202
  44.9 8.8 %collective-permute-start.17 = (bf16[2,2,12,16,128]{4,3,2,1,0:T(8,128)(2,1)S(1)}, bf16[2,2,12,16,128]{4,3,2,1,0:T(8,128)(2,1)S(1)}, u32[]{:S(2)}, u32[]{:S(2)}) collective-permute-start(bf16[2,2,12,16,128]{4,3,2,1,0:T(8,128)(2,1)S(1)} %merge_kernel.5.refs_0_.refs_1_), channel_id=1, source_target_pairs={{0,16},{1,5},{2,18},{3,7},{4,20},{5,1},{6,22},{7,3},{8,24},{9,13},... | collective-permute-start | bytes 589832 | tf_op jit(solution)/shard_map/ppermute | solution.py:202
  45.8 7.7 %collective-permute-start.19 = (bf16[2,2,12,16,128]{4,3,2,1,0:T(8,128)(2,1)S(1)}, bf16[2,2,12,16,128]{4,3,2,1,0:T(8,128)(2,1)S(1)}, u32[]{:S(2)}, u32[]{:S(2)}) collective-permute-start(bf16[2,2,12,16,128]{4,3,2,1,0:T(8,128)(2,1)S(1)} %merge_kernel.6.refs_0_.refs_2_), channel_id=1, source_target_pairs={{0,8},{1,5},{2,10},{3,7},{4,12},{5,1},{6,14},{7,3},{8,0},{9,13},{1... | collective-permute-start | bytes 589832 | tf_op jit(solution)/shard_map/ppermute | solution.py:202
  47.6 6.0 %collective-permute-start.21 = (bf16[2,2,12,16,128]{4,3,2,1,0:T(8,128)(2,1)S(1)}, bf16[2,2,12,16,128]{4,3,2,1,0:T(8,128)(2,1)S(1)}, u32[]{:S(2)}, u32[]{:S(2)}) collective-permute-start(bf16[2,2,12,16,128]{4,3,2,1,0:T(8,128)(2,1)S(1)} %merge_kernel.7.refs_3_), channel_id=1, source_target_pairs={{0,4},{1,9},{2,6},{3,11},{4,0},{5,13},{6,2},{7,15},{8,12},{9,1},{1... | collective-permute-start | bytes 589832 | tf_op jit(solution)/shard_map/ppermute | solution.py:202

commit v6 on v5

--- a/solution.py
+++ b/solution.py
@@ -8,7 +8,7 @@
 from jax.sharding import PartitionSpec as P
 
 BITS = {"y": 0, "z0": 1, "z1": 2}
-ORDERS = ((("y", "z0", "z1", "z0", "y"), ("z0", "y", "z1", "z0", "y")), (("y", "z1", "z0", "y", "z1"), ("z1", "y", "z0", "z1", "y")), (("y", "z0", "z1", "y", "z0"), ("z0", "y", "z1", "z0", "y")), (("z1", "y", "z0", "z1", "y"), ("y", "z0", "z1", "y", "z0")))
+ORDERS = ((("y", "z0", "z1", "z0", "y"), ("z0", "y", "z1", "z0", "y")), (("y", "z1", "z0", "y", "z1"), ("z1", "y", "z0", "z1", "y")), (("y", "z0", "z1", "y", "z0"), ("z0", "y", "z1", "y", "z0")), (("z1", "y", "z0", "z1", "y"), ("y", "z0", "z1", "y", "z0")))
 STEPS = (0, 1, 2, 0, 3, 1, 2, 0, 3, 1, 2, 0, 3, 1, 2, 3)
 PLACES = (((0, 0), (1, 0), (2, 0), (3, 0), (0, 1)), ((1, 1), (2, 1), (3, 1)))
 GROUP = 3

time: 54.8 us -> 55 us (level)
  no operation moved by 1% of the time
where the time goes in v6:
time: 55 us; the launch traced here: 54.2 us
  starting transfers between devices  35.7 us (65%)
  waiting for transfers between devices  8.15 us (15%)
  Pallas kernels  6.23 us (11%)
  other arithmetic  3.86 us (7%)
    ppermute x20, starting transfers between devices, swap(): return lax.ppermute(v, ('hist', 'col'), pairs)  32.1 us
    ppermute x20, waiting for transfers between devices, swap(): return lax.ppermute(v, ('hist', 'col'), pairs)  8.14 us
    pallas_call x20, Pallas kernels, call(): pl.pallas_call(kernel, out_shape=out_shape, in_specs=[vmem] * len(args),...  4.23 us
    ppermute x3, starting transfers between devices, swap_col(): return lax.ppermute(v, 'col', [(i, i ^ k) for i in range(n_col)])  3.58 us
    select_n x1, other arithmetic, staged(): jnp.where(after, green, zero)  2.17 us
    pallas_call x2, Pallas kernels, put(): pl.pallas_call(functools.partial(place_kernel, [(k, ORDERS[k], last) for...  2 us
  transfers between devices with their start and end apart: 23, of which 6 were waited for; matrix products, arithmetic and copies ran while one was open for 6% of the time, Pallas kernels for 10%

profile of v6, /device:TPU:0, one launch (start us, length us, event | category | flops | bytes accessed | tf_op | source)
XLA Modules:
  0.0 54.2 jit_solution(13329197444105812284)
XLA Ops:
  0.0 0.9 %pad_maximum_fusion.refs_0_ = bf16[2,4,4,16,128]{4,3,2,1,0:T(8,128)(2,1)S(1)} fusion(bf16[1,4,4,16,128]{4,3,2,1,0:T(8,128)(2,1)} %bitcast.2, bf16[1,4,4,16,128]{4,3,2,1,0:T(8,128)(2,1)} %bitcast.3), kind=kLoop, calls=%fused_computation.2 | loop fusion | flops 65536 | bytes 262144 | tf_op jit(solution)/shard_map/stack | solution.py:213
  0.9 3.0 %collective-permute-start.3 = (bf16[2,4,4,16,128]{4,3,2,1,0:T(8,128)(2,1)S(1)}, bf16[2,4,4,16,128]{4,3,2,1,0:T(8,128)(2,1)S(1)}, u32[]{:S(2)}, u32[]{:S(2)}) collective-permute-start(bf16[2,4,4,16,128]{4,3,2,1,0:T(8,128)(2,1)S(1)} %pad_maximum_fusion.refs_0_), channel_id=1, source_target_pairs={{0,2},{1,3},{2,0},{3,1},{4,6},{5,7},{6,4},{7,5},{8,10},{9,11},{10,... | collective-permute-start | bytes 393224 | tf_op jit(solution)/shard_map/ppermute | solution.py:205
  4.6 2.2 %broadcast_select_fusion = (bf16[4,24,64,128]{3,2,1,0:T(8,128)(2,1)S(1)}, bf16[4,24,64,128]{3,2,1,0:T(8,128)(2,1)S(1)}) fusion(bf16[4,24,64,128]{3,2,1,0:T(8,128)(2,1)} %param.9, pred[4,24]{1,0:T(4,128)(4,1)S(1)} %broadcast_compare_fusion, bf16[4,24,64,128]{3,2,1,0:T(8,128)(2,1)} %param.8), kind=kLoop, calls=%fused_computation | loop fusion | flops 1572864 | bytes 6291552 | tf_op jit(solution)/shard_map/jit(_where)/select_n | solution.py:219
  7.0 1.4 %part_kernel.3 = (f32[1,2,2,12,16,128]{5,4,3,2,1,0:T(8,128)S(1)}, s16[49,16,128]{2,1,0:T(8,128)(2,1)S(1)}, f32[1,2,2,12,16,128]{5,4,3,2,1,0:T(8,128)S(1)}, s16[49,16,128]{2,1,0:T(8,128)(2,1)S(1)}) custom-call(bf16[4,4,16,128]{3,2,1,0:T(8,128)(2,1)S(1)} %broadcast_in_dim.27.keep_ref, bf16[2,4,4,16,128]{4,3,2,1,0:T(8,128)(2,1)S(1)} %pad_maximum_fusion.refs_0_, ...), custom_call_target="tpu_custom_call" | custom-call | flops 805306368 | bytes 3145728 | tf_op jit(solution)/shard_map/part_kernel/pallas_call | solution.py:226
  9.0 1.5 %collective-permute-start.2 = (s16[49,16,128]{2,1,0:T(8,128)(2,1)S(1)}, s16[49,16,128]{2,1,0:T(8,128)(2,1)S(1)}, u32[]{:S(2)}, u32[]{:S(2)}) collective-permute-start(s16[49,16,128]{2,1,0:T(8,128)(2,1)S(1)} %get-tuple-element.24), channel_id=1, source_target_pairs={{0,4},{1,9},{2,6},{3,11},{4,0},{5,13},{6,2},{7,15},{8,12},{9,1},{1... | collective-permute-start | bytes 602120 | tf_op jit(solution)/shard_map/ppermute | solution.py:202
  11.0 0.9 %part_kernel.4 = (f32[1,2,2,12,16,128]{5,4,3,2,1,0:T(8,128)S(1)}, s16[49,16,128]{2,1,0:T(8,128)(2,1)S(1)}) custom-call(bf16[4,4,16,128]{3,2,1,0:T(8,128)(2,1)S(1)} %broadcast_in_dim.27.keep_ref, bf16[2,4,4,16,128]{4,3,2,1,0:T(8,128)(2,1)S(1)} %collective-permute-done.3.in_ref.refs_0_, bf16[4,24,64,128]{3,2,1,0:T(8,128)(2,1)S(1)} %get-tuple-element.38.refs_2_.refs_1_, ...), custom_call_target="tpu_custom_call" | custom-call | flops 402653184 | bytes 3145728 | tf_op jit(solution)/shard_map/part_kernel/pallas_call | solution.py:226
  11.9 1.6 %collective-permute-start.8 = (s16[49,16,128]{2,1,0:T(8,128)(2,1)S(1)}, s16[49,16,128]{2,1,0:T(8,128)(2,1)S(1)}, u32[]{:S(2)}, u32[]{:S(2)}) collective-permute-start(s16[49,16,128]{2,1,0:T(8,128)(2,1)S(1)} %get-tuple-element.25.refs_3_), channel_id=1, source_target_pairs={{0,4},{1,9},{2,6},{3,11},{4,0},{5,13},{6,2},{7,15},{8,12},{9,1},{1... | collective-permute-start | bytes 602120 | tf_op jit(solution)/shard_map/ppermute | solution.py:202
  14.3 2.6 %collective-permute-start.6 = (s16[49,16,128]{2,1,0:T(8,128)(2,1)S(1)}, s16[49,16,128]{2,1,0:T(8,128)(2,1)S(1)}, u32[]{:S(2)}, u32[]{:S(2)}) collective-permute-start(s16[49,16,128]{2,1,0:T(8,128)(2,1)S(1)} %get-tuple-element.26.refs_0_), channel_id=1, source_target_pairs={{0,16},{1,5},{2,18},{3,7},{4,20},{5,1},{6,22},{7,3},{8,24},{9,13},... | collective-permute-start | bytes 602120 | tf_op jit(solution)/shard_map/ppermute | solution.py:202
  17.1 1.6 %collective-permute-start.7 = (s16[25,16,128]{2,1,0:T(8,128)(2,1)S(1)}, s16[25,16,128]{2,1,0:T(8,128)(2,1)S(1)}, u32[]{:S(2)}, u32[]{:S(2)}) collective-permute-start(s16[25,16,128]{2,1,0:T(8,128)(2,1)S(1)} %get-tuple-element.27.refs_0_), channel_id=1, source_target_pairs={{0,8},{1,5},{2,10},{3,7},{4,12},{5,1},{6,14},{7,3},{8,0},{9,13},{1... | collective-permute-start | bytes 307208 | tf_op jit(solution)/shard_map/ppermute | solution.py:202
  18.9 2.4 %collective-permute-start.5 = (s16[25,16,128]{2,1,0:T(8,128)(2,1)S(1)}, s16[25,16,128]{2,1,0:T(8,128)(2,1)S(1)}, u32[]{:S(2)}, u32[]{:S(2)}) collective-permute-start(s16[25,16,128]{2,1,0:T(8,128)(2,1)S(1)} %get-tuple-element.29.refs_0_), channel_id=1, source_target_pairs={{0,16},{1,5},{2,18},{3,7},{4,20},{5,1},{6,22},{7,3},{8,24},{9,13},... | collective-permute-start | bytes 307208 | tf_op jit(solution)/shard_map/ppermute | solution.py:202
  21.4 1.6 %collective-permute-start.12 = (s16[25,16,128]{2,1,0:T(8,128)(2,1)S(1)}, s16[25,16,128]{2,1,0:T(8,128)(2,1)S(1)}, u32[]{:S(2)}, u32[]{:S(2)}) collective-permute-start(s16[25,16,128]{2,1,0:T(8,128)(2,1)S(1)} %get-tuple-element.33.refs_0_), channel_id=1, source_target_pairs={{0,8},{1,5},{2,10},{3,7},{4,12},{5,1},{6,14},{7,3},{8,0},{9,13},{1... | collective-permute-start | bytes 307208 | tf_op jit(solution)/shard_map/ppermute | solution.py:202
  23.1 4.2 %collective-permute-start.11 = (s16[25,16,128]{2,1,0:T(8,128)(2,1)S(1)}, s16[25,16,128]{2,1,0:T(8,128)(2,1)S(1)}, u32[]{:S(2)}, u32[]{:S(2)}) collective-permute-start(s16[25,16,128]{2,1,0:T(8,128)(2,1)S(1)} %cross_kernel.4.refs_0_.mine_ref), channel_id=1, source_target_pairs={{0,16},{1,17},{2,18},{3,19},{4,20},{5,21},{6,22},{7,23},{8,24},{9,... | collective-permute-start | bytes 307208 | tf_op jit(solution)/shard_map/ppermute | solution.py:202
  27.4 1.6 %collective-permute-start.10 = (s16[25,16,128]{2,1,0:T(8,128)(2,1)S(1)}, s16[25,16,128]{2,1,0:T(8,128)(2,1)S(1)}, u32[]{:S(2)}, u32[]{:S(2)}) collective-permute-start(s16[25,16,128]{2,1,0:T(8,128)(2,1)S(1)} %get-tuple-element.34.refs_0_), channel_id=1, source_target_pairs={{0,4},{1,9},{2,6},{3,11},{4,0},{5,13},{6,2},{7,15},{8,12},{9,1},{1... | collective-permute-start | bytes 307208 | tf_op jit(solution)/shard_map/ppermute | solution.py:202
  29.8 2.6 %collective-permute-start.16 = (s16[25,16,128]{2,1,0:T(8,128)(2,1)S(1)}, s16[25,16,128]{2,1,0:T(8,128)(2,1)S(1)}, u32[]{:S(2)}, u32[]{:S(2)}) collective-permute-start(s16[25,16,128]{2,1,0:T(8,128)(2,1)S(1)} %cross_kernel.6.refs_0_.mine_ref), channel_id=1, source_target_pairs={{0,16},{1,17},{2,18},{3,19},{4,20},{5,21},{6,22},{7,23},{8,24},{9,... | collective-permute-start | bytes 307208 | tf_op jit(solution)/shard_map/ppermute | solution.py:202
  32.5 2.5 %collective-permute-start.14 = (s16[25,16,128]{2,1,0:T(8,128)(2,1)S(1)}, s16[25,16,128]{2,1,0:T(8,128)(2,1)S(1)}, u32[]{:S(2)}, u32[]{:S(2)}) collective-permute-start(s16[25,16,128]{2,1,0:T(8,128)(2,1)S(1)} %cross_kernel.7.refs_0_.mine_ref), channel_id=1, source_target_pairs={{0,8},{1,17},{2,10},{3,19},{4,12},{5,21},{6,14},{7,23},{8,0},{9,25... | collective-permute-start | bytes 307208 | tf_op jit(solution)/shard_map/ppermute | solution.py:202
  36.8 3.0 %collective-permute-done.16.other_ref = s16[25,16,128]{2,1,0:T(8,128)(2,1)S(1)} collective-permute-done((s16[25,16,128]{2,1,0:T(8,128)(2,1)S(1)}, s16[25,16,128]{2,1,0:T(8,128)(2,1)S(1)}, u32[]{:S(2)}, u32[]{:S(2)}) %collective-permute-start.16) | collective-permute-done | bytes 102432 | tf_op jit(solution)/shard_map/ppermute | solution.py:202
  39.9 1.1 %collective-permute-start.18 = (bf16[2,12,16,128]{3,2,1,0:T(8,128)(2,1)S(1)}, bf16[2,12,16,128]{3,2,1,0:T(8,128)(2,1)S(1)}, u32[]{:S(2)}, u32[]{:S(2)}) collective-permute-start(bf16[2,12,16,128]{3,2,1,0:T(8,128)(2,1)S(1)} %final_kernel.6.refs_0_.mine_ref), channel_id=1, source_target_pairs={{0,4},{1,5},{2,6},{3,7},{4,0},{5,1},{6,2},{7,3},{8,12},{9,13},{10,... | collective-permute-start | bytes 294920 | tf_op jit(solution)/shard_map/ppermute | solution.py:202
  41.1 1.9 %collective-permute-start.20 = (bf16[2,12,16,128]{3,2,1,0:T(8,128)(2,1)S(1)}, bf16[2,12,16,128]{3,2,1,0:T(8,128)(2,1)S(1)}, u32[]{:S(2)}, u32[]{:S(2)}) collective-permute-start(bf16[2,12,16,128]{3,2,1,0:T(8,128)(2,1)S(1)} %final_kernel.7.refs_0_.mine_ref), channel_id=1, source_target_pairs={{0,16},{1,5},{2,18},{3,7},{4,20},{5,1},{6,22},{7,3},{8,24},{9,13},... | collective-permute-start | bytes 294920 | tf_op jit(solution)/shard_map/ppermute | solution.py:202
  43.0 1.5 %collective-permute-start.22 = (bf16[2,2,12,16,128]{4,3,2,1,0:T(8,128)(2,1)S(1)}, bf16[2,2,12,16,128]{4,3,2,1,0:T(8,128)(2,1)S(1)}, u32[]{:S(2)}, u32[]{:S(2)}) collective-permute-start(bf16[2,2,12,16,128]{4,3,2,1,0:T(8,128)(2,1)S(1)} %merge_kernel.4.refs_0_), channel_id=1, source_target_pairs={{0,4},{1,5},{2,6},{3,7},{4,0},{5,1},{6,2},{7,3},{8,12},{9,13},{10,... | collective-permute-start | bytes 589832 | tf_op jit(solution)/shard_map/ppermute | solution.py:202
  44.6 0.9 %collective-permute-start.17 = (bf16[2,2,12,16,128]{4,3,2,1,0:T(8,128)(2,1)S(1)}, bf16[2,2,12,16,128]{4,3,2,1,0:T(8,128)(2,1)S(1)}, u32[]{:S(2)}, u32[]{:S(2)}) collective-permute-start(bf16[2,2,12,16,128]{4,3,2,1,0:T(8,128)(2,1)S(1)} %merge_kernel.5.refs_0_.refs_1_), channel_id=1, source_target_pairs={{0,16},{1,5},{2,18},{3,7},{4,20},{5,1},{6,22},{7,3},{8,24},{9,13},... | collective-permute-start | bytes 589832 | tf_op jit(solution)/shard_map/ppermute | solution.py:202
  45.7 1.6 %collective-permute-start.19 = (bf16[2,2,12,16,128]{4,3,2,1,0:T(8,128)(2,1)S(1)}, bf16[2,2,12,16,128]{4,3,2,1,0:T(8,128)(2,1)S(1)}, u32[]{:S(2)}, u32[]{:S(2)}) collective-permute-start(bf16[2,2,12,16,128]{4,3,2,1,0:T(8,128)(2,1)S(1)} %merge_kernel.6.refs_0_.refs_2_), channel_id=1, source_target_pairs={{0,8},{1,9},{2,10},{3,11},{4,12},{5,13},{6,14},{7,15},{8,0},{9,1},... | collective-permute-start | bytes 589832 | tf_op jit(solution)/shard_map/ppermute | solution.py:202
  48.9 1.1 %place_part.2.refs_3_ = bf16[4,24,64,128]{3,2,1,0:T(8,128)(2,1)} custom-call(bf16[2,2,12,16,128]{4,3,2,1,0:T(8,128)(2,1)S(1)} %merge_kernel.4.refs_0_, bf16[2,2,12,16,128]{4,3,2,1,0:T(8,128)(2,1)S(1)} %merge_kernel.5.refs_0_.refs_1_, bf16[2,2,12,16,128]{4,3,2,1,0:T(8,128)(2,1)S(1)} %merge_kernel.6.refs_0_.refs_2_, ...), custom_call_target="tpu_custom_call" | custom-call | tf_op jit(solution)/shard_map/place_part/pallas_call | solution.py:280
  50.0 3.2 %collective-permute-done.19.refs_1_ = bf16[2,2,12,16,128]{4,3,2,1,0:T(8,128)(2,1)S(1)} collective-permute-done((bf16[2,2,12,16,128]{4,3,2,1,0:T(8,128)(2,1)S(1)}, bf16[2,2,12,16,128]{4,3,2,1,0:T(8,128)(2,1)S(1)}, u32[]{:S(2)}, u32[]{:S(2)}) %collective-permute-start.19) | collective-permute-done | bytes 196640 | tf_op jit(solution)/shard_map/ppermute | solution.py:202
  53.3 0.9 %place_part.3 = bf16[4,24,64,128]{3,2,1,0:T(8,128)(2,1)} custom-call(bf16[2,2,12,16,128]{4,3,2,1,0:T(8,128)(2,1)S(1)} %collective-permute-done.17.refs_0_, bf16[2,2,12,16,128]{4,3,2,1,0:T(8,128)(2,1)S(1)} %collective-permute-done.19.refs_1_, bf16[2,2,12,16,128]{4,3,2,1,0:T(8,128)(2,1)S(1)} %collective-permute-done.21.refs_2_, ...), custom_call_target="tpu_custom_call", output_to_operand_aliasing={{}: (3, {})} | custom-call | tf_op jit(solution)/shard_map/place_part/pallas_call | solution.py:280
  (52 shorter events, 8.2 us)
Async XLA Ops:
  0.9 7.5 %collective-permute-start.3 = (bf16[2,4,4,16,128]{4,3,2,1,0:T(8,128)(2,1)S(1)}, bf16[2,4,4,16,128]{4,3,2,1,0:T(8,128)(2,1)S(1)}, u32[]{:S(2)}, u32[]{:S(2)}) collective-permute-start(bf16[2,4,4,16,128]{4,3,2,1,0:T(8,128)(2,1)S(1)} %pad_maximum_fusion.refs_0_), channel_id=1, source_target_pairs={{0,2},{1,3},{2,0},{3,1},{4,6},{5,7},{6,4},{7,5},{8,10},{9,11},{10,... | collective-permute-start | bytes 393224 | tf_op jit(solution)/shard_map/ppermute | solution.py:205
  3.9 3.0 %collective-permute-start = (bf16[2,4,4,16,128]{4,3,2,1,0:T(8,128)(2,1)S(1)}, bf16[2,4,4,16,128]{4,3,2,1,0:T(8,128)(2,1)S(1)}, u32[]{:S(2)}, u32[]{:S(2)}) collective-permute-start(bf16[2,4,4,16,128]{4,3,2,1,0:T(8,128)(2,1)S(1)} %pad_maximum_fusion.refs_0_), channel_id=1, source_target_pairs={{0,1},{1,0},{2,3},{3,2},{4,5},{5,4},{6,7},{7,6},{8,9},{9,8},{10,11... | collective-permute-start | bytes 393224 | tf_op jit(solution)/shard_map/ppermute | solution.py:205
  4.6 2.2 %copy-start = (s32[4]{0:T(128)S(1)}, s32[4]{0:T(128)}, u32[]{:S(2)}) copy-start(s32[4]{0:T(128)} %param.10) | copy-start | bytes 52
  8.4 5.1 %collective-permute-start.4 = (bf16[2,4,4,16,128]{4,3,2,1,0:T(8,128)(2,1)S(1)}, bf16[2,4,4,16,128]{4,3,2,1,0:T(8,128)(2,1)S(1)}, u32[]{:S(2)}, u32[]{:S(2)}) collective-permute-start(bf16[2,4,4,16,128]{4,3,2,1,0:T(8,128)(2,1)S(1)} %copy_kernel.1.refs_3_), channel_id=1, source_target_pairs={{0,1},{1,0},{2,3},{3,2},{4,5},{5,4},{6,7},{7,6},{8,9},{9,8},{10,11... | collective-permute-start | bytes 393224 | tf_op jit(solution)/shard_map/ppermute | solution.py:205
  9.0 8.0 %collective-permute-start.2 = (s16[49,16,128]{2,1,0:T(8,128)(2,1)S(1)}, s16[49,16,128]{2,1,0:T(8,128)(2,1)S(1)}, u32[]{:S(2)}, u32[]{:S(2)}) collective-permute-start(s16[49,16,128]{2,1,0:T(8,128)(2,1)S(1)} %get-tuple-element.24), channel_id=1, source_target_pairs={{0,4},{1,9},{2,6},{3,11},{4,0},{5,13},{6,2},{7,15},{8,12},{9,1},{1... | collective-permute-start | bytes 602120 | tf_op jit(solution)/shard_map/ppermute | solution.py:202
  10.5 8.3 %collective-permute-start.1 = (s16[49,16,128]{2,1,0:T(8,128)(2,1)S(1)}, s16[49,16,128]{2,1,0:T(8,128)(2,1)S(1)}, u32[]{:S(2)}, u32[]{:S(2)}) collective-permute-start(s16[49,16,128]{2,1,0:T(8,128)(2,1)S(1)} %get-tuple-element.22.refs_0_), channel_id=1, source_target_pairs={{0,4},{1,17},{2,6},{3,19},{4,0},{5,21},{6,2},{7,23},{8,12},{9,25},... | collective-permute-start | bytes 602120 | tf_op jit(solution)/shard_map/ppermute | solution.py:202
  11.9 9.4 %collective-permute-start.8 = (s16[49,16,128]{2,1,0:T(8,128)(2,1)S(1)}, s16[49,16,128]{2,1,0:T(8,128)(2,1)S(1)}, u32[]{:S(2)}, u32[]{:S(2)}) collective-permute-start(s16[49,16,128]{2,1,0:T(8,128)(2,1)S(1)} %get-tuple-element.25.refs_3_), channel_id=1, source_target_pairs={{0,4},{1,9},{2,6},{3,11},{4,0},{5,13},{6,2},{7,15},{8,12},{9,1},{1... | collective-permute-start | bytes 602120 | tf_op jit(solution)/shard_map/ppermute | solution.py:202
  14.3 13.0 %collective-permute-start.6 = (s16[49,16,128]{2,1,0:T(8,128)(2,1)S(1)}, s16[49,16,128]{2,1,0:T(8,128)(2,1)S(1)}, u32[]{:S(2)}, u32[]{:S(2)}) collective-permute-start(s16[49,16,128]{2,1,0:T(8,128)(2,1)S(1)} %get-tuple-element.26.refs_0_), channel_id=1, source_target_pairs={{0,16},{1,5},{2,18},{3,7},{4,20},{5,1},{6,22},{7,3},{8,24},{9,13},... | collective-permute-start | bytes 602120 | tf_op jit(solution)/shard_map/ppermute | solution.py:202
  17.1 5.9 %collective-permute-start.7 = (s16[25,16,128]{2,1,0:T(8,128)(2,1)S(1)}, s16[25,16,128]{2,1,0:T(8,128)(2,1)S(1)}, u32[]{:S(2)}, u32[]{:S(2)}) collective-permute-start(s16[25,16,128]{2,1,0:T(8,128)(2,1)S(1)} %get-tuple-element.27.refs_0_), channel_id=1, source_target_pairs={{0,8},{1,5},{2,10},{3,7},{4,12},{5,1},{6,14},{7,3},{8,0},{9,13},{1... | collective-permute-start | bytes 307208 | tf_op jit(solution)/shard_map/ppermute | solution.py:202
  18.9 10.2 %collective-permute-start.5 = (s16[25,16,128]{2,1,0:T(8,128)(2,1)S(1)}, s16[25,16,128]{2,1,0:T(8,128)(2,1)S(1)}, u32[]{:S(2)}, u32[]{:S(2)}) collective-permute-start(s16[25,16,128]{2,1,0:T(8,128)(2,1)S(1)} %get-tuple-element.29.refs_0_), channel_id=1, source_target_pairs={{0,16},{1,5},{2,18},{3,7},{4,20},{5,1},{6,22},{7,3},{8,24},{9,13},... | collective-permute-start | bytes 307208 | tf_op jit(solution)/shard_map/ppermute | solution.py:202
  21.4 8.2 %collective-permute-start.12 = (s16[25,16,128]{2,1,0:T(8,128)(2,1)S(1)}, s16[25,16,128]{2,1,0:T(8,128)(2,1)S(1)}, u32[]{:S(2)}, u32[]{:S(2)}) collective-permute-start(s16[25,16,128]{2,1,0:T(8,128)(2,1)S(1)} %get-tuple-element.33.refs_0_), channel_id=1, source_target_pairs={{0,8},{1,5},{2,10},{3,7},{4,12},{5,1},{6,14},{7,3},{8,0},{9,13},{1... | collective-permute-start | bytes 307208 | tf_op jit(solution)/shard_map/ppermute | solution.py:202
  23.1 9.2 %collective-permute-start.11 = (s16[25,16,128]{2,1,0:T(8,128)(2,1)S(1)}, s16[25,16,128]{2,1,0:T(8,128)(2,1)S(1)}, u32[]{:S(2)}, u32[]{:S(2)}) collective-permute-start(s16[25,16,128]{2,1,0:T(8,128)(2,1)S(1)} %cross_kernel.4.refs_0_.mine_ref), channel_id=1, source_target_pairs={{0,16},{1,17},{2,18},{3,19},{4,20},{5,21},{6,22},{7,23},{8,24},{9,... | collective-permute-start | bytes 307208 | tf_op jit(solution)/shard_map/ppermute | solution.py:202
  27.4 4.9 %collective-permute-start.10 = (s16[25,16,128]{2,1,0:T(8,128)(2,1)S(1)}, s16[25,16,128]{2,1,0:T(8,128)(2,1)S(1)}, u32[]{:S(2)}, u32[]{:S(2)}) collective-permute-start(s16[25,16,128]{2,1,0:T(8,128)(2,1)S(1)} %get-tuple-element.34.refs_0_), channel_id=1, source_target_pairs={{0,4},{1,9},{2,6},{3,11},{4,0},{5,13},{6,2},{7,15},{8,12},{9,1},{1... | collective-permute-start | bytes 307208 | tf_op jit(solution)/shard_map/ppermute | solution.py:202
  29.1 6.7 %collective-permute-start.9 = (s16[25,16,128]{2,1,0:T(8,128)(2,1)S(1)}, s16[25,16,128]{2,1,0:T(8,128)(2,1)S(1)}, u32[]{:S(2)}, u32[]{:S(2)}) collective-permute-start(s16[25,16,128]{2,1,0:T(8,128)(2,1)S(1)} %cross_kernel.5.refs_0_.mine_ref), channel_id=1, source_target_pairs={{0,8},{1,9},{2,10},{3,11},{4,12},{5,13},{6,14},{7,15},{8,0},{9,1},... | collective-permute-start | bytes 307208 | tf_op jit(solution)/shard_map/ppermute | solution.py:202
  29.8 10.1 %collective-permute-start.16 = (s16[25,16,128]{2,1,0:T(8,128)(2,1)S(1)}, s16[25,16,128]{2,1,0:T(8,128)(2,1)S(1)}, u32[]{:S(2)}, u32[]{:S(2)}) collective-permute-start(s16[25,16,128]{2,1,0:T(8,128)(2,1)S(1)} %cross_kernel.6.refs_0_.mine_ref), channel_id=1, source_target_pairs={{0,16},{1,17},{2,18},{3,19},{4,20},{5,21},{6,22},{7,23},{8,24},{9,... | collective-permute-start | bytes 307208 | tf_op jit(solution)/shard_map/ppermute | solution.py:202
  32.5 8.6 %collective-permute-start.14 = (s16[25,16,128]{2,1,0:T(8,128)(2,1)S(1)}, s16[25,16,128]{2,1,0:T(8,128)(2,1)S(1)}, u32[]{:S(2)}, u32[]{:S(2)}) collective-permute-start(s16[25,16,128]{2,1,0:T(8,128)(2,1)S(1)} %cross_kernel.7.refs_0_.mine_ref), channel_id=1, source_target_pairs={{0,8},{1,17},{2,10},{3,19},{4,12},{5,21},{6,14},{7,23},{8,0},{9,25... | collective-permute-start | bytes 307208 | tf_op jit(solution)/shard_map/ppermute | solution.py:202
  35.0 6.0 %collective-permute-start.15 = (bf16[2,12,16,128]{3,2,1,0:T(8,128)(2,1)S(1)}, bf16[2,12,16,128]{3,2,1,0:T(8,128)(2,1)S(1)}, u32[]{:S(2)}, u32[]{:S(2)}) collective-permute-start(bf16[2,12,16,128]{3,2,1,0:T(8,128)(2,1)S(1)} %final_kernel.4.refs_0_.mine_ref), channel_id=1, source_target_pairs={{0,8},{1,9},{2,10},{3,11},{4,12},{5,13},{6,14},{7,15},{8,0},{9,1},... | collective-permute-start | bytes 294920 | tf_op jit(solution)/shard_map/ppermute | solution.py:202
  35.9 8.6 %collective-permute-start.13 = (bf16[2,12,16,128]{3,2,1,0:T(8,128)(2,1)S(1)}, bf16[2,12,16,128]{3,2,1,0:T(8,128)(2,1)S(1)}, u32[]{:S(2)}, u32[]{:S(2)}) collective-permute-start(bf16[2,12,16,128]{3,2,1,0:T(8,128)(2,1)S(1)} %final_kernel.5.refs_0_.mine_ref), channel_id=1, source_target_pairs={{0,4},{1,17},{2,6},{3,19},{4,0},{5,21},{6,2},{7,23},{8,12},{9,25},... | collective-permute-start | bytes 294920 | tf_op jit(solution)/shard_map/ppermute | solution.py:202
  39.9 5.8 %collective-permute-start.18 = (bf16[2,12,16,128]{3,2,1,0:T(8,128)(2,1)S(1)}, bf16[2,12,16,128]{3,2,1,0:T(8,128)(2,1)S(1)}, u32[]{:S(2)}, u32[]{:S(2)}) collective-permute-start(bf16[2,12,16,128]{3,2,1,0:T(8,128)(2,1)S(1)} %final_kernel.6.refs_0_.mine_ref), channel_id=1, source_target_pairs={{0,4},{1,5},{2,6},{3,7},{4,0},{5,1},{6,2},{7,3},{8,12},{9,13},{10,... | collective-permute-start | bytes 294920 | tf_op jit(solution)/shard_map/ppermute | solution.py:202
  41.1 6.2 %collective-permute-start.20 = (bf16[2,12,16,128]{3,2,1,0:T(8,128)(2,1)S(1)}, bf16[2,12,16,128]{3,2,1,0:T(8,128)(2,1)S(1)}, u32[]{:S(2)}, u32[]{:S(2)}) collective-permute-start(bf16[2,12,16,128]{3,2,1,0:T(8,128)(2,1)S(1)} %final_kernel.7.refs_0_.mine_ref), channel_id=1, source_target_pairs={{0,16},{1,5},{2,18},{3,7},{4,20},{5,1},{6,22},{7,3},{8,24},{9,13},... | collective-permute-start | bytes 294920 | tf_op jit(solution)/shard_map/ppermute | solution.py:202
  43.0 5.9 %collective-permute-start.22 = (bf16[2,2,12,16,128]{4,3,2,1,0:T(8,128)(2,1)S(1)}, bf16[2,2,12,16,128]{4,3,2,1,0:T(8,128)(2,1)S(1)}, u32[]{:S(2)}, u32[]{:S(2)}) collective-permute-start(bf16[2,2,12,16,128]{4,3,2,1,0:T(8,128)(2,1)S(1)} %merge_kernel.4.refs_0_), channel_id=1, source_target_pairs={{0,4},{1,5},{2,6},{3,7},{4,0},{5,1},{6,2},{7,3},{8,12},{9,13},{10,... | collective-permute-start | bytes 589832 | tf_op jit(solution)/shard_map/ppermute | solution.py:202
  44.6 8.8 %collective-permute-start.17 = (bf16[2,2,12,16,128]{4,3,2,1,0:T(8,128)(2,1)S(1)}, bf16[2,2,12,16,128]{4,3,2,1,0:T(8,128)(2,1)S(1)}, u32[]{:S(2)}, u32[]{:S(2)}) collective-permute-start(bf16[2,2,12,16,128]{4,3,2,1,0:T(8,128)(2,1)S(1)} %merge_kernel.5.refs_0_.refs_1_), channel_id=1, source_target_pairs={{0,16},{1,5},{2,18},{3,7},{4,20},{5,1},{6,22},{7,3},{8,24},{9,13},... | collective-permute-start | bytes 589832 | tf_op jit(solution)/shard_map/ppermute | solution.py:202
  45.7 7.5 %collective-permute-start.19 = (bf16[2,2,12,16,128]{4,3,2,1,0:T(8,128)(2,1)S(1)}, bf16[2,2,12,16,128]{4,3,2,1,0:T(8,128)(2,1)S(1)}, u32[]{:S(2)}, u32[]{:S(2)}) collective-permute-start(bf16[2,2,12,16,128]{4,3,2,1,0:T(8,128)(2,1)S(1)} %merge_kernel.6.refs_0_.refs_2_), channel_id=1, source_target_pairs={{0,8},{1,9},{2,10},{3,11},{4,12},{5,13},{6,14},{7,15},{8,0},{9,1},... | collective-permute-start | bytes 589832 | tf_op jit(solution)/shard_map/ppermute | solution.py:202
  47.3 6.0 %collective-permute-start.21 = (bf16[2,2,12,16,128]{4,3,2,1,0:T(8,128)(2,1)S(1)}, bf16[2,2,12,16,128]{4,3,2,1,0:T(8,128)(2,1)S(1)}, u32[]{:S(2)}, u32[]{:S(2)}) collective-permute-start(bf16[2,2,12,16,128]{4,3,2,1,0:T(8,128)(2,1)S(1)} %merge_kernel.7.refs_3_), channel_id=1, source_target_pairs={{0,4},{1,9},{2,6},{3,11},{4,0},{5,13},{6,2},{7,15},{8,12},{9,1},{1... | collective-permute-start | bytes 589832 | tf_op jit(solution)/shard_map/ppermute | solution.py:202

commit v7 on v6

--- a/solution.py
+++ b/solution.py
@@ -8,7 +8,7 @@
 from jax.sharding import PartitionSpec as P
 
 BITS = {"y": 0, "z0": 1, "z1": 2}
-ORDERS = ((("y", "z0", "z1", "z0", "y"), ("z0", "y", "z1", "z0", "y")), (("y", "z1", "z0", "y", "z1"), ("z1", "y", "z0", "z1", "y")), (("y", "z0", "z1", "y", "z0"), ("z0", "y", "z1", "y", "z0")), (("z1", "y", "z0", "z1", "y"), ("y", "z0", "z1", "y", "z0")))
+ORDERS = ((("y", "z0", "z1", "y", "z0"), ("z0", "y", "z1", "z0", "y")), (("y", "z1", "z0", "y", "z1"), ("z1", "y", "z0", "z1", "y")), (("y", "z0", "z1", "y", "z0"), ("z0", "y", "z1", "z0", "y")), (("z1", "y", "z0", "z1", "y"), ("y", "z0", "z1", "y", "z0")))
 STEPS = (0, 1, 2, 0, 3, 1, 2, 0, 3, 1, 2, 0, 3, 1, 2, 3)
 PLACES = (((0, 0), (1, 0), (2, 0), (3, 0), (0, 1)), ((1, 1), (2, 1), (3, 1)))
 GROUP = 3

time: 55 us -> 55 us (level); the launches traced: 54.2 us -> 54.8 us
  transfers between devices with their start and end apart: 23 -> 23, of which waited for: 6 -> 5; matrix products, arithmetic and copies ran while one was open for 6% -> 6% of each run, Pallas kernels for 10% -> 10%
where the time goes in v7:
time: 55 us; the launch traced here: 54.8 us
  starting transfers between devices  36.2 us (66%)
  waiting for transfers between devices  8.32 us (15%)
  Pallas kernels  6.23 us (11%)
  other arithmetic  3.86 us (7%)
    ppermute x20, starting transfers between devices, swap(): return lax.ppermute(v, ('hist', 'col'), pairs)  32.6 us
    ppermute x20, waiting for transfers between devices, swap(): return lax.ppermute(v, ('hist', 'col'), pairs)  8.31 us
    pallas_call x20, Pallas kernels, call(): pl.pallas_call(kernel, out_shape=out_shape, in_specs=[vmem] * len(args),...  4.23 us
    ppermute x3, starting transfers between devices, swap_col(): return lax.ppermute(v, 'col', [(i, i ^ k) for i in range(n_col)])  3.58 us
    select_n x1, other arithmetic, staged(): jnp.where(after, green, zero)  2.17 us
    pallas_call x2, Pallas kernels, put(): pl.pallas_call(functools.partial(place_kernel, [(k, ORDERS[k], last) for...  2 us
  transfers between devices with their start and end apart: 23, of which 5 were waited for; matrix products, arithmetic and copies ran while one was open for 6% of the time, Pallas kernels for 10%

profile of v7, /device:TPU:0, one launch (start us, length us, event | category | flops | bytes accessed | tf_op | source)
XLA Modules:
  0.0 54.8 jit_solution(10336971409060056182)
XLA Ops:
  0.9 3.0 %collective-permute-start.3 = (bf16[2,4,4,16,128]{4,3,2,1,0:T(8,128)(2,1)S(1)}, bf16[2,4,4,16,128]{4,3,2,1,0:T(8,128)(2,1)S(1)}, u32[]{:S(2)}, u32[]{:S(2)}) collective-permute-start(bf16[2,4,4,16,128]{4,3,2,1,0:T(8,128)(2,1)S(1)} %pad_maximum_fusion.refs_0_), channel_id=1, source_target_pairs={{0,2},{1,3},{2,0},{3,1},{4,6},{5,7},{6,4},{7,5},{8,10},{9,11},{10,... | collective-permute-start | bytes 393224 | tf_op jit(solution)/shard_map/ppermute | solution.py:205
  4.6 2.2 %broadcast_select_fusion = (bf16[4,24,64,128]{3,2,1,0:T(8,128)(2,1)S(1)}, bf16[4,24,64,128]{3,2,1,0:T(8,128)(2,1)S(1)}) fusion(bf16[4,24,64,128]{3,2,1,0:T(8,128)(2,1)} %param.9, pred[4,24]{1,0:T(4,128)(4,1)S(1)} %broadcast_compare_fusion, bf16[4,24,64,128]{3,2,1,0:T(8,128)(2,1)} %param.8), kind=kLoop, calls=%fused_computation | loop fusion | flops 1572864 | bytes 6291552 | tf_op jit(solution)/shard_map/jit(_where)/select_n | solution.py:219
  7.0 1.4 %part_kernel.3 = (f32[1,2,2,12,16,128]{5,4,3,2,1,0:T(8,128)S(1)}, s16[49,16,128]{2,1,0:T(8,128)(2,1)S(1)}, f32[1,2,2,12,16,128]{5,4,3,2,1,0:T(8,128)S(1)}, s16[49,16,128]{2,1,0:T(8,128)(2,1)S(1)}) custom-call(bf16[4,4,16,128]{3,2,1,0:T(8,128)(2,1)S(1)} %broadcast_in_dim.27.keep_ref, bf16[2,4,4,16,128]{4,3,2,1,0:T(8,128)(2,1)S(1)} %pad_maximum_fusion.refs_0_, ...), custom_call_target="tpu_custom_call" | custom-call | flops 805306368 | bytes 3145728 | tf_op jit(solution)/shard_map/part_kernel/pallas_call | solution.py:226
  9.0 1.5 %collective-permute-start.2 = (s16[49,16,128]{2,1,0:T(8,128)(2,1)S(1)}, s16[49,16,128]{2,1,0:T(8,128)(2,1)S(1)}, u32[]{:S(2)}, u32[]{:S(2)}) collective-permute-start(s16[49,16,128]{2,1,0:T(8,128)(2,1)S(1)} %get-tuple-element.24), channel_id=1, source_target_pairs={{0,4},{1,9},{2,6},{3,11},{4,0},{5,13},{6,2},{7,15},{8,12},{9,1},{1... | collective-permute-start | bytes 602120 | tf_op jit(solution)/shard_map/ppermute | solution.py:202
  11.9 1.6 %collective-permute-start.8 = (s16[49,16,128]{2,1,0:T(8,128)(2,1)S(1)}, s16[49,16,128]{2,1,0:T(8,128)(2,1)S(1)}, u32[]{:S(2)}, u32[]{:S(2)}) collective-permute-start(s16[49,16,128]{2,1,0:T(8,128)(2,1)S(1)} %get-tuple-element.25.refs_3_), channel_id=1, source_target_pairs={{0,4},{1,9},{2,6},{3,11},{4,0},{5,13},{6,2},{7,15},{8,12},{9,1},{1... | collective-permute-start | bytes 602120 | tf_op jit(solution)/shard_map/ppermute | solution.py:202
  14.3 2.6 %collective-permute-start.6 = (s16[49,16,128]{2,1,0:T(8,128)(2,1)S(1)}, s16[49,16,128]{2,1,0:T(8,128)(2,1)S(1)}, u32[]{:S(2)}, u32[]{:S(2)}) collective-permute-start(s16[49,16,128]{2,1,0:T(8,128)(2,1)S(1)} %get-tuple-element.26.refs_0_), channel_id=1, source_target_pairs={{0,16},{1,5},{2,18},{3,7},{4,20},{5,1},{6,22},{7,3},{8,24},{9,13},... | collective-permute-start | bytes 602120 | tf_op jit(solution)/shard_map/ppermute | solution.py:202
  17.1 1.6 %collective-permute-start.7 = (s16[25,16,128]{2,1,0:T(8,128)(2,1)S(1)}, s16[25,16,128]{2,1,0:T(8,128)(2,1)S(1)}, u32[]{:S(2)}, u32[]{:S(2)}) collective-permute-start(s16[25,16,128]{2,1,0:T(8,128)(2,1)S(1)} %get-tuple-element.27.refs_0_), channel_id=1, source_target_pairs={{0,8},{1,5},{2,10},{3,7},{4,12},{5,1},{6,14},{7,3},{8,0},{9,13},{1... | collective-permute-start | bytes 307208 | tf_op jit(solution)/shard_map/ppermute | solution.py:202
  18.9 2.4 %collective-permute-start.5 = (s16[25,16,128]{2,1,0:T(8,128)(2,1)S(1)}, s16[25,16,128]{2,1,0:T(8,128)(2,1)S(1)}, u32[]{:S(2)}, u32[]{:S(2)}) collective-permute-start(s16[25,16,128]{2,1,0:T(8,128)(2,1)S(1)} %get-tuple-element.29.refs_0_), channel_id=1, source_target_pairs={{0,16},{1,5},{2,18},{3,7},{4,20},{5,1},{6,22},{7,3},{8,24},{9,13},... | collective-permute-start | bytes 307208 | tf_op jit(solution)/shard_map/ppermute | solution.py:202
  21.4 1.6 %collective-permute-start.12 = (s16[25,16,128]{2,1,0:T(8,128)(2,1)S(1)}, s16[25,16,128]{2,1,0:T(8,128)(2,1)S(1)}, u32[]{:S(2)}, u32[]{:S(2)}) collective-permute-start(s16[25,16,128]{2,1,0:T(8,128)(2,1)S(1)} %get-tuple-element.33.refs_0_), channel_id=1, source_target_pairs={{0,8},{1,5},{2,10},{3,7},{4,12},{5,1},{6,14},{7,3},{8,0},{9,13},{1... | collective-permute-start | bytes 307208 | tf_op jit(solution)/shard_map/ppermute | solution.py:202
  23.1 4.2 %collective-permute-start.11 = (s16[25,16,128]{2,1,0:T(8,128)(2,1)S(1)}, s16[25,16,128]{2,1,0:T(8,128)(2,1)S(1)}, u32[]{:S(2)}, u32[]{:S(2)}) collective-permute-start(s16[25,16,128]{2,1,0:T(8,128)(2,1)S(1)} %cross_kernel.4.refs_0_.mine_ref), channel_id=1, source_target_pairs={{0,16},{1,17},{2,18},{3,19},{4,20},{5,21},{6,22},{7,23},{8,24},{9,... | collective-permute-start | bytes 307208 | tf_op jit(solution)/shard_map/ppermute | solution.py:202
  27.4 1.6 %collective-permute-start.10 = (s16[25,16,128]{2,1,0:T(8,128)(2,1)S(1)}, s16[25,16,128]{2,1,0:T(8,128)(2,1)S(1)}, u32[]{:S(2)}, u32[]{:S(2)}) collective-permute-start(s16[25,16,128]{2,1,0:T(8,128)(2,1)S(1)} %get-tuple-element.34.refs_0_), channel_id=1, source_target_pairs={{0,4},{1,9},{2,6},{3,11},{4,0},{5,13},{6,2},{7,15},{8,12},{9,1},{1... | collective-permute-start | bytes 307208 | tf_op jit(solution)/shard_map/ppermute | solution.py:202
  29.8 2.6 %collective-permute-start.16 = (s16[25,16,128]{2,1,0:T(8,128)(2,1)S(1)}, s16[25,16,128]{2,1,0:T(8,128)(2,1)S(1)}, u32[]{:S(2)}, u32[]{:S(2)}) collective-permute-start(s16[25,16,128]{2,1,0:T(8,128)(2,1)S(1)} %cross_kernel.6.refs_0_.mine_ref), channel_id=1, source_target_pairs={{0,16},{1,17},{2,18},{3,19},{4,20},{5,21},{6,22},{7,23},{8,24},{9,... | collective-permute-start | bytes 307208 | tf_op jit(solution)/shard_map/ppermute | solution.py:202
  32.5 2.5 %collective-permute-start.14 = (s16[25,16,128]{2,1,0:T(8,128)(2,1)S(1)}, s16[25,16,128]{2,1,0:T(8,128)(2,1)S(1)}, u32[]{:S(2)}, u32[]{:S(2)}) collective-permute-start(s16[25,16,128]{2,1,0:T(8,128)(2,1)S(1)} %cross_kernel.7.refs_0_.mine_ref), channel_id=1, source_target_pairs={{0,8},{1,17},{2,10},{3,19},{4,12},{5,21},{6,14},{7,23},{8,0},{9,25... | collective-permute-start | bytes 307208 | tf_op jit(solution)/shard_map/ppermute | solution.py:202
  35.0 1.6 %collective-permute-start.15 = (bf16[2,12,16,128]{3,2,1,0:T(8,128)(2,1)S(1)}, bf16[2,12,16,128]{3,2,1,0:T(8,128)(2,1)S(1)}, u32[]{:S(2)}, u32[]{:S(2)}) collective-permute-start(bf16[2,12,16,128]{3,2,1,0:T(8,128)(2,1)S(1)} %final_kernel.4.refs_0_.mine_ref), channel_id=1, source_target_pairs={{0,4},{1,9},{2,6},{3,11},{4,0},{5,13},{6,2},{7,15},{8,12},{9,1},{1... | collective-permute-start | bytes 294920 | tf_op jit(solution)/shard_map/ppermute | solution.py:202
  37.2 2.7 %collective-permute-done.16.other_ref = s16[25,16,128]{2,1,0:T(8,128)(2,1)S(1)} collective-permute-done((s16[25,16,128]{2,1,0:T(8,128)(2,1)S(1)}, s16[25,16,128]{2,1,0:T(8,128)(2,1)S(1)}, u32[]{:S(2)}, u32[]{:S(2)}) %collective-permute-start.16) | collective-permute-done | bytes 102432 | tf_op jit(solution)/shard_map/ppermute | solution.py:202
  39.9 1.1 %collective-permute-start.18 = (bf16[2,12,16,128]{3,2,1,0:T(8,128)(2,1)S(1)}, bf16[2,12,16,128]{3,2,1,0:T(8,128)(2,1)S(1)}, u32[]{:S(2)}, u32[]{:S(2)}) collective-permute-start(bf16[2,12,16,128]{3,2,1,0:T(8,128)(2,1)S(1)} %final_kernel.6.refs_0_.mine_ref), channel_id=1, source_target_pairs={{0,4},{1,9},{2,6},{3,11},{4,0},{5,13},{6,2},{7,15},{8,12},{9,1},{1... | collective-permute-start | bytes 294920 | tf_op jit(solution)/shard_map/ppermute | solution.py:202
  41.1 2.5 %collective-permute-start.20 = (bf16[2,12,16,128]{3,2,1,0:T(8,128)(2,1)S(1)}, bf16[2,12,16,128]{3,2,1,0:T(8,128)(2,1)S(1)}, u32[]{:S(2)}, u32[]{:S(2)}) collective-permute-start(bf16[2,12,16,128]{3,2,1,0:T(8,128)(2,1)S(1)} %final_kernel.7.refs_0_.mine_ref), channel_id=1, source_target_pairs={{0,16},{1,5},{2,18},{3,7},{4,20},{5,1},{6,22},{7,3},{8,24},{9,13},... | collective-permute-start | bytes 294920 | tf_op jit(solution)/shard_map/ppermute | solution.py:202
  43.6 1.5 %collective-permute-start.22 = (bf16[2,2,12,16,128]{4,3,2,1,0:T(8,128)(2,1)S(1)}, bf16[2,2,12,16,128]{4,3,2,1,0:T(8,128)(2,1)S(1)}, u32[]{:S(2)}, u32[]{:S(2)}) collective-permute-start(bf16[2,2,12,16,128]{4,3,2,1,0:T(8,128)(2,1)S(1)} %merge_kernel.4.refs_0_), channel_id=1, source_target_pairs={{0,8},{1,5},{2,10},{3,7},{4,12},{5,1},{6,14},{7,3},{8,0},{9,13},{1... | collective-permute-start | bytes 589832 | tf_op jit(solution)/shard_map/ppermute | solution.py:202
  46.3 1.1 %collective-permute-done.20.other_ref = bf16[2,12,16,128]{3,2,1,0:T(8,128)(2,1)S(1)} collective-permute-done((bf16[2,12,16,128]{3,2,1,0:T(8,128)(2,1)S(1)}, bf16[2,12,16,128]{3,2,1,0:T(8,128)(2,1)S(1)}, u32[]{:S(2)}, u32[]{:S(2)}) %collective-permute-start.20) | collective-permute-done | bytes 98336 | tf_op jit(solution)/shard_map/ppermute | solution.py:202
  47.4 0.9 %collective-permute-start.21 = (bf16[2,2,12,16,128]{4,3,2,1,0:T(8,128)(2,1)S(1)}, bf16[2,2,12,16,128]{4,3,2,1,0:T(8,128)(2,1)S(1)}, u32[]{:S(2)}, u32[]{:S(2)}) collective-permute-start(bf16[2,2,12,16,128]{4,3,2,1,0:T(8,128)(2,1)S(1)} %merge_kernel.7.refs_3_), channel_id=1, source_target_pairs={{0,4},{1,9},{2,6},{3,11},{4,0},{5,13},{6,2},{7,15},{8,12},{9,1},{1... | collective-permute-start | bytes 589832 | tf_op jit(solution)/shard_map/ppermute | solution.py:202
  48.3 1.3 %collective-permute-done.22.refs_4_ = bf16[2,2,12,16,128]{4,3,2,1,0:T(8,128)(2,1)S(1)} collective-permute-done((bf16[2,2,12,16,128]{4,3,2,1,0:T(8,128)(2,1)S(1)}, bf16[2,2,12,16,128]{4,3,2,1,0:T(8,128)(2,1)S(1)}, u32[]{:S(2)}, u32[]{:S(2)}) %collective-permute-start.22) | collective-permute-done | bytes 196640 | tf_op jit(solution)/shard_map/ppermute | solution.py:202
  49.6 1.1 %place_part.2.refs_3_ = bf16[4,24,64,128]{3,2,1,0:T(8,128)(2,1)} custom-call(bf16[2,2,12,16,128]{4,3,2,1,0:T(8,128)(2,1)S(1)} %merge_kernel.4.refs_0_, bf16[2,2,12,16,128]{4,3,2,1,0:T(8,128)(2,1)S(1)} %merge_kernel.5.refs_0_.refs_1_, bf16[2,2,12,16,128]{4,3,2,1,0:T(8,128)(2,1)S(1)} %merge_kernel.6.refs_0_.refs_2_, ...), custom_call_target="tpu_custom_call" | custom-call | tf_op jit(solution)/shard_map/place_part/pallas_call | solution.py:280
  50.7 2.3 %collective-permute-done.19.refs_1_ = bf16[2,2,12,16,128]{4,3,2,1,0:T(8,128)(2,1)S(1)} collective-permute-done((bf16[2,2,12,16,128]{4,3,2,1,0:T(8,128)(2,1)S(1)}, bf16[2,2,12,16,128]{4,3,2,1,0:T(8,128)(2,1)S(1)}, u32[]{:S(2)}, u32[]{:S(2)}) %collective-permute-start.19) | collective-permute-done | bytes 196640 | tf_op jit(solution)/shard_map/ppermute | solution.py:202
  53.0 0.9 %collective-permute-done.17.refs_0_ = bf16[2,2,12,16,128]{4,3,2,1,0:T(8,128)(2,1)S(1)} collective-permute-done((bf16[2,2,12,16,128]{4,3,2,1,0:T(8,128)(2,1)S(1)}, bf16[2,2,12,16,128]{4,3,2,1,0:T(8,128)(2,1)S(1)}, u32[]{:S(2)}, u32[]{:S(2)}) %collective-permute-start.17) | collective-permute-done | bytes 196640 | tf_op jit(solution)/shard_map/ppermute | solution.py:202
  (52 shorter events, 8.9 us)
Async XLA Ops:
  0.9 7.5 %collective-permute-start.3 = (bf16[2,4,4,16,128]{4,3,2,1,0:T(8,128)(2,1)S(1)}, bf16[2,4,4,16,128]{4,3,2,1,0:T(8,128)(2,1)S(1)}, u32[]{:S(2)}, u32[]{:S(2)}) collective-permute-start(bf16[2,4,4,16,128]{4,3,2,1,0:T(8,128)(2,1)S(1)} %pad_maximum_fusion.refs_0_), channel_id=1, source_target_pairs={{0,2},{1,3},{2,0},{3,1},{4,6},{5,7},{6,4},{7,5},{8,10},{9,11},{10,... | collective-permute-start | bytes 393224 | tf_op jit(solution)/shard_map/ppermute | solution.py:205
  3.9 3.0 %collective-permute-start = (bf16[2,4,4,16,128]{4,3,2,1,0:T(8,128)(2,1)S(1)}, bf16[2,4,4,16,128]{4,3,2,1,0:T(8,128)(2,1)S(1)}, u32[]{:S(2)}, u32[]{:S(2)}) collective-permute-start(bf16[2,4,4,16,128]{4,3,2,1,0:T(8,128)(2,1)S(1)} %pad_maximum_fusion.refs_0_), channel_id=1, source_target_pairs={{0,1},{1,0},{2,3},{3,2},{4,5},{5,4},{6,7},{7,6},{8,9},{9,8},{10,11... | collective-permute-start | bytes 393224 | tf_op jit(solution)/shard_map/ppermute | solution.py:205
  4.6 2.2 %copy-start = (s32[4]{0:T(128)S(1)}, s32[4]{0:T(128)}, u32[]{:S(2)}) copy-start(s32[4]{0:T(128)} %param.10) | copy-start | bytes 52
  8.4 5.1 %collective-permute-start.4 = (bf16[2,4,4,16,128]{4,3,2,1,0:T(8,128)(2,1)S(1)}, bf16[2,4,4,16,128]{4,3,2,1,0:T(8,128)(2,1)S(1)}, u32[]{:S(2)}, u32[]{:S(2)}) collective-permute-start(bf16[2,4,4,16,128]{4,3,2,1,0:T(8,128)(2,1)S(1)} %copy_kernel.1.refs_3_), channel_id=1, source_target_pairs={{0,1},{1,0},{2,3},{3,2},{4,5},{5,4},{6,7},{7,6},{8,9},{9,8},{10,11... | collective-permute-start | bytes 393224 | tf_op jit(solution)/shard_map/ppermute | solution.py:205
  9.0 8.0 %collective-permute-start.2 = (s16[49,16,128]{2,1,0:T(8,128)(2,1)S(1)}, s16[49,16,128]{2,1,0:T(8,128)(2,1)S(1)}, u32[]{:S(2)}, u32[]{:S(2)}) collective-permute-start(s16[49,16,128]{2,1,0:T(8,128)(2,1)S(1)} %get-tuple-element.24), channel_id=1, source_target_pairs={{0,4},{1,9},{2,6},{3,11},{4,0},{5,13},{6,2},{7,15},{8,12},{9,1},{1... | collective-permute-start | bytes 602120 | tf_op jit(solution)/shard_map/ppermute | solution.py:202
  10.5 8.3 %collective-permute-start.1 = (s16[49,16,128]{2,1,0:T(8,128)(2,1)S(1)}, s16[49,16,128]{2,1,0:T(8,128)(2,1)S(1)}, u32[]{:S(2)}, u32[]{:S(2)}) collective-permute-start(s16[49,16,128]{2,1,0:T(8,128)(2,1)S(1)} %get-tuple-element.22.refs_0_), channel_id=1, source_target_pairs={{0,4},{1,17},{2,6},{3,19},{4,0},{5,21},{6,2},{7,23},{8,12},{9,25},... | collective-permute-start | bytes 602120 | tf_op jit(solution)/shard_map/ppermute | solution.py:202
  11.9 9.4 %collective-permute-start.8 = (s16[49,16,128]{2,1,0:T(8,128)(2,1)S(1)}, s16[49,16,128]{2,1,0:T(8,128)(2,1)S(1)}, u32[]{:S(2)}, u32[]{:S(2)}) collective-permute-start(s16[49,16,128]{2,1,0:T(8,128)(2,1)S(1)} %get-tuple-element.25.refs_3_), channel_id=1, source_target_pairs={{0,4},{1,9},{2,6},{3,11},{4,0},{5,13},{6,2},{7,15},{8,12},{9,1},{1... | collective-permute-start | bytes 602120 | tf_op jit(solution)/shard_map/ppermute | solution.py:202
  14.3 13.0 %collective-permute-start.6 = (s16[49,16,128]{2,1,0:T(8,128)(2,1)S(1)}, s16[49,16,128]{2,1,0:T(8,128)(2,1)S(1)}, u32[]{:S(2)}, u32[]{:S(2)}) collective-permute-start(s16[49,16,128]{2,1,0:T(8,128)(2,1)S(1)} %get-tuple-element.26.refs_0_), channel_id=1, source_target_pairs={{0,16},{1,5},{2,18},{3,7},{4,20},{5,1},{6,22},{7,3},{8,24},{9,13},... | collective-permute-start | bytes 602120 | tf_op jit(solution)/shard_map/ppermute | solution.py:202
  17.1 5.9 %collective-permute-start.7 = (s16[25,16,128]{2,1,0:T(8,128)(2,1)S(1)}, s16[25,16,128]{2,1,0:T(8,128)(2,1)S(1)}, u32[]{:S(2)}, u32[]{:S(2)}) collective-permute-start(s16[25,16,128]{2,1,0:T(8,128)(2,1)S(1)} %get-tuple-element.27.refs_0_), channel_id=1, source_target_pairs={{0,8},{1,5},{2,10},{3,7},{4,12},{5,1},{6,14},{7,3},{8,0},{9,13},{1... | collective-permute-start | bytes 307208 | tf_op jit(solution)/shard_map/ppermute | solution.py:202
  18.9 10.2 %collective-permute-start.5 = (s16[25,16,128]{2,1,0:T(8,128)(2,1)S(1)}, s16[25,16,128]{2,1,0:T(8,128)(2,1)S(1)}, u32[]{:S(2)}, u32[]{:S(2)}) collective-permute-start(s16[25,16,128]{2,1,0:T(8,128)(2,1)S(1)} %get-tuple-element.29.refs_0_), channel_id=1, source_target_pairs={{0,16},{1,5},{2,18},{3,7},{4,20},{5,1},{6,22},{7,3},{8,24},{9,13},... | collective-permute-start | bytes 307208 | tf_op jit(solution)/shard_map/ppermute | solution.py:202
  21.4 8.2 %collective-permute-start.12 = (s16[25,16,128]{2,1,0:T(8,128)(2,1)S(1)}, s16[25,16,128]{2,1,0:T(8,128)(2,1)S(1)}, u32[]{:S(2)}, u32[]{:S(2)}) collective-permute-start(s16[25,16,128]{2,1,0:T(8,128)(2,1)S(1)} %get-tuple-element.33.refs_0_), channel_id=1, source_target_pairs={{0,8},{1,5},{2,10},{3,7},{4,12},{5,1},{6,14},{7,3},{8,0},{9,13},{1... | collective-permute-start | bytes 307208 | tf_op jit(solution)/shard_map/ppermute | solution.py:202
  23.1 9.2 %collective-permute-start.11 = (s16[25,16,128]{2,1,0:T(8,128)(2,1)S(1)}, s16[25,16,128]{2,1,0:T(8,128)(2,1)S(1)}, u32[]{:S(2)}, u32[]{:S(2)}) collective-permute-start(s16[25,16,128]{2,1,0:T(8,128)(2,1)S(1)} %cross_kernel.4.refs_0_.mine_ref), channel_id=1, source_target_pairs={{0,16},{1,17},{2,18},{3,19},{4,20},{5,21},{6,22},{7,23},{8,24},{9,... | collective-permute-start | bytes 307208 | tf_op jit(solution)/shard_map/ppermute | solution.py:202
  27.4 4.9 %collective-permute-start.10 = (s16[25,16,128]{2,1,0:T(8,128)(2,1)S(1)}, s16[25,16,128]{2,1,0:T(8,128)(2,1)S(1)}, u32[]{:S(2)}, u32[]{:S(2)}) collective-permute-start(s16[25,16,128]{2,1,0:T(8,128)(2,1)S(1)} %get-tuple-element.34.refs_0_), channel_id=1, source_target_pairs={{0,4},{1,9},{2,6},{3,11},{4,0},{5,13},{6,2},{7,15},{8,12},{9,1},{1... | collective-permute-start | bytes 307208 | tf_op jit(solution)/shard_map/ppermute | solution.py:202
  29.1 7.5 %collective-permute-start.9 = (s16[25,16,128]{2,1,0:T(8,128)(2,1)S(1)}, s16[25,16,128]{2,1,0:T(8,128)(2,1)S(1)}, u32[]{:S(2)}, u32[]{:S(2)}) collective-permute-start(s16[25,16,128]{2,1,0:T(8,128)(2,1)S(1)} %cross_kernel.5.refs_0_.mine_ref), channel_id=1, source_target_pairs={{0,8},{1,9},{2,10},{3,11},{4,12},{5,13},{6,14},{7,15},{8,0},{9,1},... | collective-permute-start | bytes 307208 | tf_op jit(solution)/shard_map/ppermute | solution.py:202
  29.8 10.1 %collective-permute-start.16 = (s16[25,16,128]{2,1,0:T(8,128)(2,1)S(1)}, s16[25,16,128]{2,1,0:T(8,128)(2,1)S(1)}, u32[]{:S(2)}, u32[]{:S(2)}) collective-permute-start(s16[25,16,128]{2,1,0:T(8,128)(2,1)S(1)} %cross_kernel.6.refs_0_.mine_ref), channel_id=1, source_target_pairs={{0,16},{1,17},{2,18},{3,19},{4,20},{5,21},{6,22},{7,23},{8,24},{9,... | collective-permute-start | bytes 307208 | tf_op jit(solution)/shard_map/ppermute | solution.py:202
  32.5 8.6 %collective-permute-start.14 = (s16[25,16,128]{2,1,0:T(8,128)(2,1)S(1)}, s16[25,16,128]{2,1,0:T(8,128)(2,1)S(1)}, u32[]{:S(2)}, u32[]{:S(2)}) collective-permute-start(s16[25,16,128]{2,1,0:T(8,128)(2,1)S(1)} %cross_kernel.7.refs_0_.mine_ref), channel_id=1, source_target_pairs={{0,8},{1,17},{2,10},{3,19},{4,12},{5,21},{6,14},{7,23},{8,0},{9,25... | collective-permute-start | bytes 307208 | tf_op jit(solution)/shard_map/ppermute | solution.py:202
  35.0 6.0 %collective-permute-start.15 = (bf16[2,12,16,128]{3,2,1,0:T(8,128)(2,1)S(1)}, bf16[2,12,16,128]{3,2,1,0:T(8,128)(2,1)S(1)}, u32[]{:S(2)}, u32[]{:S(2)}) collective-permute-start(bf16[2,12,16,128]{3,2,1,0:T(8,128)(2,1)S(1)} %final_kernel.4.refs_0_.mine_ref), channel_id=1, source_target_pairs={{0,4},{1,9},{2,6},{3,11},{4,0},{5,13},{6,2},{7,15},{8,12},{9,1},{1... | collective-permute-start | bytes 294920 | tf_op jit(solution)/shard_map/ppermute | solution.py:202
  36.7 8.5 %collective-permute-start.13 = (bf16[2,12,16,128]{3,2,1,0:T(8,128)(2,1)S(1)}, bf16[2,12,16,128]{3,2,1,0:T(8,128)(2,1)S(1)}, u32[]{:S(2)}, u32[]{:S(2)}) collective-permute-start(bf16[2,12,16,128]{3,2,1,0:T(8,128)(2,1)S(1)} %final_kernel.5.refs_0_.mine_ref), channel_id=1, source_target_pairs={{0,4},{1,17},{2,6},{3,19},{4,0},{5,21},{6,2},{7,23},{8,12},{9,25},... | collective-permute-start | bytes 294920 | tf_op jit(solution)/shard_map/ppermute | solution.py:202
  39.9 5.8 %collective-permute-start.18 = (bf16[2,12,16,128]{3,2,1,0:T(8,128)(2,1)S(1)}, bf16[2,12,16,128]{3,2,1,0:T(8,128)(2,1)S(1)}, u32[]{:S(2)}, u32[]{:S(2)}) collective-permute-start(bf16[2,12,16,128]{3,2,1,0:T(8,128)(2,1)S(1)} %final_kernel.6.refs_0_.mine_ref), channel_id=1, source_target_pairs={{0,4},{1,9},{2,6},{3,11},{4,0},{5,13},{6,2},{7,15},{8,12},{9,1},{1... | collective-permute-start | bytes 294920 | tf_op jit(solution)/shard_map/ppermute | solution.py:202
  41.1 6.2 %collective-permute-start.20 = (bf16[2,12,16,128]{3,2,1,0:T(8,128)(2,1)S(1)}, bf16[2,12,16,128]{3,2,1,0:T(8,128)(2,1)S(1)}, u32[]{:S(2)}, u32[]{:S(2)}) collective-permute-start(bf16[2,12,16,128]{3,2,1,0:T(8,128)(2,1)S(1)} %final_kernel.7.refs_0_.mine_ref), channel_id=1, source_target_pairs={{0,16},{1,5},{2,18},{3,7},{4,20},{5,1},{6,22},{7,3},{8,24},{9,13},... | collective-permute-start | bytes 294920 | tf_op jit(solution)/shard_map/ppermute | solution.py:202
  43.6 6.0 %collective-permute-start.22 = (bf16[2,2,12,16,128]{4,3,2,1,0:T(8,128)(2,1)S(1)}, bf16[2,2,12,16,128]{4,3,2,1,0:T(8,128)(2,1)S(1)}, u32[]{:S(2)}, u32[]{:S(2)}) collective-permute-start(bf16[2,2,12,16,128]{4,3,2,1,0:T(8,128)(2,1)S(1)} %merge_kernel.4.refs_0_), channel_id=1, source_target_pairs={{0,8},{1,5},{2,10},{3,7},{4,12},{5,1},{6,14},{7,3},{8,0},{9,13},{1... | collective-permute-start | bytes 589832 | tf_op jit(solution)/shard_map/ppermute | solution.py:202
  45.1 8.8 %collective-permute-start.17 = (bf16[2,2,12,16,128]{4,3,2,1,0:T(8,128)(2,1)S(1)}, bf16[2,2,12,16,128]{4,3,2,1,0:T(8,128)(2,1)S(1)}, u32[]{:S(2)}, u32[]{:S(2)}) collective-permute-start(bf16[2,2,12,16,128]{4,3,2,1,0:T(8,128)(2,1)S(1)} %merge_kernel.5.refs_0_.refs_1_), channel_id=1, source_target_pairs={{0,16},{1,5},{2,18},{3,7},{4,20},{5,1},{6,22},{7,3},{8,24},{9,13},... | collective-permute-start | bytes 589832 | tf_op jit(solution)/shard_map/ppermute | solution.py:202
  45.7 7.3 %collective-permute-start.19 = (bf16[2,2,12,16,128]{4,3,2,1,0:T(8,128)(2,1)S(1)}, bf16[2,2,12,16,128]{4,3,2,1,0:T(8,128)(2,1)S(1)}, u32[]{:S(2)}, u32[]{:S(2)}) collective-permute-start(bf16[2,2,12,16,128]{4,3,2,1,0:T(8,128)(2,1)S(1)} %merge_kernel.6.refs_0_.refs_2_), channel_id=1, source_target_pairs={{0,8},{1,5},{2,10},{3,7},{4,12},{5,1},{6,14},{7,3},{8,0},{9,13},{1... | collective-permute-start | bytes 589832 | tf_op jit(solution)/shard_map/ppermute | solution.py:202
  47.4 6.5 %collective-permute-start.21 = (bf16[2,2,12,16,128]{4,3,2,1,0:T(8,128)(2,1)S(1)}, bf16[2,2,12,16,128]{4,3,2,1,0:T(8,128)(2,1)S(1)}, u32[]{:S(2)}, u32[]{:S(2)}) collective-permute-start(bf16[2,2,12,16,128]{4,3,2,1,0:T(8,128)(2,1)S(1)} %merge_kernel.7.refs_3_), channel_id=1, source_target_pairs={{0,4},{1,9},{2,6},{3,11},{4,0},{5,13},{6,2},{7,15},{8,12},{9,1},{1... | collective-permute-start | bytes 589832 | tf_op jit(solution)/shard_map/ppermute | solution.py:202

commit v8 on v5

--- a/solution.py
+++ b/solution.py
@@ -9,7 +9,7 @@
 
 BITS = {"y": 0, "z0": 1, "z1": 2}
 ORDERS = ((("y", "z0", "z1", "z0", "y"), ("z0", "y", "z1", "z0", "y")), (("y", "z1", "z0", "y", "z1"), ("z1", "y", "z0", "z1", "y")), (("y", "z0", "z1", "y", "z0"), ("z0", "y", "z1", "z0", "y")), (("z1", "y", "z0", "z1", "y"), ("y", "z0", "z1", "y", "z0")))
-STEPS = (0, 1, 2, 0, 3, 1, 2, 0, 3, 1, 2, 0, 3, 1, 2, 3)
+STEPS = (0, 1, 2, 0, 3, 1, 2, 3, 0, 1, 2, 3, 0, 1, 2, 3)
 PLACES = (((0, 0), (1, 0), (2, 0), (3, 0), (0, 1)), ((1, 1), (2, 1), (3, 1)))
 GROUP = 3
 STEPS_PER_OCTAVE = 128.0

time: 54.8 us -> 55.5 us (1.013)
  waiting for transfers between devices: 8.39 us -> 12.6 us
  starting transfers between devices: 35.8 us -> 32.5 us
    ppermute x20, waiting for transfers between devices: 8.38 us -> 12.5 us  [swap(): return lax.ppermute(v, ('hist', 'col'), pairs)]
    ppermute x20, starting transfers between devices: 32.2 us -> 28.9 us  [swap(): return lax.ppermute(v, ('hist', 'col'), pairs)]
  transfers between devices with their start and end apart: 23 -> 23, of which waited for: 6 -> 9; matrix products, arithmetic and copies ran while one was open for 6% -> 6% of each run, Pallas kernels for 10% -> 10%
where the time goes in v8:
time: 55.5 us; the launch traced here: 55.4 us
  starting transfers between devices  32.5 us (59%)
  waiting for transfers between devices  12.6 us (23%)
  Pallas kernels  6.23 us (11%)
  other arithmetic  3.86 us (7%)
    ppermute x20, starting transfers between devices, swap(): return lax.ppermute(v, ('hist', 'col'), pairs)  28.9 us
    ppermute x20, waiting for transfers between devices, swap(): return lax.ppermute(v, ('hist', 'col'), pairs)  12.5 us
    pallas_call x20, Pallas kernels, call(): pl.pallas_call(kernel, out_shape=out_shape, in_specs=[vmem] * len(args),...  4.23 us
    ppermute x3, starting transfers between devices, swap_col(): return lax.ppermute(v, 'col', [(i, i ^ k) for i in range(n_col)])  3.58 us
    select_n x1, other arithmetic, staged(): jnp.where(after, green, zero)  2.17 us
    pallas_call x2, Pallas kernels, put(): pl.pallas_call(functools.partial(place_kernel, [(k, ORDERS[k], last) for...  2 us
  transfers between devices with their start and end apart: 23, of which 9 were waited for; matrix products, arithmetic and copies ran while one was open for 6% of the time, Pallas kernels for 10%

profile of v8, /device:TPU:0, one launch (start us, length us, event | category | flops | bytes accessed | tf_op | source)
XLA Modules:
  0.0 55.4 jit_solution(16762752280468462991)
XLA Ops:
  0.9 3.0 %collective-permute-start.3 = (bf16[2,4,4,16,128]{4,3,2,1,0:T(8,128)(2,1)S(1)}, bf16[2,4,4,16,128]{4,3,2,1,0:T(8,128)(2,1)S(1)}, u32[]{:S(2)}, u32[]{:S(2)}) collective-permute-start(bf16[2,4,4,16,128]{4,3,2,1,0:T(8,128)(2,1)S(1)} %pad_maximum_fusion.refs_0_), channel_id=1, source_target_pairs={{0,2},{1,3},{2,0},{3,1},{4,6},{5,7},{6,4},{7,5},{8,10},{9,11},{10,... | collective-permute-start | bytes 393224 | tf_op jit(solution)/shard_map/ppermute | solution.py:205
  4.6 2.2 %broadcast_select_fusion = (bf16[4,24,64,128]{3,2,1,0:T(8,128)(2,1)S(1)}, bf16[4,24,64,128]{3,2,1,0:T(8,128)(2,1)S(1)}) fusion(bf16[4,24,64,128]{3,2,1,0:T(8,128)(2,1)} %param.9, pred[4,24]{1,0:T(4,128)(4,1)S(1)} %broadcast_compare_fusion, bf16[4,24,64,128]{3,2,1,0:T(8,128)(2,1)} %param.8), kind=kLoop, calls=%fused_computation | loop fusion | flops 1572864 | bytes 6291552 | tf_op jit(solution)/shard_map/jit(_where)/select_n | solution.py:219
  7.0 1.4 %part_kernel.3 = (f32[1,2,2,12,16,128]{5,4,3,2,1,0:T(8,128)S(1)}, s16[49,16,128]{2,1,0:T(8,128)(2,1)S(1)}, f32[1,2,2,12,16,128]{5,4,3,2,1,0:T(8,128)S(1)}, s16[49,16,128]{2,1,0:T(8,128)(2,1)S(1)}) custom-call(bf16[4,4,16,128]{3,2,1,0:T(8,128)(2,1)S(1)} %broadcast_in_dim.27.keep_ref, bf16[2,4,4,16,128]{4,3,2,1,0:T(8,128)(2,1)S(1)} %pad_maximum_fusion.refs_0_, ...), custom_call_target="tpu_custom_call" | custom-call | flops 805306368 | bytes 3145728 | tf_op jit(solution)/shard_map/part_kernel/pallas_call | solution.py:226
  9.0 1.5 %collective-permute-start.2 = (s16[49,16,128]{2,1,0:T(8,128)(2,1)S(1)}, s16[49,16,128]{2,1,0:T(8,128)(2,1)S(1)}, u32[]{:S(2)}, u32[]{:S(2)}) collective-permute-start(s16[49,16,128]{2,1,0:T(8,128)(2,1)S(1)} %get-tuple-element.24), channel_id=1, source_target_pairs={{0,4},{1,9},{2,6},{3,11},{4,0},{5,13},{6,2},{7,15},{8,12},{9,1},{1... | collective-permute-start | bytes 602120 | tf_op jit(solution)/shard_map/ppermute | solution.py:202
  11.9 1.6 %collective-permute-start.8 = (s16[49,16,128]{2,1,0:T(8,128)(2,1)S(1)}, s16[49,16,128]{2,1,0:T(8,128)(2,1)S(1)}, u32[]{:S(2)}, u32[]{:S(2)}) collective-permute-start(s16[49,16,128]{2,1,0:T(8,128)(2,1)S(1)} %get-tuple-element.25.refs_3_), channel_id=1, source_target_pairs={{0,4},{1,9},{2,6},{3,11},{4,0},{5,13},{6,2},{7,15},{8,12},{9,1},{1... | collective-permute-start | bytes 602120 | tf_op jit(solution)/shard_map/ppermute | solution.py:202
  14.3 2.6 %collective-permute-start.6 = (s16[49,16,128]{2,1,0:T(8,128)(2,1)S(1)}, s16[49,16,128]{2,1,0:T(8,128)(2,1)S(1)}, u32[]{:S(2)}, u32[]{:S(2)}) collective-permute-start(s16[49,16,128]{2,1,0:T(8,128)(2,1)S(1)} %get-tuple-element.26.refs_0_), channel_id=1, source_target_pairs={{0,16},{1,5},{2,18},{3,7},{4,20},{5,1},{6,22},{7,3},{8,24},{9,13},... | collective-permute-start | bytes 602120 | tf_op jit(solution)/shard_map/ppermute | solution.py:202
  17.1 1.6 %collective-permute-start.7 = (s16[25,16,128]{2,1,0:T(8,128)(2,1)S(1)}, s16[25,16,128]{2,1,0:T(8,128)(2,1)S(1)}, u32[]{:S(2)}, u32[]{:S(2)}) collective-permute-start(s16[25,16,128]{2,1,0:T(8,128)(2,1)S(1)} %get-tuple-element.27.refs_0_), channel_id=1, source_target_pairs={{0,8},{1,5},{2,10},{3,7},{4,12},{5,1},{6,14},{7,3},{8,0},{9,13},{1... | collective-permute-start | bytes 307208 | tf_op jit(solution)/shard_map/ppermute | solution.py:202
  18.9 2.4 %collective-permute-start.5 = (s16[25,16,128]{2,1,0:T(8,128)(2,1)S(1)}, s16[25,16,128]{2,1,0:T(8,128)(2,1)S(1)}, u32[]{:S(2)}, u32[]{:S(2)}) collective-permute-start(s16[25,16,128]{2,1,0:T(8,128)(2,1)S(1)} %get-tuple-element.29.refs_0_), channel_id=1, source_target_pairs={{0,16},{1,5},{2,18},{3,7},{4,20},{5,1},{6,22},{7,3},{8,24},{9,13},... | collective-permute-start | bytes 307208 | tf_op jit(solution)/shard_map/ppermute | solution.py:202
  21.4 1.6 %collective-permute-start.12 = (s16[25,16,128]{2,1,0:T(8,128)(2,1)S(1)}, s16[25,16,128]{2,1,0:T(8,128)(2,1)S(1)}, u32[]{:S(2)}, u32[]{:S(2)}) collective-permute-start(s16[25,16,128]{2,1,0:T(8,128)(2,1)S(1)} %get-tuple-element.33.refs_0_), channel_id=1, source_target_pairs={{0,8},{1,5},{2,10},{3,7},{4,12},{5,1},{6,14},{7,3},{8,0},{9,13},{1... | collective-permute-start | bytes 307208 | tf_op jit(solution)/shard_map/ppermute | solution.py:202
  23.3 1.6 %collective-permute-start.11 = (s16[25,16,128]{2,1,0:T(8,128)(2,1)S(1)}, s16[25,16,128]{2,1,0:T(8,128)(2,1)S(1)}, u32[]{:S(2)}, u32[]{:S(2)}) collective-permute-start(s16[25,16,128]{2,1,0:T(8,128)(2,1)S(1)} %get-tuple-element.34.refs_0_), channel_id=1, source_target_pairs={{0,4},{1,9},{2,6},{3,11},{4,0},{5,13},{6,2},{7,15},{8,12},{9,1},{1... | collective-permute-start | bytes 307208 | tf_op jit(solution)/shard_map/ppermute | solution.py:202
  24.9 4.1 %collective-permute-start.10 = (s16[25,16,128]{2,1,0:T(8,128)(2,1)S(1)}, s16[25,16,128]{2,1,0:T(8,128)(2,1)S(1)}, u32[]{:S(2)}, u32[]{:S(2)}) collective-permute-start(s16[25,16,128]{2,1,0:T(8,128)(2,1)S(1)} %cross_kernel.4.refs_0_.mine_ref), channel_id=1, source_target_pairs={{0,16},{1,17},{2,18},{3,19},{4,20},{5,21},{6,22},{7,23},{8,24},{9,... | collective-permute-start | bytes 307208 | tf_op jit(solution)/shard_map/ppermute | solution.py:202
  29.7 2.3 %collective-permute-start.16 = (s16[25,16,128]{2,1,0:T(8,128)(2,1)S(1)}, s16[25,16,128]{2,1,0:T(8,128)(2,1)S(1)}, u32[]{:S(2)}, u32[]{:S(2)}) collective-permute-start(s16[25,16,128]{2,1,0:T(8,128)(2,1)S(1)} %cross_kernel.6.refs_0_.mine_ref), channel_id=1, source_target_pairs={{0,16},{1,17},{2,18},{3,19},{4,20},{5,21},{6,22},{7,23},{8,24},{9,... | collective-permute-start | bytes 307208 | tf_op jit(solution)/shard_map/ppermute | solution.py:202
  32.1 2.5 %collective-permute-start.15 = (s16[25,16,128]{2,1,0:T(8,128)(2,1)S(1)}, s16[25,16,128]{2,1,0:T(8,128)(2,1)S(1)}, u32[]{:S(2)}, u32[]{:S(2)}) collective-permute-start(s16[25,16,128]{2,1,0:T(8,128)(2,1)S(1)} %cross_kernel.7.refs_0_.mine_ref), channel_id=1, source_target_pairs={{0,8},{1,17},{2,10},{3,19},{4,12},{5,21},{6,14},{7,23},{8,0},{9,25... | collective-permute-start | bytes 307208 | tf_op jit(solution)/shard_map/ppermute | solution.py:202
  34.6 1.5 %collective-permute-done.10.other_ref = s16[25,16,128]{2,1,0:T(8,128)(2,1)S(1)} collective-permute-done((s16[25,16,128]{2,1,0:T(8,128)(2,1)S(1)}, s16[25,16,128]{2,1,0:T(8,128)(2,1)S(1)}, u32[]{:S(2)}, u32[]{:S(2)}) %collective-permute-start.10) | collective-permute-done | bytes 102432 | tf_op jit(solution)/shard_map/ppermute | solution.py:202
  36.6 3.6 %collective-permute-done.16.other_ref = s16[25,16,128]{2,1,0:T(8,128)(2,1)S(1)} collective-permute-done((s16[25,16,128]{2,1,0:T(8,128)(2,1)S(1)}, s16[25,16,128]{2,1,0:T(8,128)(2,1)S(1)}, u32[]{:S(2)}, u32[]{:S(2)}) %collective-permute-start.16) | collective-permute-done | bytes 102432 | tf_op jit(solution)/shard_map/ppermute | solution.py:202
  42.0 1.3 %collective-permute-start.22 = (bf16[2,2,12,16,128]{4,3,2,1,0:T(8,128)(2,1)S(1)}, bf16[2,2,12,16,128]{4,3,2,1,0:T(8,128)(2,1)S(1)}, u32[]{:S(2)}, u32[]{:S(2)}) collective-permute-start(bf16[2,2,12,16,128]{4,3,2,1,0:T(8,128)(2,1)S(1)} %merge_kernel.4.refs_0_), channel_id=1, source_target_pairs={{0,4},{1,5},{2,6},{3,7},{4,0},{5,1},{6,2},{7,3},{8,12},{9,13},{10,... | collective-permute-start | bytes 589832 | tf_op jit(solution)/shard_map/ppermute | solution.py:202
  43.4 2.2 %collective-permute-start.17 = (bf16[2,2,12,16,128]{4,3,2,1,0:T(8,128)(2,1)S(1)}, bf16[2,2,12,16,128]{4,3,2,1,0:T(8,128)(2,1)S(1)}, u32[]{:S(2)}, u32[]{:S(2)}) collective-permute-start(bf16[2,2,12,16,128]{4,3,2,1,0:T(8,128)(2,1)S(1)} %merge_kernel.5.refs_0_.refs_1_), channel_id=1, source_target_pairs={{0,16},{1,5},{2,18},{3,7},{4,20},{5,1},{6,22},{7,3},{8,24},{9,13},... | collective-permute-start | bytes 589832 | tf_op jit(solution)/shard_map/ppermute | solution.py:202
  46.4 1.1 %collective-permute-done.20.other_ref = bf16[2,12,16,128]{3,2,1,0:T(8,128)(2,1)S(1)} collective-permute-done((bf16[2,12,16,128]{3,2,1,0:T(8,128)(2,1)S(1)}, bf16[2,12,16,128]{3,2,1,0:T(8,128)(2,1)S(1)}, u32[]{:S(2)}, u32[]{:S(2)}) %collective-permute-start.20) | collective-permute-done | bytes 98336 | tf_op jit(solution)/shard_map/ppermute | solution.py:202
  47.5 1.1 %collective-permute-start.21 = (bf16[2,2,12,16,128]{4,3,2,1,0:T(8,128)(2,1)S(1)}, bf16[2,2,12,16,128]{4,3,2,1,0:T(8,128)(2,1)S(1)}, u32[]{:S(2)}, u32[]{:S(2)}) collective-permute-start(bf16[2,2,12,16,128]{4,3,2,1,0:T(8,128)(2,1)S(1)} %merge_kernel.7.refs_3_), channel_id=1, source_target_pairs={{0,4},{1,9},{2,6},{3,11},{4,0},{5,13},{6,2},{7,15},{8,12},{9,1},{1... | collective-permute-start | bytes 589832 | tf_op jit(solution)/shard_map/ppermute | solution.py:202
  48.6 1.6 %collective-permute-done.22.refs_4_ = bf16[2,2,12,16,128]{4,3,2,1,0:T(8,128)(2,1)S(1)} collective-permute-done((bf16[2,2,12,16,128]{4,3,2,1,0:T(8,128)(2,1)S(1)}, bf16[2,2,12,16,128]{4,3,2,1,0:T(8,128)(2,1)S(1)}, u32[]{:S(2)}, u32[]{:S(2)}) %collective-permute-start.22) | collective-permute-done | bytes 196640 | tf_op jit(solution)/shard_map/ppermute | solution.py:202
  50.2 1.1 %place_part.2.refs_3_ = bf16[4,24,64,128]{3,2,1,0:T(8,128)(2,1)} custom-call(bf16[2,2,12,16,128]{4,3,2,1,0:T(8,128)(2,1)S(1)} %merge_kernel.4.refs_0_, bf16[2,2,12,16,128]{4,3,2,1,0:T(8,128)(2,1)S(1)} %merge_kernel.5.refs_0_.refs_1_, bf16[2,2,12,16,128]{4,3,2,1,0:T(8,128)(2,1)S(1)} %merge_kernel.6.refs_0_.refs_2_, ...), custom_call_target="tpu_custom_call" | custom-call | tf_op jit(solution)/shard_map/place_part/pallas_call | solution.py:280
  51.3 1.5 %collective-permute-done.19.refs_1_ = bf16[2,2,12,16,128]{4,3,2,1,0:T(8,128)(2,1)S(1)} collective-permute-done((bf16[2,2,12,16,128]{4,3,2,1,0:T(8,128)(2,1)S(1)}, bf16[2,2,12,16,128]{4,3,2,1,0:T(8,128)(2,1)S(1)}, u32[]{:S(2)}, u32[]{:S(2)}) %collective-permute-start.19) | collective-permute-done | bytes 196640 | tf_op jit(solution)/shard_map/ppermute | solution.py:202
  52.8 1.6 %collective-permute-done.21.refs_2_ = bf16[2,2,12,16,128]{4,3,2,1,0:T(8,128)(2,1)S(1)} collective-permute-done((bf16[2,2,12,16,128]{4,3,2,1,0:T(8,128)(2,1)S(1)}, bf16[2,2,12,16,128]{4,3,2,1,0:T(8,128)(2,1)S(1)}, u32[]{:S(2)}, u32[]{:S(2)}) %collective-permute-start.21) | collective-permute-done | bytes 196640 | tf_op jit(solution)/shard_map/ppermute | solution.py:202
  54.5 0.9 %place_part.3 = bf16[4,24,64,128]{3,2,1,0:T(8,128)(2,1)} custom-call(bf16[2,2,12,16,128]{4,3,2,1,0:T(8,128)(2,1)S(1)} %collective-permute-done.17.refs_0_, bf16[2,2,12,16,128]{4,3,2,1,0:T(8,128)(2,1)S(1)} %collective-permute-done.19.refs_1_, bf16[2,2,12,16,128]{4,3,2,1,0:T(8,128)(2,1)S(1)} %collective-permute-done.21.refs_2_, ...), custom_call_target="tpu_custom_call", output_to_operand_aliasing={{}: (3, {})} | custom-call | tf_op jit(solution)/shard_map/place_part/pallas_call | solution.py:280
  (52 shorter events, 9.2 us)
Async XLA Ops:
  0.9 7.5 %collective-permute-start.3 = (bf16[2,4,4,16,128]{4,3,2,1,0:T(8,128)(2,1)S(1)}, bf16[2,4,4,16,128]{4,3,2,1,0:T(8,128)(2,1)S(1)}, u32[]{:S(2)}, u32[]{:S(2)}) collective-permute-start(bf16[2,4,4,16,128]{4,3,2,1,0:T(8,128)(2,1)S(1)} %pad_maximum_fusion.refs_0_), channel_id=1, source_target_pairs={{0,2},{1,3},{2,0},{3,1},{4,6},{5,7},{6,4},{7,5},{8,10},{9,11},{10,... | collective-permute-start | bytes 393224 | tf_op jit(solution)/shard_map/ppermute | solution.py:205
  3.9 3.0 %collective-permute-start = (bf16[2,4,4,16,128]{4,3,2,1,0:T(8,128)(2,1)S(1)}, bf16[2,4,4,16,128]{4,3,2,1,0:T(8,128)(2,1)S(1)}, u32[]{:S(2)}, u32[]{:S(2)}) collective-permute-start(bf16[2,4,4,16,128]{4,3,2,1,0:T(8,128)(2,1)S(1)} %pad_maximum_fusion.refs_0_), channel_id=1, source_target_pairs={{0,1},{1,0},{2,3},{3,2},{4,5},{5,4},{6,7},{7,6},{8,9},{9,8},{10,11... | collective-permute-start | bytes 393224 | tf_op jit(solution)/shard_map/ppermute | solution.py:205
  4.6 2.2 %copy-start = (s32[4]{0:T(128)S(1)}, s32[4]{0:T(128)}, u32[]{:S(2)}) copy-start(s32[4]{0:T(128)} %param.10) | copy-start | bytes 52
  8.4 5.1 %collective-permute-start.4 = (bf16[2,4,4,16,128]{4,3,2,1,0:T(8,128)(2,1)S(1)}, bf16[2,4,4,16,128]{4,3,2,1,0:T(8,128)(2,1)S(1)}, u32[]{:S(2)}, u32[]{:S(2)}) collective-permute-start(bf16[2,4,4,16,128]{4,3,2,1,0:T(8,128)(2,1)S(1)} %copy_kernel.1.refs_3_), channel_id=1, source_target_pairs={{0,1},{1,0},{2,3},{3,2},{4,5},{5,4},{6,7},{7,6},{8,9},{9,8},{10,11... | collective-permute-start | bytes 393224 | tf_op jit(solution)/shard_map/ppermute | solution.py:205
  9.0 8.0 %collective-permute-start.2 = (s16[49,16,128]{2,1,0:T(8,128)(2,1)S(1)}, s16[49,16,128]{2,1,0:T(8,128)(2,1)S(1)}, u32[]{:S(2)}, u32[]{:S(2)}) collective-permute-start(s16[49,16,128]{2,1,0:T(8,128)(2,1)S(1)} %get-tuple-element.24), channel_id=1, source_target_pairs={{0,4},{1,9},{2,6},{3,11},{4,0},{5,13},{6,2},{7,15},{8,12},{9,1},{1... | collective-permute-start | bytes 602120 | tf_op jit(solution)/shard_map/ppermute | solution.py:202
  10.5 8.3 %collective-permute-start.1 = (s16[49,16,128]{2,1,0:T(8,128)(2,1)S(1)}, s16[49,16,128]{2,1,0:T(8,128)(2,1)S(1)}, u32[]{:S(2)}, u32[]{:S(2)}) collective-permute-start(s16[49,16,128]{2,1,0:T(8,128)(2,1)S(1)} %get-tuple-element.22.refs_0_), channel_id=1, source_target_pairs={{0,4},{1,17},{2,6},{3,19},{4,0},{5,21},{6,2},{7,23},{8,12},{9,25},... | collective-permute-start | bytes 602120 | tf_op jit(solution)/shard_map/ppermute | solution.py:202
  11.9 9.4 %collective-permute-start.8 = (s16[49,16,128]{2,1,0:T(8,128)(2,1)S(1)}, s16[49,16,128]{2,1,0:T(8,128)(2,1)S(1)}, u32[]{:S(2)}, u32[]{:S(2)}) collective-permute-start(s16[49,16,128]{2,1,0:T(8,128)(2,1)S(1)} %get-tuple-element.25.refs_3_), channel_id=1, source_target_pairs={{0,4},{1,9},{2,6},{3,11},{4,0},{5,13},{6,2},{7,15},{8,12},{9,1},{1... | collective-permute-start | bytes 602120 | tf_op jit(solution)/shard_map/ppermute | solution.py:202
  14.3 8.8 %collective-permute-start.6 = (s16[49,16,128]{2,1,0:T(8,128)(2,1)S(1)}, s16[49,16,128]{2,1,0:T(8,128)(2,1)S(1)}, u32[]{:S(2)}, u32[]{:S(2)}) collective-permute-start(s16[49,16,128]{2,1,0:T(8,128)(2,1)S(1)} %get-tuple-element.26.refs_0_), channel_id=1, source_target_pairs={{0,16},{1,5},{2,18},{3,7},{4,20},{5,1},{6,22},{7,3},{8,24},{9,13},... | collective-permute-start | bytes 602120 | tf_op jit(solution)/shard_map/ppermute | solution.py:202
  17.1 5.9 %collective-permute-start.7 = (s16[25,16,128]{2,1,0:T(8,128)(2,1)S(1)}, s16[25,16,128]{2,1,0:T(8,128)(2,1)S(1)}, u32[]{:S(2)}, u32[]{:S(2)}) collective-permute-start(s16[25,16,128]{2,1,0:T(8,128)(2,1)S(1)} %get-tuple-element.27.refs_0_), channel_id=1, source_target_pairs={{0,8},{1,5},{2,10},{3,7},{4,12},{5,1},{6,14},{7,3},{8,0},{9,13},{1... | collective-permute-start | bytes 307208 | tf_op jit(solution)/shard_map/ppermute | solution.py:202
  18.9 10.1 %collective-permute-start.5 = (s16[25,16,128]{2,1,0:T(8,128)(2,1)S(1)}, s16[25,16,128]{2,1,0:T(8,128)(2,1)S(1)}, u32[]{:S(2)}, u32[]{:S(2)}) collective-permute-start(s16[25,16,128]{2,1,0:T(8,128)(2,1)S(1)} %get-tuple-element.29.refs_0_), channel_id=1, source_target_pairs={{0,16},{1,5},{2,18},{3,7},{4,20},{5,1},{6,22},{7,3},{8,24},{9,13},... | collective-permute-start | bytes 307208 | tf_op jit(solution)/shard_map/ppermute | solution.py:202
  21.4 8.2 %collective-permute-start.12 = (s16[25,16,128]{2,1,0:T(8,128)(2,1)S(1)}, s16[25,16,128]{2,1,0:T(8,128)(2,1)S(1)}, u32[]{:S(2)}, u32[]{:S(2)}) collective-permute-start(s16[25,16,128]{2,1,0:T(8,128)(2,1)S(1)} %get-tuple-element.33.refs_0_), channel_id=1, source_target_pairs={{0,8},{1,5},{2,10},{3,7},{4,12},{5,1},{6,14},{7,3},{8,0},{9,13},{1... | collective-permute-start | bytes 307208 | tf_op jit(solution)/shard_map/ppermute | solution.py:202
  23.3 8.7 %collective-permute-start.11 = (s16[25,16,128]{2,1,0:T(8,128)(2,1)S(1)}, s16[25,16,128]{2,1,0:T(8,128)(2,1)S(1)}, u32[]{:S(2)}, u32[]{:S(2)}) collective-permute-start(s16[25,16,128]{2,1,0:T(8,128)(2,1)S(1)} %get-tuple-element.34.refs_0_), channel_id=1, source_target_pairs={{0,4},{1,9},{2,6},{3,11},{4,0},{5,13},{6,2},{7,15},{8,12},{9,1},{1... | collective-permute-start | bytes 307208 | tf_op jit(solution)/shard_map/ppermute | solution.py:202
  24.9 11.2 %collective-permute-start.10 = (s16[25,16,128]{2,1,0:T(8,128)(2,1)S(1)}, s16[25,16,128]{2,1,0:T(8,128)(2,1)S(1)}, u32[]{:S(2)}, u32[]{:S(2)}) collective-permute-start(s16[25,16,128]{2,1,0:T(8,128)(2,1)S(1)} %cross_kernel.4.refs_0_.mine_ref), channel_id=1, source_target_pairs={{0,16},{1,17},{2,18},{3,19},{4,20},{5,21},{6,22},{7,23},{8,24},{9,... | collective-permute-start | bytes 307208 | tf_op jit(solution)/shard_map/ppermute | solution.py:202
  29.1 7.2 %collective-permute-start.9 = (s16[25,16,128]{2,1,0:T(8,128)(2,1)S(1)}, s16[25,16,128]{2,1,0:T(8,128)(2,1)S(1)}, u32[]{:S(2)}, u32[]{:S(2)}) collective-permute-start(s16[25,16,128]{2,1,0:T(8,128)(2,1)S(1)} %cross_kernel.5.refs_0_.mine_ref), channel_id=1, source_target_pairs={{0,8},{1,9},{2,10},{3,11},{4,12},{5,13},{6,14},{7,15},{8,0},{9,1},... | collective-permute-start | bytes 307208 | tf_op jit(solution)/shard_map/ppermute | solution.py:202
  29.7 10.5 %collective-permute-start.16 = (s16[25,16,128]{2,1,0:T(8,128)(2,1)S(1)}, s16[25,16,128]{2,1,0:T(8,128)(2,1)S(1)}, u32[]{:S(2)}, u32[]{:S(2)}) collective-permute-start(s16[25,16,128]{2,1,0:T(8,128)(2,1)S(1)} %cross_kernel.6.refs_0_.mine_ref), channel_id=1, source_target_pairs={{0,16},{1,17},{2,18},{3,19},{4,20},{5,21},{6,22},{7,23},{8,24},{9,... | collective-permute-start | bytes 307208 | tf_op jit(solution)/shard_map/ppermute | solution.py:202
  32.1 8.8 %collective-permute-start.15 = (s16[25,16,128]{2,1,0:T(8,128)(2,1)S(1)}, s16[25,16,128]{2,1,0:T(8,128)(2,1)S(1)}, u32[]{:S(2)}, u32[]{:S(2)}) collective-permute-start(s16[25,16,128]{2,1,0:T(8,128)(2,1)S(1)} %cross_kernel.7.refs_0_.mine_ref), channel_id=1, source_target_pairs={{0,8},{1,17},{2,10},{3,19},{4,12},{5,21},{6,14},{7,23},{8,0},{9,25... | collective-permute-start | bytes 307208 | tf_op jit(solution)/shard_map/ppermute | solution.py:202
  36.2 5.9 %collective-permute-start.14 = (bf16[2,12,16,128]{3,2,1,0:T(8,128)(2,1)S(1)}, bf16[2,12,16,128]{3,2,1,0:T(8,128)(2,1)S(1)}, u32[]{:S(2)}, u32[]{:S(2)}) collective-permute-start(bf16[2,12,16,128]{3,2,1,0:T(8,128)(2,1)S(1)} %final_kernel.4.refs_0_.mine_ref), channel_id=1, source_target_pairs={{0,8},{1,9},{2,10},{3,11},{4,12},{5,13},{6,14},{7,15},{8,0},{9,1},... | collective-permute-start | bytes 294920 | tf_op jit(solution)/shard_map/ppermute | solution.py:202
  36.3 7.0 %collective-permute-start.13 = (bf16[2,12,16,128]{3,2,1,0:T(8,128)(2,1)S(1)}, bf16[2,12,16,128]{3,2,1,0:T(8,128)(2,1)S(1)}, u32[]{:S(2)}, u32[]{:S(2)}) collective-permute-start(bf16[2,12,16,128]{3,2,1,0:T(8,128)(2,1)S(1)} %final_kernel.5.refs_0_.mine_ref), channel_id=1, source_target_pairs={{0,4},{1,17},{2,6},{3,19},{4,0},{5,21},{6,2},{7,23},{8,12},{9,25},... | collective-permute-start | bytes 294920 | tf_op jit(solution)/shard_map/ppermute | solution.py:202
  40.3 5.7 %collective-permute-start.18 = (bf16[2,12,16,128]{3,2,1,0:T(8,128)(2,1)S(1)}, bf16[2,12,16,128]{3,2,1,0:T(8,128)(2,1)S(1)}, u32[]{:S(2)}, u32[]{:S(2)}) collective-permute-start(bf16[2,12,16,128]{3,2,1,0:T(8,128)(2,1)S(1)} %final_kernel.6.refs_0_.mine_ref), channel_id=1, source_target_pairs={{0,4},{1,9},{2,6},{3,11},{4,0},{5,13},{6,2},{7,15},{8,12},{9,1},{1... | collective-permute-start | bytes 294920 | tf_op jit(solution)/shard_map/ppermute | solution.py:202
  40.9 6.6 %collective-permute-start.20 = (bf16[2,12,16,128]{3,2,1,0:T(8,128)(2,1)S(1)}, bf16[2,12,16,128]{3,2,1,0:T(8,128)(2,1)S(1)}, u32[]{:S(2)}, u32[]{:S(2)}) collective-permute-start(bf16[2,12,16,128]{3,2,1,0:T(8,128)(2,1)S(1)} %final_kernel.7.refs_0_.mine_ref), channel_id=1, source_target_pairs={{0,16},{1,5},{2,18},{3,7},{4,20},{5,1},{6,22},{7,3},{8,24},{9,13},... | collective-permute-start | bytes 294920 | tf_op jit(solution)/shard_map/ppermute | solution.py:202
  42.0 8.2 %collective-permute-start.22 = (bf16[2,2,12,16,128]{4,3,2,1,0:T(8,128)(2,1)S(1)}, bf16[2,2,12,16,128]{4,3,2,1,0:T(8,128)(2,1)S(1)}, u32[]{:S(2)}, u32[]{:S(2)}) collective-permute-start(bf16[2,2,12,16,128]{4,3,2,1,0:T(8,128)(2,1)S(1)} %merge_kernel.4.refs_0_), channel_id=1, source_target_pairs={{0,4},{1,5},{2,6},{3,7},{4,0},{5,1},{6,2},{7,3},{8,12},{9,13},{10,... | collective-permute-start | bytes 589832 | tf_op jit(solution)/shard_map/ppermute | solution.py:202
  43.4 9.4 %collective-permute-start.17 = (bf16[2,2,12,16,128]{4,3,2,1,0:T(8,128)(2,1)S(1)}, bf16[2,2,12,16,128]{4,3,2,1,0:T(8,128)(2,1)S(1)}, u32[]{:S(2)}, u32[]{:S(2)}) collective-permute-start(bf16[2,2,12,16,128]{4,3,2,1,0:T(8,128)(2,1)S(1)} %merge_kernel.5.refs_0_.refs_1_), channel_id=1, source_target_pairs={{0,16},{1,5},{2,18},{3,7},{4,20},{5,1},{6,22},{7,3},{8,24},{9,13},... | collective-permute-start | bytes 589832 | tf_op jit(solution)/shard_map/ppermute | solution.py:202
  46.0 6.8 %collective-permute-start.19 = (bf16[2,2,12,16,128]{4,3,2,1,0:T(8,128)(2,1)S(1)}, bf16[2,2,12,16,128]{4,3,2,1,0:T(8,128)(2,1)S(1)}, u32[]{:S(2)}, u32[]{:S(2)}) collective-permute-start(bf16[2,2,12,16,128]{4,3,2,1,0:T(8,128)(2,1)S(1)} %merge_kernel.6.refs_0_.refs_2_), channel_id=1, source_target_pairs={{0,8},{1,5},{2,10},{3,7},{4,12},{5,1},{6,14},{7,3},{8,0},{9,13},{1... | collective-permute-start | bytes 589832 | tf_op jit(solution)/shard_map/ppermute | solution.py:202
  47.5 6.9 %collective-permute-start.21 = (bf16[2,2,12,16,128]{4,3,2,1,0:T(8,128)(2,1)S(1)}, bf16[2,2,12,16,128]{4,3,2,1,0:T(8,128)(2,1)S(1)}, u32[]{:S(2)}, u32[]{:S(2)}) collective-permute-start(bf16[2,2,12,16,128]{4,3,2,1,0:T(8,128)(2,1)S(1)} %merge_kernel.7.refs_3_), channel_id=1, source_target_pairs={{0,4},{1,9},{2,6},{3,11},{4,0},{5,13},{6,2},{7,15},{8,12},{9,1},{1... | collective-permute-start | bytes 589832 | tf_op jit(solution)/shard_map/ppermute | solution.py:202
